TPU v7x, 32 devices: a whole 2x2x4 slice. The times are simulated.
32 devices in a mesh: path: 2 (over core), dp: 16 (over z, y, x).
Axes of the slice: x: 2, y: 2, z: 4, core: 2. Of those that a mesh axis runs over, the one named last changes fastest.
Arguments:
- slow_in: bfloat16 [2, 128, 196, 1024], P(None, ('path', 'dp')), may hold values from -6 to 6
- fast_in: bfloat16 [2, 512, 196, 128], P(None, ('path', 'dp')), may hold values from -6 to 6
- clip_starts: int32 [2, 128], P(None, ('path', 'dp')), may hold values from 0 to 1, as said below
- w_lateral: bfloat16 [163840], P(('path', 'dp')), may hold values from -0.25 to 0.25
- w_slow_time: bfloat16 [983040], P(('path', 'dp')), may hold values from -0.09375 to 0.09375
- w_slow_space: bfloat16 [589824], P(('path', 'dp')), may hold values from -0.125 to 0.125
- w_slow_out: bfloat16 [262144], P(('path', 'dp')), may hold values from -0.375 to 0.375
- w_projection: bfloat16 [1310720], P(('path', 'dp')), may hold values from -0.15625 to 0.15625
- w_fast_time: bfloat16 [12288], P(('path', 'dp')), may hold values from -0.3125 to 0.3125
- w_fast_space: bfloat16 [9216], P(('path', 'dp')), may hold values from -0.375 to 0.375
- w_fast_out: bfloat16 [4096], P(('path', 'dp')), may hold values from -1 to 1
- slow_gain: bfloat16 [2816], P(('path', 'dp')), may hold values from 0.25 to 1.75
- slow_bias: bfloat16 [2816], P(('path', 'dp')), may hold values from -3 to 3
- fast_gain: bfloat16 [192], replicated, may hold values from 0.25 to 1.75
- fast_bias: bfloat16 [192], replicated, may hold values from -3 to 3
- slow_cotangent: bfloat16 [2, 128, 196, 1024], P(None, ('path', 'dp')), may hold values from -6 to 6
- fast_cotangent: bfloat16 [2, 512, 196, 128], P(None, ('path', 'dp')), may hold values from -6 to 6
Outputs:
- slow_out: bfloat16 [2, 128, 196, 1024], P(None, ('path', 'dp'))
- fast_out: bfloat16 [2, 512, 196, 128], P(None, ('path', 'dp'))
- slow_in_grad: bfloat16 [2, 128, 196, 1024], P(None, ('path', 'dp'))
- fast_in_grad: bfloat16 [2, 512, 196, 128], P(None, ('path', 'dp'))
- lateral_grad: float32 [163840], P(('path', 'dp'))
- slow_time_grad: float32 [983040], P(('path', 'dp'))
- slow_space_grad: float32 [589824], P(('path', 'dp'))
- slow_out_grad: float32 [262144], P(('path', 'dp'))
- projection_grad: float32 [1310720], P(('path', 'dp'))
- fast_time_grad: float32 [12288], P(('path', 'dp'))
- fast_space_grad: float32 [9216], P(('path', 'dp'))
- fast_out_grad: float32 [4096], P(('path', 'dp'))
- slow_gain_grad: float32 [2816], P(('path', 'dp'))
- slow_bias_grad: float32 [2816], P(('path', 'dp'))
- fast_gain_grad: float32 [192], replicated
- fast_bias_grad: float32 [192], replicated
Inputs may be any that keep to these rules, and one draw needn't show every extreme that they name: `clip_starts`: 1 marks the first slow frame of a clip; frame 0 of every stream is 1; clips never span streams.
All inputs are finite; a program needn't handle non-finite values.
Results may differ from a plain program's by a relative error of at most 0.0085.
Values may be sent and summed in bfloat16 or wider, within the bound.
No kernel may reach another device: no remote copies, remote signals or barrier semaphores. Data moves between devices by JAX's collectives and lax.ppermute only.
A program may use at most 256 MiB of HBM per device.

v0:
```python
import functools
import math

import jax
import jax.numpy as jnp
import numpy as np
from jax import lax
from jax.experimental import pallas as pl
from jax.experimental.pallas import tpu as pltpu
from jax.sharding import PartitionSpec as P

CS = 1024
CL = 256
CM = 256
CF = 128
CFM = 32
HH = 14
WW = 14
PIX = HH * WW
ROWS = 208
EPS = 1e-05
AXES = ("path", "dp")
BF = jnp.bfloat16
F32 = jnp.float32


def swap(value, bit):
    count = lax.axis_size(AXES)
    return lax.ppermute(value, AXES, [(i, i ^ bit) for i in range(count)])


def dp_pairs():
    bits = []
    bit = 1
    while bit < lax.axis_size("dp"):
        bits.append(bit)
        bit *= 2
    return [bits[at : at + 2] for at in range(0, len(bits), 2)]


def all_sum(value, hook=lambda value, stage: value):
    value = hook(value + swap(value, lax.axis_size("dp")), 0)
    for stage, pair in enumerate(dp_pairs()):
        if len(pair) == 1:
            value = value + swap(value, pair[0])
        else:
            one, two = pair
            first, second, third = swap(value, one), swap(value, two), swap(value, one + two)
            value = (value + first) + (second + third)
        value = hook(value, stage + 1)
    return value


def has_bits(me):
    bits = [bit for pair in dp_pairs() for bit in pair] + [lax.axis_size("dp")]
    return {bit: (me & bit) != 0 for bit in bits}


def in_order(parts, bits, mine):
    parts = [part[None] for part in parts]
    step = 1
    for bit in bits:
        parts = [jnp.where(mine[bit], parts[k ^ step], parts[k]) for k in range(len(parts))]
        step *= 2
    return jnp.concatenate(parts, 0)


class Gather:
    def __init__(self, mine, value):
        self.mine = mine
        self.shape = value.shape
        self.value = value[None]
        self.stages = dp_pairs()[::-1] + [[lax.axis_size("dp")]]
        self.flight = None
        self.start()

    def start(self):
        if not self.stages:
            self.value = self.value.reshape((-1,) + self.shape)
            return
        self.bits = self.stages.pop(0)
        steps = [
            sum(bit for n, bit in enumerate(self.bits) if k >> n & 1)
            for k in range(1, 2 ** len(self.bits))
        ]
        self.flight = [swap(self.value, step) for step in steps]

    def finish(self):
        stacked = in_order([self.value] + self.flight, self.bits, self.mine)
        if self.stages:
            stacked = jnp.swapaxes(stacked, 0, 1)
        self.value = stacked.reshape((-1,) + self.shape)
        self.flight = None
        self.start()

    def result(self):
        while self.flight is not None:
            self.finish()
        return self.value


def pick(value, start, extent, axis):
    starts = [jnp.int32(0)] * value.ndim
    starts[axis] = start
    sizes = list(value.shape)
    sizes[axis] = extent
    return lax.dynamic_slice(value, starts, sizes, allow_negative_indices=False)


def share_stages():
    return [[lax.axis_size("dp")]] + dp_pairs()


def slice_spots(me):
    spots = []
    for bits in share_stages():
        count = 2 ** len(bits)
        spot = lax.shift_right_logical(me, bits[0].bit_length() - 1) & (count - 1)
        spots.append([spot ^ k for k in range(count)])
    return spots


class Shares:
    def __init__(self, spots, value):
        self.value = value
        self.stages = list(zip(share_stages(), spots))
        self.flight = None
        self.start()

    def start(self):
        if not self.stages:
            return
        bits, spots = self.stages.pop(0)
        count = 2 ** len(bits)
        rest = self.value.shape[-2:]
        axis = 0 if bits[0] == lax.axis_size("dp") else 1
        shaped = self.value.reshape(((2, -1), (-1, count))[axis] + rest)
        parts = [pick(shaped, spot, 1, axis) for spot in spots]
        parts = [part.reshape((-1,) + rest) for part in parts]
        self.keep = parts[0]
        steps = [sum(bit for n, bit in enumerate(bits) if k >> n & 1) for k in range(1, count)]
        self.flight = [swap(part.astype(BF), step) for part, step in zip(parts[1:], steps)]

    def finish(self):
        terms = [self.keep.astype(F32)] + [part.astype(F32) for part in self.flight]
        while len(terms) > 1:
            terms = [sum(terms[at : at + 2]) for at in range(0, len(terms), 2)]
        self.value = terms[0]
        self.flight = None
        self.start()

    def result(self):
        while self.flight is not None:
            self.finish()
        return self.value.reshape(-1)


def tie(flows, *values):
    flows = [flow for flow in flows if flow.flight is not None]
    values, flights = lax.optimization_barrier((values, [flow.flight for flow in flows]))
    for flow, flight in zip(flows, flights):
        flow.flight = flight
        flow.finish()
    return values if len(values) > 1 else values[0]


def from_before(value):
    count = lax.axis_size(AXES)
    return lax.ppermute(value, AXES, [(i, i + 1) for i in range(count - 1)])


def from_after(value):
    count = lax.axis_size(AXES)
    return lax.ppermute(value, AXES, [(i + 1, i) for i in range(count - 1)])


def gelu_tan(value):
    return jnp.tanh(value * (0.7978845608028654 + 0.035677408136300125 * (value * value)))


def gelu(value):
    return value * (0.5 + 0.5 * gelu_tan(value))


def gelu_slope(value):
    tan = gelu_tan(value)
    inner = 0.7978845608028654 + 0.10703222440890037 * (value * value)
    return (0.5 + 0.5 * tan) + (0.5 * value) * (1.0 - tan * tan) * inner


def pad_rows(value):
    return jnp.pad(value, [(0, 0)] * (value.ndim - 2) + [(0, ROWS - PIX), (0, 0)])


def to_quads(value):
    micro, frames, _, lanes = value.shape
    quads = pad_rows(value).reshape(micro * frames // 4, 4, ROWS, lanes)
    return jnp.concatenate([quads[:, place] for place in range(4)], -1)


def in_vmem(array):
    return pltpu.with_memory_space_constraint(array, pltpu.VMEM)


PARTS = dict(
    short=CS,
    grad=CS,
    grad_two=CM,
    fgrad_two=128,
    grad_one=CM,
    fgrad_one=128,
    lat_grad=CL,
    fthree=4 * CF,
    fgrad=4 * CF,
    one=CM,
    two=CM,
    ftwo=128,
)


def in_vmem(array):
    return pltpu.with_memory_space_constraint(array, pltpu.VMEM)


def call(body, steps, ins, outs, scratch=(), flops=0, name=None, limit=16, unroll=False, state=None):
    names = [given[0] if len(given) == 2 else None for given in outs]
    ins = [group(state[given[0]], given[1]) if len(given) == 2 else given for given in ins]
    if state is not None:
        groups = ins[0][0].shape[0] if not state else next(iter(state.values())).shape[0]
    outs = [
        out_group((groups, ROWS, PARTS[given[0]]), F32, given[1]) if len(given) == 2 else given
        for given in outs
    ]
    arrays = [array for array, _, _ in ins]
    blocks = [(array.shape, block, index) for array, block, index in ins]
    blocks += [(shape, block, index) for shape, _, block, index, _ in outs]

    def view(ref, shape, block, index, step):
        if block is None or tuple(block) == tuple(shape):
            return ref
        spot = [
            slice(None) if size == full else pl.ds(place * size, size)
            for place, size, full in zip(index(step), block, shape)
        ]
        return ref.at[tuple(spot)]

    def kernel(*refs):
        def run(step, carry):
            views = [view(ref, *given, step) for ref, given in zip(refs, blocks)]
            body(step, *views, *refs[len(blocks) :])
            return carry

        if steps == 1 or unroll:
            for step in range(steps):
                run(step, 0)
        else:
            lax.fori_loop(0, steps, run, 0)

    moved = sum(array.size * array.dtype.itemsize for array in arrays)
    moved += sum(math.prod(shape) * jnp.dtype(dtype).itemsize for shape, dtype, *_ in outs)
    vmem = pl.BlockSpec(memory_space=pltpu.VMEM)
    result = pl.pallas_call(
        kernel,
        in_specs=[
            pl.BlockSpec(memory_space=pltpu.SMEM) if block is None else vmem
            for _, block, _ in ins
        ],
        out_specs=[vmem] * len(outs),
        out_shape=[
            pltpu.VMEM(shape, dtype) if stays else jax.ShapeDtypeStruct(shape, dtype)
            for shape, dtype, _, _, stays in outs
        ],
        scratch_shapes=list(scratch),
        compiler_params=pltpu.CompilerParams(vmem_limit_bytes=limit * 1024 * 1024),
        cost_estimate=pl.CostEstimate(
            flops=int(flops), bytes_accessed=int(moved), transcendentals=0
        ),
        name=name,
    )(*[array if block is None else in_vmem(array) for array, block, _ in ins])
    if state is None:
        return result
    fresh = {name: array for name, array in zip(names, result) if name}
    return [{**state, **fresh}] + [array for name, array in zip(names, result) if not name]


def group(array, per):
    tail = (0,) * (array.ndim - 1)
    return (array, (per,) + array.shape[1:], lambda g: (g,) + tail)


def whole(array):
    return (array, array.shape, None)


def scalar(array):
    return (array, None, None)


def stream(array, steps):
    tail = (0,) * (array.ndim - 1)
    return (array, (1,) + array.shape[1:], lambda g: (g // steps,) + tail)


def out_group(shape, dtype, per, stays=True):
    tail = (0,) * (len(shape) - 1)
    return (shape, dtype, (per,) + shape[1:], lambda g: (g,) + tail, stays)


def out_stream(shape, dtype, steps, stays=True):
    tail = (0,) * (len(shape) - 1)
    return (shape, dtype, (1,) + shape[1:], lambda g: (g // steps,) + tail, stays)


def out_whole(shape, dtype, stays=True):
    return (shape, dtype, shape, None, stays)


def rows_of(ref):
    return ref[...].reshape(-1, ref.shape[-1])


def put(ref, value):
    ref[...] = value.reshape(ref.shape).astype(ref.dtype)


def spread(value, mask):
    lanes = value.shape[-1]
    shaped = value.reshape(-1, ROWS, lanes) * mask[None, :, :lanes]
    return shaped.reshape(value.shape)


def add_rows(ref, step, steps, lanes, *values):
    first = step % steps == 0
    for row, value in enumerate(values):
        total = jnp.sum(value, 0, keepdims=True)
        spot = (0, slice(row, row + 1), slice(lanes, lanes + value.shape[-1]))
        if steps > 1:
            total = jnp.where(first, 0.0, ref[spot]) + total
        ref[spot] = total


def stats(total, start, extent, count, folded=0):
    first = total[0, 0:1, start : start + extent]
    second = total[0, 1:2, start : start + extent]
    if folded:
        first, second = fold_lanes(first, folded), fold_lanes(second, folded)
    mean = first / count
    return mean, lax.rsqrt(second / count - mean * mean + EPS)


def fold_lanes(vector, width):
    lanes = vector.shape[-1]
    if width % 128 == 0:
        parts = [vector[:, at : at + width] for at in range(0, lanes, width)]
        one = (parts[0] + parts[1]) + (parts[2] + parts[3])
        return jnp.concatenate([one] * 4, -1)
    wide = jnp.broadcast_to(vector, (8, lanes))
    wide = wide + pltpu.roll(wide, 2 * width, 1)
    wide = wide + pltpu.roll(wide, width, 1)
    return wide[0:1]


def back_parts(sums, start, extent, count, folded=0, rows=(0, 1)):
    one = sums[0, rows[0] : rows[0] + 1, start : start + extent]
    two = sums[0, rows[1] : rows[1] + 1, start : start + extent]
    if folded:
        one, two = fold_lanes(one, folded), fold_lanes(two, folded)
    return one / count, two / count


def norm_back(grad, hat, factor, one, two):
    return factor * (grad - one - hat * two)


def turn(value, step):
    return pltpu.roll(value, step % value.shape[0], 0)


def mul(left, right):
    return jnp.dot(left, right, preferred_element_type=F32)


def mul_t(left, right):
    return lax.dot_general(left, right, (((1,), (1,)), ((), ())), preferred_element_type=F32)


def mul_rows(left, right):
    return lax.dot_general(
        rows_of(left), rows_of(right), (((0,), (0,)), ((), ())), preferred_element_type=F32
    )


def column_cat(act, masks):
    act = act.astype(BF).astype(F32)
    left = spread(turn(act, 1), masks[1])
    right = spread(turn(act, -1), masks[2])
    return jnp.concatenate([left.astype(BF), act.astype(BF), right.astype(BF)], -1)


def row_sum(taps, masks):
    lanes = taps.shape[-1] // 3
    return (
        spread(turn(taps[:, :lanes], WW), masks[3])
        + taps[:, lanes : 2 * lanes]
        + spread(turn(taps[:, 2 * lanes :], -WW), masks[4])
    )


def row_cat(grad, masks):
    grad = grad.astype(BF).astype(F32)
    above = spread(turn(grad, -WW), masks[4])
    below = spread(turn(grad, WW), masks[3])
    return jnp.concatenate([above.astype(BF), grad.astype(BF), below.astype(BF)], -1)


def column_sum(taps, masks):
    lanes = taps.shape[-1] // 3
    return (
        spread(turn(taps[:, :lanes], -1), masks[2])
        + taps[:, lanes : 2 * lanes]
        + spread(turn(taps[:, 2 * lanes :], 1), masks[1])
    )


def fill_z(z, at, links, nexts, fast, edge_down, edge_up):
    frames = fast.shape[0]
    for f in range(frames):
        link, following = links[at + f], nexts[at + f]
        for q in range(4):
            z[f, :PIX, q * CF : (q + 1) * CF] = fast[f, q]
        for q in range(2):
            prev = edge_down[0, q] if f == 0 else fast[f - 1, 2 + q]
            z[f, :PIX, (4 + q) * CF : (5 + q) * CF] = (link * prev.astype(F32)).astype(BF)
        follow = edge_up[0, 0] if f == frames - 1 else fast[f + 1, 0]
        z[f, :PIX, 6 * CF :] = (following * follow.astype(F32)).astype(BF)


def k_first(
    step, links, nexts, fast, edge_down, edge_up, weight, lat, fone, total, z
):
    z[...] = jnp.zeros_like(z)
    fill_z(z, step * fast.shape[0], links, nexts, fast, edge_down, edge_up)
    value = mul(rows_of(z), weight[...])
    put(lat, value[:, :CL])
    put(fone, value[:, CL:])
    add_rows(total, step, 1, 0, value, value * value)


def k_taps(step, links, lat, total, gb, slow, w_time, masks, lat_act, taps, tail, head, *, count):
    frames = slow.shape[0]
    mean, scale = stats(total, 0, CL, count)
    hat = (rows_of(lat) - mean) * scale
    act = spread(gelu(hat * gb[0:1, :CL] + gb[1:2, :CL]), masks[0]).astype(BF)
    put(lat_act, act)
    value = mul(rows_of(slow), w_time[:CS]) + mul(act, w_time[CS:])
    put(taps, value)
    tail[0] = value[(frames - 1) * ROWS :, :CM].astype(BF)
    head[0] = (links[step * frames] * value[:ROWS, 2 * CM :]).astype(BF)


def block_taps(taps, out):
    lane = lax.broadcasted_iota(jnp.int32, (CFM, 128), 1)
    row = lax.broadcasted_iota(jnp.int32, (CFM, 128), 0)
    four = sum(jnp.where(lane == row + q * CFM, 1.0, 0.0) for q in range(4))
    wide = mul(taps[...], four.astype(BF))
    for a in range(3):
        for c in range(3):
            tap = wide[(3 * a + c) * CFM : (3 * a + c + 1) * CFM]
            for q in range(4):
                mine = (lane >= q * CFM) & (lane < (q + 1) * CFM)
                at = c * 128 + q * CFM
                out[at : at + CFM, a * 128 : (a + 1) * 128] = jnp.where(mine, tap, 0.0).astype(BF)


def k_short(
    step, slow, lat_act, w_proj, fone, total, fgb, fast_taps, masks,
    short, fact, ftwo, sums, fspace, *, steps, count
):
    block_taps(fast_taps, fspace)
    value = mul(rows_of(slow), w_proj[:CS]) + mul(rows_of(lat_act), w_proj[CS:])
    put(short, value)
    add_rows(sums, step, steps, 0, value, value * value)
    mean, scale = stats(total, CL, 128, 4.0 * count, CFM)
    hat = (rows_of(fone) - mean) * scale
    act = spread(gelu(hat * fgb[0:1, :128] + fgb[1:2, :128]), masks[0])
    cat = column_cat(act, masks)
    put(fact, cat)
    value = row_sum(mul(cat, fspace[...]), masks)
    put(ftwo, value)
    add_rows(sums, step, steps, CS, value, value * value)


def k_one(step, links, nexts, taps, rim_before, rim_after, given, slow_one, sums):
    frames = taps.shape[0]
    base = step * frames
    one = two = 0.0
    for f in range(frames):
        prev = rim_before[0].astype(F32) if f == 0 else taps[f - 1, :, :CM]
        follow = rim_after[0].astype(F32) if f == frames - 1 else taps[f + 1, :, 2 * CM :]
        value = links[base + f] * prev + taps[f, :, CM : 2 * CM] + nexts[base + f] * follow
        slow_one[f] = value
        one += jnp.sum(value, 0, keepdims=True)
        two += jnp.sum(value * value, 0, keepdims=True)
    sums[0, :, : CS + 128] = given[0]
    sums[0, 0:1, CS + 128 :] = one
    sums[0, 1:2, CS + 128 :] = two


def k_two(
    step, slow_one, ftwo, total, gb, fgb, space, fproj, masks,
    cat_out, two_out, fact_out, fthree, sums, w_space, *, steps, count
):
    for a in range(3):
        for c in range(3):
            tap = space[(3 * a + c) * CM : (3 * a + c + 1) * CM]
            w_space[c * CM : (c + 1) * CM, a * CM : (a + 1) * CM] = tap

    mean, scale = stats(total, CS + 128, CM, count)
    hat = (rows_of(slow_one) - mean) * scale
    act = spread(gelu(hat * gb[0:1, CL : 2 * CL] + gb[1:2, CL : 2 * CL]), masks[0])
    cat = column_cat(act, masks)
    put(cat_out, cat)
    value = row_sum(mul(cat, w_space[...]), masks)
    put(two_out, value)
    add_rows(sums, step, steps, 0, value, value * value)
    mean, scale = stats(total, CS, 128, 4.0 * count, CFM)
    hat = (rows_of(ftwo) - mean) * scale
    act = spread(gelu(hat * fgb[0:1, 128:256] + fgb[1:2, 128:256]), masks[0]).astype(BF)
    put(fact_out, act)
    value = mul(act, fproj[...])
    put(fthree, value)
    add_rows(sums, step, steps, CM, value, value * value)


def k_three(step, slow_two, total, gb, w_out, masks, act_out, sums, *, steps, count):
    mean, scale = stats(total, 0, CM, count)
    hat = (rows_of(slow_two) - mean) * scale
    act = gelu(hat * gb[0:1, 2 * CL : 3 * CL] + gb[1:2, 2 * CL : 3 * CL])
    act = spread(act, masks[0]).astype(BF)
    put(act_out, act)
    value = mul(act, w_out[...])
    add_rows(sums, step, steps, 0, value, value * value)


CHUNK = 16
SPAN = 512


def gelu_both(value):
    square = value * value
    tan = jnp.tanh(value * (0.7978845608028654 + 0.035677408136300125 * square))
    half = 0.5 + 0.5 * tan
    inner = 0.7978845608028654 + 0.10703222440890037 * square
    slope = half + (0.5 * value) * (1.0 - tan * tan) * inner
    return value * half, slope


def chunked(body, frames, lanes):
    full = PIX // CHUNK
    last = full * CHUNK

    def frame(f, carry):
        def step(i, carry):
            at = pl.ds(pl.multiple_of(i * CHUNK, CHUNK), CHUNK)
            for start in range(0, lanes, SPAN):
                body(f, at, CHUNK, slice(start, start + SPAN))
            return carry

        lax.fori_loop(0, full, step, 0)
        for start in range(0, lanes, SPAN):
            body(f, pl.ds(last, CHUNK), PIX - last, slice(start, start + SPAN))
        return carry

    lax.fori_loop(0, frames, frame, 0)


def halves(value):
    return value[:8] + value[8:]


def k_fast_out(step, fthree, fast, cot, total, fgb, out, grad, sums, acc, *, steps, count):
    mean, scale = stats(total, CM, 4 * CF, 4.0 * count, CF)
    gain, bias = fgb[0:1, 256:], fgb[1:2, 256:]

    @pl.when(step % steps == 0)
    def _():
        acc[...] = jnp.zeros_like(acc)

    def body(f, rows, real, lanes):
        hat = (fthree[f, rows, lanes] - mean[:, lanes]) * scale[:, lanes]
        quads = [fast[f, q, pl.ds(rows.start, real), :].astype(F32) for q in range(4)]
        if real < CHUNK:
            blank = jnp.zeros((CHUNK - real, CF), F32)
            quads = [jnp.concatenate([part, blank], 0) for part in quads]
        value = hat * gain[:, lanes] + bias[:, lanes] + jnp.concatenate(quads, -1)
        act, slope = gelu_both(value)
        act = act.astype(BF)
        for q in range(4):
            piece = act[:real, q * CF : (q + 1) * CF]
            out[f, q, pl.ds(rows.start, real), :] = piece
        slope = slope * cot[f, rows, lanes].astype(F32)
        grad[f, rows, lanes] = slope
        acc[0] += halves(slope)
        acc[1] += halves(slope * hat)

    chunked(body, fthree.shape[0], 4 * CF)

    @pl.when(step % steps == steps - 1)
    def _():
        for row in range(2):
            sums[0, row : row + 1] = jnp.sum(acc[row], 0, keepdims=True)


def k_out(
    step, act, w_out, short, cot, total, short_total, gb, given, out, grad_out, sums, three, acc,
    *, steps, count
):
    three[...] = mul(rows_of(act), w_out[...]).reshape(three.shape)
    mean_a, scale_a = stats(total, 0, CS, count)
    mean_b, scale_b = stats(short_total, 0, CS, count)
    gain_a, gain_b = gb[0:1, 768:1792], gb[0:1, 1792:]
    bias = gb[1:2, 768:1792] + gb[1:2, 1792:]

    @pl.when(step % steps == 0)
    def _():
        acc[...] = jnp.zeros_like(acc)

    def body(f, rows, real, lanes):
        hat_a = (three[f, rows, lanes] - mean_a[:, lanes]) * scale_a[:, lanes]
        hat_b = (short[f, rows, lanes] - mean_b[:, lanes]) * scale_b[:, lanes]
        value = hat_a * gain_a[:, lanes] + (hat_b * gain_b[:, lanes] + bias[:, lanes])
        smooth, slope = gelu_both(value)
        out[f, pl.ds(rows.start, real), lanes] = smooth.astype(BF)[:real]
        grad = slope * cot[f, rows, lanes].astype(F32)
        grad_out[f, rows, lanes] = grad
        acc[0, :, lanes] += halves(grad)
        acc[1, :, lanes] += halves(grad * hat_a)
        acc[2, :, lanes] += halves(grad * hat_b)

    chunked(body, act.shape[0], CS)

    @pl.when(step % steps == steps - 1)
    def _():
        for row in range(3):
            sums[0, row : row + 1, :CS] = jnp.sum(acc[row], 0, keepdims=True)
        sums[0, 0:2, CS:] = given[0]
        sums[0, 2:3, CS:] = jnp.zeros((1, 4 * CF), F32)


def k_back_three(
    step, act, w_out, short, grad, total, short_total, sums, gb, slow_two, total3,
    fgrad, fthree, ftwo, fgb, fproj, masks,
    d_three, d_short, grad_two, d_fthree, fgrad_two, sums_out, three, *, steps, count
):
    three[...] = mul(rows_of(act), w_out[...]).reshape(three.shape)
    mean_a, scale_a = stats(total, 0, CS, count)
    mean_b, scale_b = stats(short_total, 0, CS, count)
    one, two_a = back_parts(sums, 0, CS, count)
    _, two_b = back_parts(sums, 0, CS, count, rows=(0, 2))
    factor_a = gb[0:1, 768:1792] * scale_a
    factor_b = gb[0:1, 1792:] * scale_b

    def body(f, rows, real, lanes):
        given = grad[f, rows, lanes] - one[:, lanes]
        hat_a = (three[f, rows, lanes] - mean_a[:, lanes]) * scale_a[:, lanes]
        hat_b = (short[f, rows, lanes] - mean_b[:, lanes]) * scale_b[:, lanes]
        value_a = factor_a[:, lanes] * (given - hat_a * two_a[:, lanes])
        value_b = factor_b[:, lanes] * (given - hat_b * two_b[:, lanes])
        if real < CHUNK:
            row = lax.broadcasted_iota(jnp.int32, value_a.shape, 0)
            value_a = jnp.where(row < real, value_a, 0.0)
            value_b = jnp.where(row < real, value_b, 0.0)
        d_three[f, rows, lanes] = value_a.astype(BF)
        d_short[f, rows, lanes] = value_b.astype(BF)

    chunked(body, act.shape[0], CS)
    mean, scale = stats(total3, 0, CM, count)
    hat = (rows_of(slow_two) - mean) * scale
    slope = gelu_slope(hat * gb[0:1, 2 * CL : 3 * CL] + gb[1:2, 2 * CL : 3 * CL])
    value = slope * mul_t(rows_of(d_three), w_out[...])
    put(grad_two, value)
    add_rows(sums_out, step, steps, 0, value, value * hat)

    mean, scale = stats(total3, CM, 4 * CF, 4.0 * count, CF)
    one, two = back_parts(sums, CS, 4 * CF, 4.0 * count, CF)
    hat = (rows_of(fthree) - mean) * scale
    value = norm_back(rows_of(fgrad), hat, fgb[0:1, 256:] * scale, one, two)
    lanes = value.shape[-1]
    row = lax.broadcasted_iota(jnp.int32, (1, ROWS, lanes), 1)
    value = jnp.where(row < PIX, value.reshape(-1, ROWS, lanes), 0.0)
    value = value.reshape(-1, lanes).astype(BF)
    put(d_fthree, value)
    mean, scale = stats(short_total, CS, 128, 4.0 * count, CFM)
    hat = (rows_of(ftwo) - mean) * scale
    slope = gelu_slope(hat * fgb[0:1, 128:256] + fgb[1:2, 128:256])
    value = slope * mul_t(value, fproj[...])
    put(fgrad_two, value)
    add_rows(sums_out, step, steps, CM, value, value * hat)


def k_back_two(
    step, slow_two, total3, grad_two, sums, gb, w_space, slow_one, total2,
    ftwo, fgrad_two, fgb, fspace, fone, total1, masks,
    taps_out, grad_one, ftaps_out, fgrad_one, sums_out, *, steps, count
):
    mean, scale = stats(total3, 0, CM, count)
    one, two = back_parts(sums, 0, CM, count)
    hat = (rows_of(slow_two) - mean) * scale
    value = norm_back(rows_of(grad_two), hat, gb[0:1, 2 * CL : 3 * CL] * scale, one, two)
    cat = row_cat(spread(value, masks[0]), masks)
    put(taps_out, cat)
    value = column_sum(mul_t(cat, w_space[...]), masks)
    mean, scale = stats(total2, CS + 128, CM, count)
    hat = (rows_of(slow_one) - mean) * scale
    value = gelu_slope(hat * gb[0:1, CL : 2 * CL] + gb[1:2, CL : 2 * CL]) * value
    put(grad_one, value)
    add_rows(sums_out, step, steps, 0, value, value * hat)

    mean, scale = stats(total2, CS, 128, 4.0 * count, CFM)
    one, two = back_parts(sums, CM, 128, 4.0 * count, CFM)
    hat = (rows_of(ftwo) - mean) * scale
    value = norm_back(rows_of(fgrad_two), hat, fgb[0:1, 128:256] * scale, one, two)
    cat = row_cat(spread(value, masks[0]), masks)
    put(ftaps_out, cat)
    value = column_sum(mul_t(cat, fspace[...]), masks)
    mean, scale = stats(total1, CL, 128, 4.0 * count, CFM)
    hat = (rows_of(fone) - mean) * scale
    value = gelu_slope(hat * fgb[0:1, :128] + fgb[1:2, :128]) * value
    put(fgrad_one, value)
    add_rows(sums_out, step, steps, CM, value, value * hat)


def k_back_one(
    step, links, slow_one, total2, grad_one, fone, total1, fgrad_one, sums, gb, fgb, masks,
    d_one, d_fone, tail, head, *, count
):
    frames = slow_one.shape[0]
    mean, scale = stats(total2, CS + 128, CM, count)
    one, two = back_parts(sums, 0, CM, count)
    hat = (rows_of(slow_one) - mean) * scale
    value = norm_back(rows_of(grad_one), hat, gb[0:1, CL : 2 * CL] * scale, one, two)
    value = spread(value, masks[0])
    put(d_one, value)
    mean, scale = stats(total1, CL, 128, 4.0 * count, CFM)
    one, two = back_parts(sums, CM, 128, 4.0 * count, CFM)
    hat = (rows_of(fone) - mean) * scale
    fvalue = norm_back(rows_of(fgrad_one), hat, fgb[0:1, :128] * scale, one, two)
    fvalue = spread(fvalue, masks[0])
    put(d_fone, fvalue)
    last = (frames - 1) * ROWS
    tail[0, :, :CM] = value[last:].astype(BF)
    tail[0, :, CM:] = fvalue[last:].astype(BF)
    link = links[step * frames]
    head[0, :, :CM] = (link * value[:ROWS]).astype(BF)
    head[0, :, CM:] = (link * fvalue[:ROWS]).astype(BF)


def k_trio(
    step, links, nexts, d_one, rim_before, rim_after, d_short, w_time, w_proj, lat, total1, gb,
    trio, grad, sums, *, count
):
    frames = d_one.shape[0]
    base = step * frames
    for f in range(frames):
        prev = rim_before[0, :, :CM] if f == 0 else d_one[f - 1]
        follow = rim_after[0, :, :CM] if f == frames - 1 else d_one[f + 1]
        trio[f, :, :CM] = (nexts[base + f] * follow.astype(F32)).astype(BF)
        trio[f, :, CM : 2 * CM] = d_one[f]
        trio[f, :, 2 * CM :] = (links[base + f] * prev.astype(F32)).astype(BF)
    value = mul_t(rows_of(trio), w_time[CS:]) + mul_t(rows_of(d_short), w_proj[CS:])
    mean, scale = stats(total1, 0, CL, count)
    hat = (rows_of(lat) - mean) * scale
    value = gelu_slope(hat * gb[0:1, :CL] + gb[1:2, :CL]) * value
    put(grad, value)
    add_rows(sums, step, 1, 0, value, value * hat)


def k_slow_grad(step, trio, d_short, w_time, w_proj, out):
    value = mul_t(rows_of(trio), w_time[:CS]) + mul_t(rows_of(d_short), w_proj[:CS])
    out[...] = value.reshape(-1, ROWS, CS)[:, :PIX].astype(BF)


def k_back_lat(step, links, lat, total1, grad, sums, gb, masks, d_lat, head, *, count):
    frames = lat.shape[0]
    mean, scale = stats(total1, 0, CL, count)
    one, two = back_parts(sums, 0, CL, count)
    hat = (rows_of(lat) - mean) * scale
    value = norm_back(rows_of(grad), hat, gb[0:1, :CL] * scale, one, two)
    value = spread(value, masks[0])
    put(d_lat, value)
    head[0] = (links[step * frames] * value[:ROWS]).astype(BF)


def k_fast_grad(
    step, links, nexts, fgrad, d_lat, lat_rim, d_fone, rim_before, rim_after, w_back, out, cat
):
    frames = d_lat.shape[0]
    base = step * frames
    for f in range(frames):
        last = f == frames - 1
        follow = lat_rim[0] if last else d_lat[f + 1]
        prev_f = rim_before[0, :, CM:] if f == 0 else d_fone[f - 1]
        next_f = rim_after[0, :, CM:] if last else d_fone[f + 1]
        lane = lax.broadcasted_iota(jnp.int32, prev_f.shape, 1)
        rim = jnp.where(lane >= 96, links[base + f] * prev_f.astype(F32), 0.0)
        rim += jnp.where(lane < 32, nexts[base + f] * next_f.astype(F32), 0.0)
        cat[f, :, :CL] = d_lat[f]
        cat[f, :, CL : CL + 128] = d_fone[f]
        cat[f, :, CL + 128 : 2 * CL + 128] = (nexts[base + f] * follow.astype(F32)).astype(BF)
        cat[f, :, 2 * CL + 128 :] = rim.astype(BF)
    value = rows_of(fgrad) + mul_t(rows_of(cat), w_back[...])
    value = value.reshape(-1, ROWS, 4 * CF)
    for q in range(4):
        out[:, q] = value[:, :PIX, q * CF : (q + 1) * CF].astype(BF)


def k_outer_joined(step, slow, lat, right, out, *, parts, taps):
    value = mul_rows(slow if step < parts else lat, right).astype(BF)
    if taps == 1:
        out[...] = value
    else:
        for tap in range(taps):
            out[tap] = value[:, tap * CM : (tap + 1) * CM]


def outer_joined(slow, lat, right, taps, name):
    wide = 256
    parts = slow.shape[-1] // wide
    block = slow.shape[:2] + (wide,)
    rows, lanes = slow.shape[-1] + lat.shape[-1], right.shape[-1]
    if taps == 1:
        out = ((rows, lanes), BF, (wide, lanes), lambda g: (g, 0), True)
    else:
        out = ((taps, rows, CM), BF, (taps, wide, CM), lambda g: (0, g, 0), True)
    return call(
        functools.partial(k_outer_joined, parts=parts, taps=taps),
        rows // wide,
        [
            (slow, block, lambda g: (0, 0, min(g, parts - 1))),
            whole(lat),
            whole(right),
        ],
        [out],
        flops=2 * slow.shape[0] * slow.shape[1] * rows * lanes,
        name=name,
        unroll=True,
    )[0]


def k_outer_out(step, left, right, fleft, fright, out, fout):
    out[...] = mul_rows(left, right).astype(BF)
    value = mul_rows(fleft, fright)
    fout[...] = sum(
        value[q * CFM : (q + 1) * CFM, q * CF : (q + 1) * CF] for q in range(4)
    ).astype(BF)


def lanes_at(value, at):
    return (pltpu.roll(value, (128 - at) % 128, 1) if at else value)[:, :CFM]


def k_outer_space(step, left, right, fleft, fright, out, fout):
    value = mul_rows(left, right).astype(BF)
    for a in range(3):
        out[a, 0] = value[:, a * CM : (a + 1) * CM]
    value = mul_rows(fleft, fright)
    for a in range(3):
        block = value[:, a * 128 : (a + 1) * 128]
        folded = sum(
            lanes_at(block[q * CFM : (q + 1) * CFM], q * CFM) for q in range(4)
        )
        fout[a, 0] = folded.astype(BF)


def k_outer_first(
    step, links, nexts, fast, edge_down, edge_up, d_lat, d_fone, out, fout, z, *, micro
):
    z[...] = jnp.zeros_like(z)
    frames = z.shape[0] // micro
    for m in range(micro):
        part = pl.ds(m * frames, frames)
        fill_z(
            z.at[part], m * frames, links, nexts, fast.at[part],
            edge_down.at[pl.ds(m, 1)], edge_up.at[pl.ds(m, 1)],
        )
    blocks = [4, 5, 0, 1, 2]
    taps = [0.0, 0.0, 0.0]
    fast = mul_rows(z, d_fone)
    lat = mul_rows(z, d_lat)
    for tap, block in enumerate(blocks):
        out[tap * CF : (tap + 1) * CF] = lat[block * CF : (block + 1) * CF].astype(BF)
    for q in range(4):
        for k in range(3):
            block = [5, 0, 1, 2, 3, 6][q + k]
            taps[k] += lanes_at(fast[block * CF : (block + 1) * CF], q * CFM)
    for k in range(3):
        fout[k] = taps[k].astype(BF)


def k_params(step, sums_a, sums_b, sums_c, sums_d, out, fast):
    a, b, c, d = (ref[0] + ref[1] for ref in (sums_a, sums_b, sums_c, sums_d))
    for row, place in enumerate((1, 0)):
        out[row : row + 1, :CL] = d[place : place + 1]
        out[row : row + 1, CL : 2 * CL] = c[place : place + 1, :CM]
        out[row : row + 1, 2 * CL : 3 * CL] = b[place : place + 1, :CM]
        out[row : row + 1, 768:1792] = a[place : place + 1, :CS]
        third = 2 if row == 0 else 0
        out[row : row + 1, 1792:] = a[third : third + 1, :CS]
        fast[row : row + 1] = fold_lanes(c[place : place + 1, CM:], CFM)
        fast[row + 2 : row + 3] = fold_lanes(b[place : place + 1, CM:], CFM)
        fast[row + 4 : row + 5] = fold_lanes(a[place : place + 1, CS:], CF)[:, :128]


def mask_table():
    row = np.arange(ROWS)
    col = row % WW
    real = row < PIX
    table = [real, real & (col != 0), real & (col != WW - 1), real & (row >= WW), row < PIX - WW]
    return np.broadcast_to(np.stack(table)[:, :, None], (5, ROWS, CM)).astype(np.float32)


def as_rows(shard):
    return jnp.pad(shard, (0, -shard.shape[0] % CM)).reshape(-1, CM)


def flat_of(gathered, at, shard, lanes):
    rows = -(-shard.shape[0] // CM)
    part = gathered[:, at : at + rows]
    if shard.shape[0] % CM:
        part = part.reshape(part.shape[0], -1)[:, : shard.shape[0]]
    return part.reshape(-1, lanes)


def local(
    slow_in,
    fast_in,
    clip_starts,
    w_lateral,
    w_slow_time,
    w_slow_space,
    w_slow_out,
    w_projection,
    w_fast_time,
    w_fast_space,
    w_fast_out,
    slow_gain,
    slow_bias,
    fast_gain,
    fast_bias,
    slow_cotangent,
    fast_cotangent,
):
    devices = lax.axis_size(AXES)
    micro, frames = slow_in.shape[:2]
    groups = micro * frames
    masks = jnp.asarray(mask_table())
    count = float(frames * PIX * devices)
    me = lax.axis_index(AXES)
    share = slow_gain.shape[0]
    mine, spots, share_start = has_bits(me), slice_spots(me), me * share

    shards = [
        w_slow_time, w_lateral, w_fast_time, w_fast_space, w_fast_out, slow_gain, slow_bias
    ]
    packed = [as_rows(shard) for shard in shards]
    places = np.cumsum([0] + [part.shape[0] for part in packed])
    packed = jnp.concatenate(packed, 0)
    near = Gather(mine, jnp.pad(packed, ((0, -packed.shape[0] % 8), (0, 0))))
    projection = lax.all_gather(w_projection.reshape(-1, CS), AXES, axis=0, tiled=True)

    slow = pad_rows(slow_in).reshape(groups, ROWS, CS)
    cot = pad_rows(slow_cotangent).reshape(groups, ROWS, CS)
    fast = fast_in.reshape(groups, 4, PIX, CF)
    fcot = to_quads(fast_cotangent)

    link = (1 - clip_starts).astype(F32)
    links = link.reshape(groups)
    nexts = jnp.concatenate([link[:, 1:], jnp.ones((micro, 1), F32)], 1).reshape(groups)
    edge_down = from_before(fast_in[:, -2:])
    edge_up = from_after(fast_in[:, :1] * link[:, :1, None, None].astype(BF))
    slow = tie([near], slow)
    fast, fcot = tie([near], fast, fcot)
    cot = tie([near], cot)

    weights = near.result()
    cuts = [
        flat_of(weights, int(at), shard, lanes)
        for at, shard, lanes in zip(places, shards, (CM, CL, CFM, CFM, CF, share, share))
    ]
    slow_time = cuts[0].reshape(3, CS + CL, CM)
    slow_time = jnp.concatenate([slow_time[tap] for tap in range(3)], -1)
    lateral, fast_time, fast_space, fast_proj = cuts[1:5]
    gb = jnp.stack([cuts[5].reshape(-1), cuts[6].reshape(-1)]).astype(F32)
    fast_both = jnp.stack([fast_gain, fast_bias]).astype(F32)
    fgb = jnp.concatenate(
        [
            jnp.tile(part, (1, 4))
            for part in (fast_both[:, :CFM], fast_both[:, CFM : 2 * CFM], fast_both[:, 2 * CFM :])
        ],
        1,
    )

    fast_time = fast_time.reshape(3, CF, CFM)
    order = [5, 0, 1, 2, 3, 6]
    band = np.zeros((3, 7, 4), np.float32)
    for q in range(4):
        for k in range(3):
            band[k, order[q + k], q] = 1
    band = jnp.asarray(band, BF)
    fast_band = jnp.sum(
        band[:, :, None, :, None] * fast_time[:, None, :, None, :], 0, dtype=F32
    ).astype(BF).reshape(7 * CF, 4 * CFM)
    none = jnp.zeros((CF, CL), BF)
    lat_band = jnp.concatenate([lateral[2 * CF :], none, lateral[: 2 * CF], none], 0)
    w_first = jnp.concatenate([lat_band, fast_band], -1)
    eye4 = jnp.eye(4, dtype=BF)
    fproj = (fast_proj[None, :, None, :] * eye4[:, None, :, None]).reshape(4 * CFM, 4 * CF)
    lat_prev = jnp.concatenate([jnp.zeros((2 * CF, CL), BF), lateral[: 2 * CF]], 0)
    blank = jnp.zeros((CF, 3 * CFM), BF)
    rim_rows = jnp.concatenate(
        [
            jnp.concatenate([blank, fast_time[2]], -1),
            jnp.zeros((2 * CF, 4 * CFM), BF),
            jnp.concatenate([fast_time[0], blank], -1),
        ],
        0,
    )
    w_back = jnp.concatenate([w_first[: 4 * CF], lat_prev, rim_rows], -1)

    links, nexts, w_first, spots, mine, share_start, *mids = tie(
        [], links, nexts, w_first, spots, mine, share_start,
        gb, fgb, fast_space, fproj, w_back, projection, slow_time,
    )
    gb, fgb, fast_space, fproj, w_back, projection, slow_time = mids
    far = Gather(mine, jnp.concatenate([as_rows(w_slow_space), as_rows(w_slow_out)], 0))
    space_rows = -(-w_slow_space.shape[0] // CM)

    rows = groups * ROWS
    bind = functools.partial

    def og(lanes, dtype, per):
        return out_group((groups, ROWS, lanes), dtype, per)

    def os(per, n, lanes):
        return out_stream((micro, n, lanes), F32, frames // per)

    def edge(lanes):
        return out_stream((micro, ROWS, lanes), BF, 1)

    def hooked(*stages):
        return lambda value, stage: tie(stages[stage], value) if stage < len(stages) else value

    lat_pre, fone, sums = call(
        k_first,
        micro,
        [
            scalar(links), scalar(nexts), group(fast, frames), stream(edge_down, 1),
            stream(edge_up, 1), whole(w_first),
        ],
        [og(CL, F32, frames), og(128, F32, frames), os(frames, 2, CL + 128)],
        scratch=[pltpu.VMEM((frames, ROWS, 7 * CF), BF)],
        flops=2 * rows * 896 * 384,
        name="lateral_and_fast_time",
    )
    total1 = all_sum(sums, hooked([far]))

    lat_act, taps, tail, head = call(
        bind(k_taps, count=count),
        micro,
        [
            scalar(links), group(lat_pre, frames), stream(total1, 1), whole(gb),
            group(slow, frames), whole(slow_time), whole(masks),
        ],
        [og(CL, BF, frames), og(3 * CM, F32, frames), edge(CM), edge(CM)],
        flops=2 * rows * 1280 * 768,
        name="slow_time_taps",
    )
    rim_before, rim_after = from_before(tail), from_after(head)
    lat_act, taps = tie([far], lat_act, taps)
    per = frames
    state, fact_cat, sums, fspace = call(
        bind(k_short, steps=1, count=count),
        micro,
        [
            group(slow, per), group(lat_act, per), whole(projection), group(fone, per),
            stream(total1, 1), whole(fgb), whole(fast_space), whole(masks),
        ],
        [
            ("short", per), og(384, BF, per), ("ftwo", per), os(per, 2, CS + 128),
            out_whole((384, 384), BF),
        ],
        state={},
        flops=2 * rows * 1280 * 1024,
        name="shortcut_and_fast_space",
    )
    state, sums = call(
        k_one,
        micro,
        [
            scalar(links), scalar(nexts), group(taps, frames),
            stream(rim_before, 1), stream(rim_after, 1), stream(sums, 1),
        ],
        [("one", frames), os(frames, 2, CS + 128 + CM)],
        state=state,
        name="slow_one",
    )
    total2 = all_sum(sums, hooked([far]))
    weights = far.result()
    space = flat_of(weights, 0, w_slow_space, CM)
    slow_proj = flat_of(weights, space_rows, w_slow_out, CM).reshape(CM, 4, CM)
    slow_proj = jnp.concatenate([slow_proj[:, part] for part in range(4)], -1)

    state, cat_one, fact_two, sums, slow_space = call(
        bind(k_two, steps=1, count=count),
        micro,
        [
            ("one", per), ("ftwo", per), stream(total2, 1), whole(gb), whole(fgb),
            whole(space), whole(fproj), whole(masks),
        ],
        [
            og(3 * CM, BF, per), ("two", per), og(128, BF, per), ("fthree", per),
            os(per, 2, CM + 4 * CF), out_whole((3 * CM, 3 * CM), BF),
        ],
        state=state,
        flops=2 * rows * 768 * 768,
        name="slow_space",
    )
    total3 = all_sum(sums)

    state, act_two, sums = call(
        bind(k_three, steps=1, count=count),
        micro,
        [
            ("two", per), stream(total3, 1), whole(gb), whole(slow_proj),
            whole(masks),
        ],
        [og(CM, BF, per), os(per, 2, CS)],
        state=state,
        flops=2 * rows * 256 * 1024,
        name="slow_three",
    )
    per = 2 if frames % 2 == 0 else 1
    steps = frames // per
    quarters = ((groups, 4, PIX, CF), BF)
    state, fast_out, fsums = call(
        bind(k_fast_out, steps=steps, count=count),
        groups // per,
        [
            ("fthree", per), group(fast, per), group(fcot, per), stream(total3, steps),
            whole(fgb),
        ],
        [out_group(*quarters, per, False), ("fgrad", per), os(per, 2, 4 * CF)],
        state=state,
        scratch=[pltpu.VMEM((2, 8, 4 * CF), F32)],
        flops=rows * 512 * 200,
        name="fast_out",
    )
    total4 = all_sum(sums)

    state, slow_out, sums = call(
        bind(k_out, steps=steps, count=count),
        groups // per,
        [
            group(act_two, per), whole(slow_proj), ("short", per), group(cot, per),
            stream(total4, steps), stream(total2, steps), whole(gb), stream(fsums, steps),
        ],
        [
            out_group((groups, PIX, CS), BF, per, False), ("grad", per), os(per, 3, CS + 4 * CF),
        ],
        state=state,
        scratch=[pltpu.VMEM((per, ROWS, CS), F32), pltpu.VMEM((3, 8, CS), F32)],
        flops=2 * rows * 256 * 1024,
        name="slow_out",
    )
    sums_a = all_sum(sums)

    def pixels_first(value, whole_shape):
        return jnp.swapaxes(value.reshape(whole_shape), 1, 2)

    state, d_three, d_short, d_fthree, sums = call(
        bind(k_back_three, steps=steps, count=count),
        groups // per,
        [
            group(act_two, per), whole(slow_proj), ("short", per), ("grad", per),
            stream(total4, steps), stream(total2, steps), stream(sums_a, steps), whole(gb),
            ("two", per), stream(total3, steps), ("fgrad", per), ("fthree", per),
            ("ftwo", per), whole(fgb), whole(fproj), whole(masks),
        ],
        [
            og(CS, BF, per), og(CS, BF, per), ("grad_two", per), og(4 * CF, BF, per),
            ("fgrad_two", per), os(per, 2, CM + 128),
        ],
        state=state,
        scratch=[pltpu.VMEM((per, ROWS, CS), F32)],
        flops=4 * rows * 256 * 1024,
        name="back_three",
    )

    def shares(value):
        return value.reshape(devices, -1, value.shape[-1])

    flows = {}

    def weights_of_three(value, stage):
        if stage == 0:
            proj_grad = outer_joined(slow, lat_act, d_short, 1, "projection_grad")
            out_grad, flows["fast_out"] = call(
                k_outer_out,
                1,
                [whole(act_two), whole(d_three), whole(fact_two), whole(d_fthree)],
                [out_whole((CM, CS), BF), out_whole((CFM, CF), BF)],
                flops=2 * rows * 256 * 1024,
                name="slow_out_grad",
            )
            value, proj_grad, out_grad = tie([], value, proj_grad, out_grad)
            both = jnp.concatenate([shares(proj_grad), shares(out_grad)], 1)
            flows["a"] = Shares(spots, both)
            flows["proj_rows"] = proj_grad.shape[0] // devices
        elif stage == 1:
            value = tie([flows["a"]], value)
        return value

    sums_b = all_sum(sums, weights_of_three)

    per = frames
    state, two_taps, ftwo_taps, sums = call(
        bind(k_back_two, steps=1, count=count),
        micro,
        [
            ("two", per), stream(total3, 1), ("grad_two", per),
            stream(sums_b, 1), whole(gb), whole(slow_space), ("one", per),
            stream(total2, 1), ("ftwo", per), ("fgrad_two", per), whole(fgb),
            whole(fspace), group(fone, per), stream(total1, 1), whole(masks),
        ],
        [
            og(3 * CM, BF, per), ("grad_one", per), og(384, BF, per), ("fgrad_one", per),
            os(per, 2, CM + 128),
        ],
        state=state,
        flops=2 * rows * 768 * 768,
        name="back_two",
    )
    block = (groups, ROWS, CM)
    slim = (groups, ROWS, 128)

    def weights_of_two(value, stage):
        if stage == 0:
            flows["space"], flows["fspace"] = call(
                k_outer_space,
                3,
                [
                    (cat_one, block, lambda g: (0, 0, g)), whole(two_taps),
                    (fact_cat, slim, lambda g: (0, 0, g)), whole(ftwo_taps),
                ],
                [
                    ((3, 3, CM, CM), BF, (3, 1, CM, CM), lambda g: (0, g, 0, 0), True),
                    ((3, 3, CFM, CFM), BF, (3, 1, CFM, CFM), lambda g: (0, g, 0, 0), True),
                ],
                flops=2 * rows * 768 * 768,
                name="slow_space_grad",
                unroll=True,
            )
            value, flows["space"] = tie([], value, flows["space"])
        elif stage == 1:
            value = tie([flows["a"]], value)
        return value

    sums_c = all_sum(sums, weights_of_two)

    state, d_one, d_fone, tail, head = call(
        bind(k_back_one, count=count),
        micro,
        [
            scalar(links), ("one", frames), stream(total2, 1), ("grad_one", frames),
            group(fone, frames), stream(total1, 1), ("fgrad_one", frames), stream(sums_c, 1),
            whole(gb), whole(fgb), whole(masks),
        ],
        [og(CM, BF, frames), og(128, BF, frames), edge(CM + 128), edge(CM + 128)],
        state=state,
        name="back_one",
    )
    rim_before, rim_after = from_before(tail), from_after(head)
    slow_out = pixels_first(slow_out, slow_in.shape)
    rim_before, rim_after, slow_out = tie([], rim_before, rim_after, slow_out)
    state, trio, sums = call(
        bind(k_trio, count=count),
        micro,
        [
            scalar(links), scalar(nexts), group(d_one, frames),
            stream(rim_before, 1), stream(rim_after, 1), group(d_short, frames),
            whole(slow_time), whole(projection),
            group(lat_pre, frames), stream(total1, 1), whole(gb),
        ],
        [og(3 * CM, BF, frames), ("lat_grad", frames), os(frames, 2, CL)],
        state=state,
        flops=2 * rows * 1792 * 256,
        name="back_lateral",
    )

    def weights_of_one(value, stage):
        if stage == 0:
            time_grad = outer_joined(slow, lat_act, trio, 3, "slow_time_grad")
            value, time_grad = tie([flows["a"]], value, time_grad)
            both = jnp.concatenate([shares(time_grad), shares(flows["space"])], 1)
            flows["b"] = Shares(spots, both)
            flows["time_rows"] = time_grad.shape[0] * time_grad.shape[1] // devices
        elif stage == 1:
            value = tie([flows["b"]], value)
        return value

    sums_d = all_sum(sums, weights_of_one)

    state, d_lat, head = call(
        bind(k_back_lat, count=count),
        micro,
        [
            scalar(links), group(lat_pre, frames), stream(total1, 1), ("lat_grad", frames),
            stream(sums_d, 1), whole(gb), whole(masks),
        ],
        [og(CL, BF, frames), edge(CL)],
        state=state,
        name="back_lat",
    )
    lat_rim = from_after(head)
    first_grad, ftime_grad = call(
        bind(k_outer_first, micro=micro),
        1,
        [
            scalar(links), scalar(nexts), whole(fast), whole(edge_down), whole(edge_up),
            whole(d_lat), whole(d_fone),
        ],
        [out_whole((5 * CF, CL), BF), out_whole((3, CF, CFM), BF)],
        scratch=[pltpu.VMEM((groups, ROWS, 7 * CF), BF)],
        flops=2 * rows * 896 * 384,
        name="lateral_grad",
    )
    flat = [
        part.reshape(devices, -1)
        for part in (first_grad, ftime_grad, flows["fspace"], flows["fast_out"])
    ]
    sizes = [part.shape[1] for part in flat]
    flat = jnp.concatenate(flat, 1)
    flat = jnp.pad(flat, ((0, 0), (0, -flat.shape[1] % 1024)))
    flat = flat.reshape(devices, -1, 128)
    trio, flat = tie([], trio, flat)
    last = Shares(spots, flat)
    per = frames
    slow_in_grad = call(
        k_slow_grad,
        micro,
        [group(trio, per), group(d_short, per), whole(slow_time), whole(projection)],
        [out_group((groups, PIX, CS), BF, per, False)],
        flops=2 * rows * 1792 * 1024,
        name="slow_in_grad",
    )[0]
    lat_rim, slow_in_grad = tie([flows["b"], last], lat_rim, slow_in_grad)
    state, fast_in_grad = call(
        k_fast_grad,
        micro,
        [
            scalar(links), scalar(nexts), ("fgrad", frames), group(d_lat, frames),
            stream(lat_rim, 1), group(d_fone, frames), stream(rim_before, 1),
            stream(rim_after, 1), whole(w_back),
        ],
        [out_group(*quarters, frames, False)],
        state=state,
        scratch=[pltpu.VMEM((frames, ROWS, 768), BF)],
        flops=2 * rows * 768 * 512,
        name="fast_in_grad",
    )
    fast_in_grad, slow_in_grad = tie([flows["b"], last], fast_in_grad, slow_in_grad)
    both_out = flows["a"].result().reshape(-1, CS)
    cut = flows["proj_rows"]
    proj_out, out_out = both_out[:cut].reshape(-1), both_out[cut:].reshape(-1)
    both_out = flows["b"].result().reshape(-1, CM)
    cut = flows["time_rows"]
    time_out, space_out = both_out[:cut].reshape(-1), both_out[cut:].reshape(-1)
    flat = last.result()
    smalls = []
    at = 0
    for size in sizes:
        smalls.append(flat[at : at + size])
        at += size

    norms, fnorms = call(
        k_params,
        1,
        [whole(sums_a), whole(sums_b), whole(sums_c), whole(sums_d)],
        [out_whole((2, 2816), F32), out_whole((8, 128), F32)],
        name="norm_grads",
    )
    norms = pick(norms, share_start, share, 1)
    fast_gain_grad, fast_bias_grad = (
        jnp.concatenate([fnorms[row, :CFM], fnorms[row + 2, :CFM], fnorms[row + 4]])
        for row in range(2)
    )
    return (
        jnp.swapaxes(slow_out, 1, 2),
        fast_out.reshape(fast_in.shape),
        slow_in_grad.reshape(slow_in.shape),
        fast_in_grad.reshape(fast_in.shape),
        smalls[0],
        time_out,
        space_out,
        out_out,
        proj_out,
        smalls[1],
        smalls[2],
        smalls[3],
        norms[0],
        norms[1],
        fast_gain_grad,
        fast_bias_grad,
    )


def solution(mesh):
    frames = P(None, AXES, None, None)
    flat = P(AXES)
    return jax.shard_map(
        local,
        mesh=mesh,
        in_specs=(frames, frames, P(None, AXES))
        + (flat,) * 10
        + (P(), P(), frames, frames),
        out_specs=(frames,) * 4 + (flat,) * 10 + (P(), P()),
        check_vma=False,
    )
```

profile of v0, /device:TPU:0, one launch (start us, length us, event | category | flops | bytes accessed | tf_op | source)
XLA Modules:
  0.0 402.4 jit_solution(5687085976101581082)
XLA Ops:
  12.3 5.1 %collective-permute-start.2 = (bf16[1,152,256]{2,1,0:T(8,128)(2,1)S(1)}, bf16[1,152,256]{2,1,0:T(8,128)(2,1)S(1)}, u32[]{:S(2)}, u32[]{:S(2)}) collective-permute-start(bf16[1,152,256]{2,1,0:T(8,128)(2,1)S(1)} %pad_bitcast_fusion.1), channel_id=1, source_target_pairs={{0,12},{1,13},{2,14},{3,15},{4,8},{5,9},{6,10},{7,11},{8,4},{9,5},... | collective-permute-start | bytes 233480 | tf_op jit(solution)/shard_map/ppermute | solution.py:29
  20.2 3.7 collective-permute-start.12
  39.2 6.5 %collective-permute-done.5 = bf16[4,152,256]{2,1,0:T(8,128)(2,1)S(1)} collective-permute-done((bf16[4,152,256]{2,1,0:T(8,128)(2,1)S(1)}, bf16[4,152,256]{2,1,0:T(8,128)(2,1)S(1)}, u32[]{:S(2)}, u32[]{:S(2)}) %collective-permute-start.5) | collective-permute-done | bytes 311328 | tf_op jit(solution)/shard_map/ppermute | solution.py:29
  46.7 3.7 collective-permute-done.4
  60.7 5.1 %collective-permute-start.7 = (bf16[2,2,196,128]{3,2,1,0:T(8,128)(2,1)}, bf16[2,2,196,128]{3,2,1,0:T(8,128)(2,1)S(1)}, u32[]{:S(2)}, u32[]{:S(2)}) collective-permute-start(bf16[2,2,196,128]{3,2,1,0:T(8,128)(2,1)} %slice.253), channel_id=1, source_target_pairs={{0,1},{1,2},{2,3},{3,4},{4,5},{5,6},{6,7},{7,8},{8,9},{9,10},{10,1... | collective-permute-start | bytes 602120 | tf_op jit(solution)/shard_map/ppermute | solution.py:169
  75.6 13.3 %all-gather.2.cloned.1.call-done.refs_2_.refs_7_.refs_3_ = bf16[1280,1024]{1,0:T(8,128)(2,1)} async-done(((bf16[40,1024]{1,0:T(8,128)(2,1)}), bf16[1280,1024]{1,0:T(8,128)(2,1)}) %all-gather.2.cloned.1.call-update) | async-done | bytes 2621456 | tf_op jit(solution)/shard_map/all_gather | solution.py:969
  91.5 3.3 lateral_and_fast_time.1
  110.7 4.6 %slow_time_taps.1 = (bf16[8,208,256]{2,1,0:T(8,128)(2,1)S(1)}, f32[8,208,768]{2,1,0:T(8,128)S(1)}, bf16[2,208,256]{2,1,0:T(8,128)(2,1)S(1)}, bf16[2,208,256]{2,1,0:T(8,128)(2,1)S(1)}) custom-call(f32[8]{0:T(128)S(1)} %reshape.581.refs_0_, f32[8,208,256]{2,1,0:T(8,128)S(1)} %get-tuple-element.168.refs_1_.refs_8_, ...), custom_call_target="tpu_custom_call" | custom-call | flops 3271557120 | bytes 14561312 | tf_op jit(solution)/shard_map/slow_time_taps/pallas_call | solution.py:262
  122.4 6.1 %shortcut_and_fast_space.1 = (f32[8,208,1024]{2,1,0:T(8,128)S(1)}, bf16[8,208,384]{2,1,0:T(8,128)(2,1)S(1)}, f32[8,208,128]{2,1,0:T(8,128)S(1)}, f32[2,2,1152]{2,1,0:T(2,128)S(1)}, bf16[384,384]{1,0:T(8,128)(2,1)S(1)}) custom-call(bf16[8,208,1024]{2,1,0:T(8,128)(2,1)S(1)} %bitcast.331, bf16[8,208,256]{2,1,0:T(8,128)(2,1)S(1)} %get-tuple-element.184.refs_1_, ...), custom_call_target="tpu_custom_call" | custom-call | flops 4362076160 | bytes 18087936 | tf_op jit(solution)/shard_map/shortcut_and_fast_space/pallas_call | solution.py:262
  133.5 4.5 %collective-permute-start.24 = (f32[2,2,1408]{2,1,0:T(2,128)S(1)}, f32[2,2,1408]{2,1,0:T(2,128)S(1)}, u32[]{:S(2)}, u32[]{:S(2)}) collective-permute-start(f32[2,2,1408]{2,1,0:T(2,128)S(1)} %get-tuple-element.191), channel_id=1, source_target_pairs={{0,16},{1,17},{2,18},{3,19},{4,20},{5,21},{6,22},{7,23},{8,24},{9,... | collective-permute-start | bytes 67592 | tf_op jit(solution)/shard_map/ppermute | solution.py:29
  139.0 3.4 collective-permute-start.26
  145.0 3.7 collective-permute-start.29
  150.5 3.9 slow_space.1
  194.0 4.1 %fast_out.1 = (bf16[8,4,196,128]{3,2,1,0:T(8,128)(2,1)S(1)}, f32[8,208,512]{2,1,0:T(8,128)S(1)}, f32[2,2,512]{2,1,0:T(2,128)S(1)}) custom-call(f32[8,208,512]{2,1,0:T(8,128)S(1)} %copy-done.3, bf16[8,4,196,128]{3,2,1,0:T(8,128)(2,1)S(1)} %bitcast.325, bf16[8,208,512]{2,1,0:T(8,128)(2,1)S(1)} %copy-done.21, ...), custom_call_target="tpu_custom_call" | custom-call | flops 170393600 | bytes 11757568 | tf_op jit(solution)/shard_map/fast_out/pallas_call | solution.py:262
  201.2 10.5 %slow_out.1 = (bf16[8,196,1024]{2,1,0:T(8,128)(2,1)S(1)}, f32[8,208,1024]{2,1,0:T(8,128)S(1)}, f32[2,3,1536]{2,1,0:T(4,128)S(1)}) custom-call(bf16[8,208,256]{2,1,0:T(8,128)(2,1)S(1)} %get-tuple-element.204.refs_0_, bf16[256,1024]{1,0:T(8,128)(2,1)S(1)} %pad_maximum_fusion.6.refs_3_.refs_1_, f32[8,208,1024]{2,1,0:T(8,128)S(1)} %bitcast.318, ...), custom_call_target="tpu_custom_call" | custom-call | flops 872415232 | bytes 21733376 | tf_op jit(solution)/shard_map/slow_out/pallas_call | solution.py:262
  230.1 10.2 %back_three.1 = (bf16[8,208,1024]{2,1,0:T(8,128)(2,1)S(1)}, bf16[8,208,1024]{2,1,0:T(8,128)(2,1)S(1)}, f32[8,208,256]{2,1,0:T(8,128)S(1)}, bf16[8,208,512]{2,1,0...) custom-call(bf16[8,208,256]{2,1,0:T(8,128)(2,1)S(1)} %get-tuple-element.204.refs_0_, ...), custom_call_target="tpu_custom_call" | custom-call | flops 1744830464 | bytes 36773888 | tf_op jit(solution)/shard_map/back_three/pallas_call | solution.py:262
  240.4 5.0 %projection_grad.1 = bf16[1280,1024]{1,0:T(8,128)(2,1)S(1)} custom-call(bf16[8,208,1024]{2,1,0:T(8,128)(2,1)S(1)} %bitcast.332, bf16[8,208,256]{2,1,0:T(8,128)(2,1)S(1)} %copy-done.70, bf16[8,208,1024]{2,1,0:T(8,128)(2,1)S(1)} %get-tuple-element.216.refs_2_.refs_5_.refs_1_), custom_call_target="tpu_custom_call" | custom-call | flops 4362076160 | bytes 10289152 | tf_op jit(solution)/shard_map/projection_grad/pallas_call | solution.py:262
  263.0 6.4 %back_two.1 = (bf16[8,208,768]{2,1,0:T(8,128)(2,1)S(1)}, f32[8,208,256]{2,1,0:T(8,128)S(1)}, bf16[8,208,384]{2,1,0:T(8,128)(2,1)S(1)}, f32[8,208,128]{2,1,0:T(8,128)S(1)}, f32[2,2,384]{2,1,0:T(2,128)S(1)}) custom-call(f32[8,208,256]{2,1,0:T(8,128)S(1)} %get-tuple-element.202.refs_0_.refs_8_, f32[2,2,768]{2,1,0:T(2,128)S(1)} %add_add_fusion.9.refs_1_.refs_3_.refs_9_, ...), custom_call_target="tpu_custom_call" | custom-call | flops 1962934272 | bytes 16678912 | tf_op jit(solution)/shard_map/back_two/pallas_call | solution.py:262
  269.5 3.3 slow_space_grad.1
  285.7 4.2 %copy.236 = bf16[2,4,196,1024]{3,1,2,0:T(4,128)(2,1)} copy(bf16[2,4,196,1024]{3,2,1,0:T(8,128)(2,1)S(1)} %bitcast.334) | data formatting | bytes 6422528 | tf_op jit(solution)/shard_map/reshape | solution.py:1178
  292.0 3.0 collective-permute-start.71
  296.6 5.4 %collective-permute-start.76 = (bf16[1,48,1024]{2,1,0:T(8,128)(2,1)S(1)}, bf16[1,48,1024]{2,1,0:T(8,128)(2,1)S(1)}, u32[]{:S(2)}, u32[]{:S(2)}) collective-permute-start(bf16[1,48,1024]{2,1,0:T(8,128)(2,1)S(1)} %get-tuple-element.409), channel_id=1, source_target_pairs={{0,12},{1,13},{2,14},{3,15},{4,8},{5,9},{6,10},{7,11},{8,4},{9,5},... | collective-permute-start | bytes 294920 | tf_op jit(solution)/shard_map/ppermute | solution.py:29
  302.7 3.1 collective-permute-done.71.refs_3_.refs_6_
  307.2 3.6 back_lateral.1
  310.9 3.8 slow_time_grad.1
  319.6 3.2 collective-permute-start.79
  339.4 3.1 lateral_grad.1
  348.8 6.6 %slow_in_grad.1 = bf16[8,196,1024]{2,1,0:T(8,128)(2,1)S(1)} custom-call(bf16[8,208,768]{2,1,0:T(8,128)(2,1)S(1)} %copy-done.64, bf16[8,208,1024]{2,1,0:T(8,128)(2,1)S(1)} %copy-done.31, bf16[1280,768]{1,0:T(8,128)(2,1)S(1)} %copy-done.10, bf16[1280,1024]{1,0:T(8,128)(2,1)S(1)} %copy-done.39), custom_call_target="tpu_custom_call" | custom-call | flops 6106906624 | bytes 13762560 | tf_op jit(solution)/shard_map/slow_in_grad/pallas_call | solution.py:262
  358.9 6.1 %collective-permute-done.84.refs_4_ = bf16[2,208,256]{2,1,0:T(8,128)(2,1)S(1)} collective-permute-done((bf16[2,208,256]{2,1,0:T(8,128)(2,1)S(1)}, bf16[2,208,256]{2,1,0:T(8,128)(2,1)S(1)}, u32[]{:S(2)}, u32[]{:S(2)}) %collective-permute-start.84) | collective-permute-done | bytes 213024 | tf_op jit(solution)/shard_map/ppermute | solution.py:174
  365.1 4.2 %collective-permute-start.94 = (bf16[4,48,128]{2,1,0:T(8,128)(2,1)S(1)}, bf16[4,48,128]{2,1,0:T(8,128)(2,1)S(1)}, u32[]{:S(2)}, u32[]{:S(2)}) collective-permute-start(bf16[4,48,128]{2,1,0:T(8,128)(2,1)S(1)} %get-tuple-element.416), channel_id=1, source_target_pairs={{0,3},{1,2},{2,1},{3,0},{4,7},{5,6},{6,5},{7,4},{8,11},{9,10},{10,... | collective-permute-start | bytes 147464 | tf_op jit(solution)/shard_map/ppermute | solution.py:29
  379.3 3.0 collective-permute-done.90
  386.0 4.2 %copy.193 = bf16[2,4,196,1024]{3,1,2,0:T(4,128)(2,1)} copy(bf16[2,4,196,1024]{3,2,1,0:T(8,128)(2,1)S(1)} %bitcast.335) | data formatting | bytes 6422528
  (550 shorter events, 226.0 us)
Async XLA Ops:
  7.2 81.7 %all-gather.2.cloned.1.call-start = ((), (), s32[]{:S(2)}) async-start(), calls=%async_computation | async-start | bytes 2703360 | tf_op jit(solution)/shard_map/all_gather | solution.py:969
  12.3 20.9 %collective-permute-start.2 = (bf16[1,152,256]{2,1,0:T(8,128)(2,1)S(1)}, bf16[1,152,256]{2,1,0:T(8,128)(2,1)S(1)}, u32[]{:S(2)}, u32[]{:S(2)}) collective-permute-start(bf16[1,152,256]{2,1,0:T(8,128)(2,1)S(1)} %pad_bitcast_fusion.1), channel_id=1, source_target_pairs={{0,12},{1,13},{2,14},{3,15},{4,8},{5,9},{6,10},{7,11},{8,4},{9,5},... | collective-permute-start | bytes 233480 | tf_op jit(solution)/shard_map/ppermute | solution.py:29
  17.4 15.8 %collective-permute-start.1 = (bf16[1,152,256]{2,1,0:T(8,128)(2,1)S(1)}, bf16[1,152,256]{2,1,0:T(8,128)(2,1)S(1)}, u32[]{:S(2)}, u32[]{:S(2)}) collective-permute-start(bf16[1,152,256]{2,1,0:T(8,128)(2,1)S(1)} %pad_bitcast_fusion.1), channel_id=1, source_target_pairs={{0,8},{1,9},{2,10},{3,11},{4,12},{5,13},{6,14},{7,15},{8,0},{9,1},... | collective-permute-start | bytes 233480 | tf_op jit(solution)/shard_map/ppermute | solution.py:29
  17.4 15.8 %collective-permute-start = (bf16[1,152,256]{2,1,0:T(8,128)(2,1)S(1)}, bf16[1,152,256]{2,1,0:T(8,128)(2,1)}, u32[]{:S(2)}, u32[]{:S(2)}) collective-permute-start(bf16[1,152,256]{2,1,0:T(8,128)(2,1)S(1)} %pad_bitcast_fusion.1), channel_id=1, source_target_pairs={{0,4},{1,5},{2,6},{3,7},{4,0},{5,1},{6,2},{7,3},{8,12},{9,13},{10,... | collective-permute-start | bytes 233480 | tf_op jit(solution)/shard_map/ppermute | solution.py:29
  20.2 76.0 %collective-permute-start.12 = (bf16[1,104,256]{2,1,0:T(8,128)(2,1)}, bf16[1,104,256]{2,1,0:T(8,128)(2,1)}, u32[]{:S(2)}, u32[]{:S(2)}) collective-permute-start(bf16[1,104,256]{2,1,0:T(8,128)(2,1)} %maximum_bitcast_fusion.3), channel_id=1, source_target_pairs={{0,12},{1,13},{2,14},{3,15},{4,8},{5,9},{6,10},{7,11},{8,4},{9,5},... | collective-permute-start | bytes 159752 | tf_op jit(solution)/shard_map/ppermute | solution.py:29
  23.9 72.2 %collective-permute-start.11 = (bf16[1,104,256]{2,1,0:T(8,128)(2,1)}, bf16[1,104,256]{2,1,0:T(8,128)(2,1)}, u32[]{:S(2)}, u32[]{:S(2)}) collective-permute-start(bf16[1,104,256]{2,1,0:T(8,128)(2,1)} %maximum_bitcast_fusion.3), channel_id=1, source_target_pairs={{0,8},{1,9},{2,10},{3,11},{4,12},{5,13},{6,14},{7,15},{8,0},{9,1},... | collective-permute-start | bytes 159752 | tf_op jit(solution)/shard_map/ppermute | solution.py:29
  34.2 11.6 %collective-permute-start.5 = (bf16[4,152,256]{2,1,0:T(8,128)(2,1)S(1)}, bf16[4,152,256]{2,1,0:T(8,128)(2,1)S(1)}, u32[]{:S(2)}, u32[]{:S(2)}) collective-permute-start(bf16[4,152,256]{2,1,0:T(8,128)(2,1)S(1)} %maximum_bitcast_fusion.1), channel_id=1, source_target_pairs={{0,3},{1,2},{2,1},{3,0},{4,7},{5,6},{6,5},{7,4},{8,11},{9,10},{10,... | collective-permute-start | bytes 933896 | tf_op jit(solution)/shard_map/ppermute | solution.py:29
  36.7 13.7 %collective-permute-start.4 = (bf16[4,152,256]{2,1,0:T(8,128)(2,1)S(1)}, bf16[4,152,256]{2,1,0:T(8,128)(2,1)S(1)}, u32[]{:S(2)}, u32[]{:S(2)}) collective-permute-start(bf16[4,152,256]{2,1,0:T(8,128)(2,1)S(1)} %maximum_bitcast_fusion.1), channel_id=1, source_target_pairs={{0,2},{1,3},{2,0},{3,1},{4,6},{5,7},{6,4},{7,5},{8,10},{9,11},{10,... | collective-permute-start | bytes 933896 | tf_op jit(solution)/shard_map/ppermute | solution.py:29
  37.2 13.2 %collective-permute-start.3 = (bf16[4,152,256]{2,1,0:T(8,128)(2,1)S(1)}, bf16[4,152,256]{2,1,0:T(8,128)(2,1)S(1)}, u32[]{:S(2)}, u32[]{:S(2)}) collective-permute-start(bf16[4,152,256]{2,1,0:T(8,128)(2,1)S(1)} %maximum_bitcast_fusion.1), channel_id=1, source_target_pairs={{0,1},{1,0},{2,3},{3,2},{4,5},{5,4},{6,7},{7,6},{8,9},{9,8},{10,11... | collective-permute-start | bytes 933896 | tf_op jit(solution)/shard_map/ppermute | solution.py:29
  45.8 50.4 %collective-permute-start.10 = (bf16[1,104,256]{2,1,0:T(8,128)(2,1)}, bf16[1,104,256]{2,1,0:T(8,128)(2,1)}, u32[]{:S(2)}, u32[]{:S(2)}) collective-permute-start(bf16[1,104,256]{2,1,0:T(8,128)(2,1)} %maximum_bitcast_fusion.3), channel_id=1, source_target_pairs={{0,4},{1,5},{2,6},{3,7},{4,0},{5,1},{6,2},{7,3},{8,12},{9,13},{10,... | collective-permute-start | bytes 159752 | tf_op jit(solution)/shard_map/ppermute | solution.py:29
  52.4 36.6 %collective-permute-start.8 = (bf16[2,1,196,128]{3,2,1,0:T(8,128)(2,1)}, bf16[2,1,196,128]{3,2,1,0:T(8,128)(2,1)}, u32[]{:S(2)}, u32[]{:S(2)}) collective-permute-start(bf16[2,1,196,128]{3,2,1,0:T(8,128)(2,1)} %slice_multiply_fusion), channel_id=1, source_target_pairs={{1,0},{2,1},{3,2},{4,3},{5,4},{6,5},{7,6},{8,7},{9,8},{10,9},{11,1... | collective-permute-start | bytes 301064 | tf_op jit(solution)/shard_map/ppermute | solution.py:174
  60.7 28.2 %collective-permute-start.7 = (bf16[2,2,196,128]{3,2,1,0:T(8,128)(2,1)}, bf16[2,2,196,128]{3,2,1,0:T(8,128)(2,1)S(1)}, u32[]{:S(2)}, u32[]{:S(2)}) collective-permute-start(bf16[2,2,196,128]{3,2,1,0:T(8,128)(2,1)} %slice.253), channel_id=1, source_target_pairs={{0,1},{1,2},{2,3},{3,4},{4,5},{5,6},{6,7},{7,8},{8,9},{9,10},{10,1... | collective-permute-start | bytes 602120 | tf_op jit(solution)/shard_map/ppermute | solution.py:169
  118.0 20.9 %collective-permute-start.25 = (bf16[16,104,256]{2,1,0:T(8,128)(2,1)S(1)}, bf16[16,104,256]{2,1,0:T(8,128)(2,1)S(1)}, u32[]{:S(2)}, u32[]{:S(2)}) collective-permute-start(bf16[16,104,256]{2,1,0:T(8,128)(2,1)S(1)} %bitcast.355), channel_id=1, source_target_pairs={{0,16},{1,17},{2,18},{3,19},{4,20},{5,21},{6,22},{7,23},{8,24},{9,... | collective-permute-start | bytes 2555912 | tf_op jit(solution)/shard_map/ppermute | solution.py:29
  118.1 13.2 %collective-permute-start.22 = (bf16[2,208,256]{2,1,0:T(8,128)(2,1)S(1)}, bf16[2,208,256]{2,1,0:T(8,128)(2,1)S(1)}, u32[]{:S(2)}, u32[]{:S(2)}) collective-permute-start(bf16[2,208,256]{2,1,0:T(8,128)(2,1)S(1)} %get-tuple-element.182), channel_id=1, source_target_pairs={{0,1},{1,2},{2,3},{3,4},{4,5},{5,6},{6,7},{7,8},{8,9},{9,10},{10,1... | collective-permute-start | bytes 638984 | tf_op jit(solution)/shard_map/ppermute | solution.py:169
  120.9 11.6 %collective-permute-start.23 = (bf16[2,208,256]{2,1,0:T(8,128)(2,1)S(1)}, bf16[2,208,256]{2,1,0:T(8,128)(2,1)S(1)}, u32[]{:S(2)}, u32[]{:S(2)}) collective-permute-start(bf16[2,208,256]{2,1,0:T(8,128)(2,1)S(1)} %get-tuple-element.183), channel_id=1, source_target_pairs={{1,0},{2,1},{3,2},{4,3},{5,4},{6,5},{7,6},{8,7},{9,8},{10,9},{11,1... | collective-permute-start | bytes 638984 | tf_op jit(solution)/shard_map/ppermute | solution.py:174
  186.6 14.5 %collective-permute-start.45 = (f32[2,2,1024]{2,1,0:T(2,128)S(1)}, f32[2,2,1024]{2,1,0:T(2,128)S(1)}, u32[]{:S(2)}, u32[]{:S(2)}) collective-permute-start(f32[2,2,1024]{2,1,0:T(2,128)S(1)} %add_add_fusion.8), channel_id=1, source_target_pairs={{0,12},{1,13},{2,14},{3,15},{4,8},{5,9},{6,10},{7,11},{8,4},{9,5},... | collective-permute-start | bytes 49160 | tf_op jit(solution)/shard_map/ppermute | solution.py:29
  188.0 13.1 %collective-permute-start.44 = (f32[2,2,1024]{2,1,0:T(2,128)S(1)}, f32[2,2,1024]{2,1,0:T(2,128)S(1)}, u32[]{:S(2)}, u32[]{:S(2)}) collective-permute-start(f32[2,2,1024]{2,1,0:T(2,128)S(1)} %add_add_fusion.8), channel_id=1, source_target_pairs={{0,8},{1,9},{2,10},{3,11},{4,12},{5,13},{6,14},{7,15},{8,0},{9,1},... | collective-permute-start | bytes 49160 | tf_op jit(solution)/shard_map/ppermute | solution.py:29
  189.0 12.1 %collective-permute-start.43 = (f32[2,2,1024]{2,1,0:T(2,128)S(1)}, f32[2,2,1024]{2,1,0:T(2,128)S(1)}, u32[]{:S(2)}, u32[]{:S(2)}) collective-permute-start(f32[2,2,1024]{2,1,0:T(2,128)S(1)} %add_add_fusion.8), channel_id=1, source_target_pairs={{0,4},{1,5},{2,6},{3,7},{4,0},{5,1},{6,2},{7,3},{8,12},{9,13},{10,... | collective-permute-start | bytes 49160 | tf_op jit(solution)/shard_map/ppermute | solution.py:29
  259.4 21.8 %collective-permute-start.67 = (bf16[4,48,1024]{2,1,0:T(8,128)(2,1)S(1)}, bf16[4,48,1024]{2,1,0:T(8,128)(2,1)S(1)}, u32[]{:S(2)}, u32[]{:S(2)}) collective-permute-start(bf16[4,48,1024]{2,1,0:T(8,128)(2,1)S(1)} %get-tuple-element.381), channel_id=1, source_target_pairs={{0,3},{1,2},{2,1},{3,0},{4,7},{5,6},{6,5},{7,4},{8,11},{9,10},{10,... | collective-permute-start | bytes 1179656 | tf_op jit(solution)/shard_map/ppermute | solution.py:29
  259.6 21.6 %collective-permute-start.65 = (bf16[4,48,1024]{2,1,0:T(8,128)(2,1)S(1)}, bf16[4,48,1024]{2,1,0:T(8,128)(2,1)S(1)}, u32[]{:S(2)}, u32[]{:S(2)}) collective-permute-start(bf16[4,48,1024]{2,1,0:T(8,128)(2,1)S(1)} %get-tuple-element.382), channel_id=1, source_target_pairs={{0,1},{1,0},{2,3},{3,2},{4,5},{5,4},{6,7},{7,6},{8,9},{9,8},{10,11... | collective-permute-start | bytes 1179656 | tf_op jit(solution)/shard_map/ppermute | solution.py:29
  260.9 20.3 %collective-permute-start.66 = (bf16[4,48,1024]{2,1,0:T(8,128)(2,1)S(1)}, bf16[4,48,1024]{2,1,0:T(8,128)(2,1)S(1)}, u32[]{:S(2)}, u32[]{:S(2)}) collective-permute-start(bf16[4,48,1024]{2,1,0:T(8,128)(2,1)S(1)} %get-tuple-element.383), channel_id=1, source_target_pairs={{0,2},{1,3},{2,0},{3,1},{4,6},{5,7},{6,4},{7,5},{8,10},{9,11},{10,... | collective-permute-start | bytes 1179656 | tf_op jit(solution)/shard_map/ppermute | solution.py:29
  292.0 13.7 %collective-permute-start.71 = (bf16[2,208,384]{2,1,0:T(8,128)(2,1)S(1)}, bf16[2,208,384]{2,1,0:T(8,128)(2,1)S(1)}, u32[]{:S(2)}, u32[]{:S(2)}) collective-permute-start(bf16[2,208,384]{2,1,0:T(8,128)(2,1)S(1)} %get-tuple-element.244), channel_id=1, source_target_pairs={{0,1},{1,2},{2,3},{3,4},{4,5},{5,6},{6,7},{7,8},{8,9},{9,10},{10,1... | collective-permute-start | bytes 958472 | tf_op jit(solution)/shard_map/ppermute | solution.py:169
  295.0 12.1 %collective-permute-start.72 = (bf16[2,208,384]{2,1,0:T(8,128)(2,1)S(1)}, bf16[2,208,384]{2,1,0:T(8,128)(2,1)S(1)}, u32[]{:S(2)}, u32[]{:S(2)}) collective-permute-start(bf16[2,208,384]{2,1,0:T(8,128)(2,1)S(1)} %get-tuple-element.245), channel_id=1, source_target_pairs={{1,0},{2,1},{3,2},{4,3},{5,4},{6,5},{7,6},{8,7},{9,8},{10,9},{11,1... | collective-permute-start | bytes 958472 | tf_op jit(solution)/shard_map/ppermute | solution.py:174
  296.6 18.2 %collective-permute-start.76 = (bf16[1,48,1024]{2,1,0:T(8,128)(2,1)S(1)}, bf16[1,48,1024]{2,1,0:T(8,128)(2,1)S(1)}, u32[]{:S(2)}, u32[]{:S(2)}) collective-permute-start(bf16[1,48,1024]{2,1,0:T(8,128)(2,1)S(1)} %get-tuple-element.409), channel_id=1, source_target_pairs={{0,12},{1,13},{2,14},{3,15},{4,8},{5,9},{6,10},{7,11},{8,4},{9,5},... | collective-permute-start | bytes 294920 | tf_op jit(solution)/shard_map/ppermute | solution.py:29
  302.1 12.8 %collective-permute-start.75 = (bf16[1,48,1024]{2,1,0:T(8,128)(2,1)S(1)}, bf16[1,48,1024]{2,1,0:T(8,128)(2,1)S(1)}, u32[]{:S(2)}, u32[]{:S(2)}) collective-permute-start(bf16[1,48,1024]{2,1,0:T(8,128)(2,1)S(1)} %get-tuple-element.410), channel_id=1, source_target_pairs={{0,8},{1,9},{2,10},{3,11},{4,12},{5,13},{6,14},{7,15},{8,0},{9,1},... | collective-permute-start | bytes 294920 | tf_op jit(solution)/shard_map/ppermute | solution.py:29
  302.1 12.8 %collective-permute-start.74 = (bf16[1,48,1024]{2,1,0:T(8,128)(2,1)S(1)}, bf16[1,48,1024]{2,1,0:T(8,128)(2,1)S(1)}, u32[]{:S(2)}, u32[]{:S(2)}) collective-permute-start(bf16[1,48,1024]{2,1,0:T(8,128)(2,1)S(1)} %get-tuple-element.411), channel_id=1, source_target_pairs={{0,4},{1,5},{2,6},{3,7},{4,0},{5,1},{6,2},{7,3},{8,12},{9,13},{10,... | collective-permute-start | bytes 294920 | tf_op jit(solution)/shard_map/ppermute | solution.py:29
  326.4 11.3 %collective-permute-start.83 = (f32[2,2,256]{2,1,0:T(2,128)S(1)}, f32[2,2,256]{2,1,0:T(2,128)S(1)}, u32[]{:S(2)}, u32[]{:S(2)}) collective-permute-start(f32[2,2,256]{2,1,0:T(2,128)S(1)} %add_add_fusion.18), channel_id=1, source_target_pairs={{0,12},{1,13},{2,14},{3,15},{4,8},{5,9},{6,10},{7,11},{8,4},{9,5},... | collective-permute-start | bytes 12296 | tf_op jit(solution)/shard_map/ppermute | solution.py:29
  334.2 30.8 %collective-permute-start.87 = (bf16[4,192,256]{2,1,0:T(8,128)(2,1)}, bf16[4,192,256]{2,1,0:T(8,128)(2,1)}, u32[]{:S(2)}, u32[]{:S(2)}) collective-permute-start(bf16[4,192,256]{2,1,0:T(8,128)(2,1)} %get-tuple-element.378), channel_id=1, source_target_pairs={{0,3},{1,2},{2,1},{3,0},{4,7},{5,6},{6,5},{7,4},{8,11},{9,10},{10,... | collective-permute-start | bytes 1179656 | tf_op jit(solution)/shard_map/ppermute | solution.py:29
  336.6 28.5 %collective-permute-start.85 = (bf16[4,192,256]{2,1,0:T(8,128)(2,1)}, bf16[4,192,256]{2,1,0:T(8,128)(2,1)}, u32[]{:S(2)}, u32[]{:S(2)}) collective-permute-start(bf16[4,192,256]{2,1,0:T(8,128)(2,1)} %get-tuple-element.379), channel_id=1, source_target_pairs={{0,1},{1,0},{2,3},{3,2},{4,5},{5,4},{6,7},{7,6},{8,9},{9,8},{10,11... | collective-permute-start | bytes 1179656 | tf_op jit(solution)/shard_map/ppermute | solution.py:29
  337.7 27.3 %collective-permute-start.86 = (bf16[4,192,256]{2,1,0:T(8,128)(2,1)}, bf16[4,192,256]{2,1,0:T(8,128)(2,1)}, u32[]{:S(2)}, u32[]{:S(2)}) collective-permute-start(bf16[4,192,256]{2,1,0:T(8,128)(2,1)} %get-tuple-element.380), channel_id=1, source_target_pairs={{0,2},{1,3},{2,0},{3,1},{4,6},{5,7},{6,4},{7,5},{8,10},{9,11},{10,... | collective-permute-start | bytes 1179656 | tf_op jit(solution)/shard_map/ppermute | solution.py:29
  382.4 10.5 %collective-permute-start.95 = (bf16[1,48,128]{2,1,0:T(8,128)(2,1)S(1)}, bf16[1,48,128]{2,1,0:T(8,128)(2,1)S(1)}, u32[]{:S(2)}, u32[]{:S(2)}) collective-permute-start(bf16[1,48,128]{2,1,0:T(8,128)(2,1)S(1)} %get-tuple-element.427), channel_id=1, source_target_pairs={{0,4},{1,5},{2,6},{3,7},{4,0},{5,1},{6,2},{7,3},{8,12},{9,13},{10,... | collective-permute-start | bytes 36872 | tf_op jit(solution)/shard_map/ppermute | solution.py:29
  382.4 10.5 %collective-permute-start.97 = (bf16[1,48,128]{2,1,0:T(8,128)(2,1)S(1)}, bf16[1,48,128]{2,1,0:T(8,128)(2,1)S(1)}, u32[]{:S(2)}, u32[]{:S(2)}) collective-permute-start(bf16[1,48,128]{2,1,0:T(8,128)(2,1)S(1)} %get-tuple-element.428), channel_id=1, source_target_pairs={{0,12},{1,13},{2,14},{3,15},{4,8},{5,9},{6,10},{7,11},{8,4},{9,5},... | collective-permute-start | bytes 36872 | tf_op jit(solution)/shard_map/ppermute | solution.py:29
  (157 other events, 1177.2 us)
Sparse Core Ops, SparseCore 0:
  25.6 63.2 all-gather.1
where the time goes:
time: 409 us; the launch traced here: 402 us
  starting transfers between devices  130 us (32%)
  Pallas kernels  84.4 us (21%)
  local copies, waits for them, and re-layouts  83.1 us (20%)
  waiting for transfers between devices  70.7 us (17%)
  other arithmetic  17.9 us (4%)
  between operations  16.3 us (4%)
    ppermute x91, starting transfers between devices, swap(): return lax.ppermute(value, AXES, [(i, i ^ bit) for i in range(count)])  114 us
    pallas_call x21, Pallas kernels, call(): pl.pallas_call(kernel, in_specs=[pl.BlockSpec(memory_space=pltpu.SMEM) if...  84.4 us
    unnamed x207, local copies, waits for them, and re-layouts  47.5 us
    ppermute x91, waiting for transfers between devices, swap(): return lax.ppermute(value, AXES, [(i, i ^ bit) for i in range(count)])  45.7 us
    all_gather x1, waiting for transfers between devices, local(): lax.all_gather(w_projection.reshape(-1, CS), AXES, axis=0, tiled=True)  13.3 us
    ppermute x3, starting transfers between devices, from_before(): return lax.ppermute(value, AXES, [(i, i + 1) for i in range(count - 1)])  10.8 us
    ppermute x4, waiting for transfers between devices, from_after(): return lax.ppermute(value, AXES, [(i + 1, i) for i in range(count - 1)])  8.63 us
  transfers between devices with their start and end apart: 99, of which 37 were waited for; matrix products, arithmetic and copies ran while one was open for 15% of the time, Pallas kernels for 14%

commit v1 on v0

--- a/solution.py
+++ b/solution.py
@@ -222,7 +222,7 @@
     return pltpu.with_memory_space_constraint(array, pltpu.VMEM)
 
 
-def call(body, steps, ins, outs, scratch=(), flops=0, name=None, limit=16, unroll=False, state=None):
+def call(body, steps, ins, outs, scratch=(), flops=0, name=None, limit=8, unroll=False, state=None):
     names = [given[0] if len(given) == 2 else None for given in outs]
     ins = [group(state[given[0]], given[1]) if len(given) == 2 else given for given in ins]
     if state is not None:
@@ -422,6 +422,77 @@
     )
 
 
+def k_prep(
+    step, near, w_time, w_first, w_back, fproj, fspace, gb, wide, lat, fast, *, shares
+):
+    places = [sum(shares[:n]) for n in range(len(shares))]
+    devices = near.shape[0]
+    starts = [0, 3 * CF, 3 * CF + 9 * CFM]
+    for d in range(devices):
+        block = near[d].astype(F32)
+        parts = [block[at : at + rows] for at, rows in zip(places, shares)]
+        wide[d * shares[0] : (d + 1) * shares[0]] = parts[0]
+        lat[d * shares[1] : (d + 1) * shares[1]] = parts[1]
+        for start, part in zip(starts, parts[2:5]):
+            at = start + d * part.shape[0]
+            fast[at : at + part.shape[0]] = part[:, :128]
+    for tap in range(3):
+        rows = CS + CL
+        w_time[:, tap * CM : (tap + 1) * CM] = wide[tap * rows : (tap + 1) * rows].astype(BF)
+
+    w_first[...] = jnp.zeros_like(w_first)
+    w_first[: 3 * CF, :CL] = lat[2 * CF :].astype(BF)
+    w_first[4 * CF : 6 * CF, :CL] = lat[: 2 * CF].astype(BF)
+    taps = [fast[k * CF : (k + 1) * CF] for k in range(3)]
+    order = [5, 0, 1, 2, 3, 6]
+    for block in range(7):
+        band = [
+            pltpu.roll(taps[k], q * CFM, 1) if q else taps[k]
+            for q in range(4)
+            for k in range(3)
+            if order[q + k] == block
+        ]
+        if band:
+            w_first[block * CF : (block + 1) * CF, CL:] = sum(band).astype(BF)
+    w_back[...] = jnp.zeros_like(w_back)
+    w_back[:, : CL + 128] = w_first[: 4 * CF]
+    w_back[2 * CF :, CL + 128 : 2 * CL + 128] = lat[: 2 * CF].astype(BF)
+    w_back[:CF, 2 * CL + 128 :] = pltpu.roll(taps[2], 3 * CFM, 1).astype(BF)
+    w_back[3 * CF :, 2 * CL + 128 :] = taps[0].astype(BF)
+
+    fproj[...] = jnp.zeros_like(fproj)
+    last = fast[starts[2] : starts[2] + CFM].astype(BF)
+    for q in range(4):
+        fproj[q * CFM : (q + 1) * CFM, q * CF : (q + 1) * CF] = last
+    for a in range(3):
+        for c in range(3):
+            at = starts[1] + (3 * a + c) * CFM
+            tap = fast[at : at + CFM]
+            for q in range(4):
+                rows = c * 128 + q * CFM
+                moved = pltpu.roll(tap, q * CFM, 1) if q else tap
+                fspace[rows : rows + CFM, a * 128 : (a + 1) * 128] = moved.astype(BF)
+
+    lane = lax.broadcasted_iota(jnp.int32, (8, 128), 1)
+    extent = gb.shape[1] // devices
+    for row in range(2):
+        own = [
+            jnp.broadcast_to(
+                near[d, places[5 + row] : places[5 + row] + 1, :128].astype(F32), (8, 128)
+            )
+            for d in range(devices)
+        ]
+        for tile in range(gb.shape[1] // 128):
+            value = jnp.zeros((8, 128), F32)
+            for d in range(devices):
+                at = d * extent - tile * 128
+                if -extent < at < 128:
+                    mine = (lane >= at) & (lane < at + extent)
+                    moved = pltpu.roll(own[d], at % 128, 1) if at % 128 else own[d]
+                    value = jnp.where(mine, moved, value)
+            gb[row : row + 1, tile * 128 : (tile + 1) * 128] = value[0:1]
+
+
 def fill_z(z, at, links, nexts, fast, edge_down, edge_up):
     frames = fast.shape[0]
     for f in range(frames):
@@ -458,25 +529,10 @@
     head[0] = (links[step * frames] * value[:ROWS, 2 * CM :]).astype(BF)
 
 
-def block_taps(taps, out):
-    lane = lax.broadcasted_iota(jnp.int32, (CFM, 128), 1)
-    row = lax.broadcasted_iota(jnp.int32, (CFM, 128), 0)
-    four = sum(jnp.where(lane == row + q * CFM, 1.0, 0.0) for q in range(4))
-    wide = mul(taps[...], four.astype(BF))
-    for a in range(3):
-        for c in range(3):
-            tap = wide[(3 * a + c) * CFM : (3 * a + c + 1) * CFM]
-            for q in range(4):
-                mine = (lane >= q * CFM) & (lane < (q + 1) * CFM)
-                at = c * 128 + q * CFM
-                out[at : at + CFM, a * 128 : (a + 1) * 128] = jnp.where(mine, tap, 0.0).astype(BF)
-
-
 def k_short(
-    step, slow, lat_act, w_proj, fone, total, fgb, fast_taps, masks,
-    short, fact, ftwo, sums, fspace, *, steps, count
+    step, slow, lat_act, w_proj, fone, total, fgb, fspace, masks,
+    short, fact, ftwo, sums, *, steps, count
 ):
-    block_taps(fast_taps, fspace)
     value = mul(rows_of(slow), w_proj[:CS]) + mul(rows_of(lat_act), w_proj[CS:])
     put(short, value)
     add_rows(sums, step, steps, 0, value, value * value)
@@ -510,10 +566,12 @@
     step, slow_one, ftwo, total, gb, fgb, space, fproj, masks,
     cat_out, two_out, fact_out, fthree, sums, w_space, *, steps, count
 ):
-    for a in range(3):
-        for c in range(3):
-            tap = space[(3 * a + c) * CM : (3 * a + c + 1) * CM]
-            w_space[c * CM : (c + 1) * CM, a * CM : (a + 1) * CM] = tap
+    @pl.when(step == 0)
+    def _():
+        for a in range(3):
+            for c in range(3):
+                tap = space[(3 * a + c) * CM : (3 * a + c + 1) * CM]
+                w_space[c * CM : (c + 1) * CM, a * CM : (a + 1) * CM] = tap
 
     mean, scale = stats(total, CS + 128, CM, count)
     hat = (rows_of(slow_one) - mean) * scale
@@ -532,7 +590,16 @@
     add_rows(sums, step, steps, CM, value, value * value)
 
 
-def k_three(step, slow_two, total, gb, w_out, masks, act_out, sums, *, steps, count):
+def k_three(
+    step, slow_two, total, gb, rows_out, masks, act_out, sums, w_out, wide, *, steps, count
+):
+    @pl.when(step == 0)
+    def _():
+        for half in range(2):
+            wide[half] = rows_out[:, half * 128 : (half + 1) * 128].astype(F32)
+            for j in range(4):
+                at = j * CM + half * 128
+                w_out[:, at : at + 128] = wide[half, pl.ds(j, CM, stride=4), :].astype(BF)
     mean, scale = stats(total, 0, CM, count)
     hat = (rows_of(slow_two) - mean) * scale
     act = gelu(hat * gb[0:1, 2 * CL : 3 * CL] + gb[1:2, 2 * CL : 3 * CL])
@@ -555,11 +622,13 @@
     return value * half, slope
 
 
-def chunked(body, frames, lanes):
+def chunked(body, frames, lanes, first=lambda f: None):
     full = PIX // CHUNK
     last = full * CHUNK
 
     def frame(f, carry):
+        first(f)
+
         def step(i, carry):
             at = pl.ds(pl.multiple_of(i * CHUNK, CHUNK), CHUNK)
             for start in range(0, lanes, SPAN):
@@ -615,7 +684,9 @@
     step, act, w_out, short, cot, total, short_total, gb, given, out, grad_out, sums, three, acc,
     *, steps, count
 ):
-    three[...] = mul(rows_of(act), w_out[...]).reshape(three.shape)
+    def expand(f):
+        three[...] = mul(act[f], w_out[...])
+
     mean_a, scale_a = stats(total, 0, CS, count)
     mean_b, scale_b = stats(short_total, 0, CS, count)
     gain_a, gain_b = gb[0:1, 768:1792], gb[0:1, 1792:]
@@ -626,7 +697,7 @@
         acc[...] = jnp.zeros_like(acc)
 
     def body(f, rows, real, lanes):
-        hat_a = (three[f, rows, lanes] - mean_a[:, lanes]) * scale_a[:, lanes]
+        hat_a = (three[rows, lanes] - mean_a[:, lanes]) * scale_a[:, lanes]
         hat_b = (short[f, rows, lanes] - mean_b[:, lanes]) * scale_b[:, lanes]
         value = hat_a * gain_a[:, lanes] + (hat_b * gain_b[:, lanes] + bias[:, lanes])
         smooth, slope = gelu_both(value)
@@ -637,7 +708,7 @@
         acc[1, :, lanes] += halves(grad * hat_a)
         acc[2, :, lanes] += halves(grad * hat_b)
 
-    chunked(body, act.shape[0], CS)
+    chunked(body, act.shape[0], CS, expand)
 
     @pl.when(step % steps == steps - 1)
     def _():
@@ -649,10 +720,11 @@
 
 def k_back_three(
     step, act, w_out, short, grad, total, short_total, sums, gb, slow_two, total3,
-    fgrad, fthree, ftwo, fgb, fproj, masks,
-    d_three, d_short, grad_two, d_fthree, fgrad_two, sums_out, three, *, steps, count
+    d_three, d_short, grad_two, sums_out, three, *, steps, count
 ):
-    three[...] = mul(rows_of(act), w_out[...]).reshape(three.shape)
+    def expand(f):
+        three[...] = mul(act[f], w_out[...])
+
     mean_a, scale_a = stats(total, 0, CS, count)
     mean_b, scale_b = stats(short_total, 0, CS, count)
     one, two_a = back_parts(sums, 0, CS, count)
@@ -662,7 +734,7 @@
 
     def body(f, rows, real, lanes):
         given = grad[f, rows, lanes] - one[:, lanes]
-        hat_a = (three[f, rows, lanes] - mean_a[:, lanes]) * scale_a[:, lanes]
+        hat_a = (three[rows, lanes] - mean_a[:, lanes]) * scale_a[:, lanes]
         hat_b = (short[f, rows, lanes] - mean_b[:, lanes]) * scale_b[:, lanes]
         value_a = factor_a[:, lanes] * (given - hat_a * two_a[:, lanes])
         value_b = factor_b[:, lanes] * (given - hat_b * two_b[:, lanes])
@@ -673,7 +745,7 @@
         d_three[f, rows, lanes] = value_a.astype(BF)
         d_short[f, rows, lanes] = value_b.astype(BF)
 
-    chunked(body, act.shape[0], CS)
+    chunked(body, act.shape[0], CS, expand)
     mean, scale = stats(total3, 0, CM, count)
     hat = (rows_of(slow_two) - mean) * scale
     slope = gelu_slope(hat * gb[0:1, 2 * CL : 3 * CL] + gb[1:2, 2 * CL : 3 * CL])
@@ -681,19 +753,33 @@
     put(grad_two, value)
     add_rows(sums_out, step, steps, 0, value, value * hat)
 
+
+def k_back_fast_three(
+    step, given, sums, total3, fgrad, fthree, ftwo, fgb, fproj, total2,
+    d_fthree, fgrad_two, sums_out, *, steps, count
+):
+    @pl.when(step % steps == 0)
+    def _():
+        sums_out[0, :, :CM] = given[0]
+
     mean, scale = stats(total3, CM, 4 * CF, 4.0 * count, CF)
     one, two = back_parts(sums, CS, 4 * CF, 4.0 * count, CF)
-    hat = (rows_of(fthree) - mean) * scale
-    value = norm_back(rows_of(fgrad), hat, fgb[0:1, 256:] * scale, one, two)
-    lanes = value.shape[-1]
-    row = lax.broadcasted_iota(jnp.int32, (1, ROWS, lanes), 1)
-    value = jnp.where(row < PIX, value.reshape(-1, ROWS, lanes), 0.0)
-    value = value.reshape(-1, lanes).astype(BF)
-    put(d_fthree, value)
-    mean, scale = stats(short_total, CS, 128, 4.0 * count, CFM)
+    factor = fgb[0:1, 256:] * scale
+
+    def fast_body(f, rows, real, lanes):
+        hat = (fthree[f, rows, lanes] - mean[:, lanes]) * scale[:, lanes]
+        value = fgrad[f, rows, lanes] - one[:, lanes] - hat * two[:, lanes]
+        value = factor[:, lanes] * value
+        if real < CHUNK:
+            row = lax.broadcasted_iota(jnp.int32, value.shape, 0)
+            value = jnp.where(row < real, value, 0.0)
+        d_fthree[f, rows, lanes] = value.astype(BF)
+
+    chunked(fast_body, fthree.shape[0], 4 * CF)
+    mean, scale = stats(total2, CS, 128, 4.0 * count, CFM)
     hat = (rows_of(ftwo) - mean) * scale
     slope = gelu_slope(hat * fgb[0:1, 128:256] + fgb[1:2, 128:256])
-    value = slope * mul_t(value, fproj[...])
+    value = slope * mul_t(rows_of(d_fthree), fproj[...])
     put(fgrad_two, value)
     add_rows(sums_out, step, steps, CM, value, value * hat)
 
@@ -873,8 +959,9 @@
 
 
 def k_outer_first(
-    step, links, nexts, fast, edge_down, edge_up, d_lat, d_fone, out, fout, z, *, micro
+    step, links, nexts, fast, edge_down, edge_up, d_lat, d_fone, *rest, micro
 ):
+    z = rest[-1]
     z[...] = jnp.zeros_like(z)
     frames = z.shape[0] // micro
     for m in range(micro):
@@ -887,14 +974,26 @@
     taps = [0.0, 0.0, 0.0]
     fast = mul_rows(z, d_fone)
     lat = mul_rows(z, d_lat)
-    for tap, block in enumerate(blocks):
-        out[tap * CF : (tap + 1) * CF] = lat[block * CF : (block + 1) * CF].astype(BF)
+    lat = jnp.concatenate([lat[block * CF : (block + 1) * CF] for block in blocks], 0)
     for q in range(4):
         for k in range(3):
             block = [5, 0, 1, 2, 3, 6][q + k]
             taps[k] += lanes_at(fast[block * CF : (block + 1) * CF], q * CFM)
-    for k in range(3):
-        fout[k] = taps[k].astype(BF)
+    if len(rest) == 3:
+        out, fout, _ = rest
+        out[...] = lat.astype(BF)
+        for k in range(3):
+            fout[k] = taps[k].astype(BF)
+        return
+    fspace, fproj, out, _ = rest
+    devices = out.shape[0]
+    taps = jnp.concatenate(taps, 0)
+    at = 0
+    for value in (lat[:, :128], lat[:, 128:], taps, fspace[...].astype(F32), fproj[...].astype(F32)):
+        rows, lanes = value.shape[0] // devices, value.shape[1]
+        for d in range(devices):
+            out[d, at : at + rows, :lanes] = value[d * rows : (d + 1) * rows].astype(BF)
+        at += rows
 
 
 def k_params(step, sums_a, sums_b, sums_c, sums_d, out, fast):
@@ -959,38 +1058,38 @@
     share = slow_gain.shape[0]
     mine, spots, share_start = has_bits(me), slice_spots(me), me * share
 
+    wide = w_projection.reshape(-1, CS)
     shards = [
         w_slow_time, w_lateral, w_fast_time, w_fast_space, w_fast_out, slow_gain, slow_bias
     ]
-    packed = [as_rows(shard) for shard in shards]
-    places = np.cumsum([0] + [part.shape[0] for part in packed])
+    widths = (CM, CM, CFM, CFM, CF, share, share)
+    whole_rows = all(shard.shape[0] % width == 0 for shard, width in zip(shards, widths))
+    if whole_rows:
+        packed = [shard.reshape(-1, width) for shard, width in zip(shards, widths)]
+        packed = [jnp.pad(part, ((0, 0), (0, CM - part.shape[1]))) for part in packed]
+    else:
+        packed = [as_rows(shard) for shard in shards]
+    near_rows = [part.shape[0] for part in packed]
+    places = np.cumsum([0] + near_rows)
     packed = jnp.concatenate(packed, 0)
     near = Gather(mine, jnp.pad(packed, ((0, -packed.shape[0] % 8), (0, 0))))
-    projection = lax.all_gather(w_projection.reshape(-1, CS), AXES, axis=0, tiled=True)
-
-    slow = pad_rows(slow_in).reshape(groups, ROWS, CS)
-    cot = pad_rows(slow_cotangent).reshape(groups, ROWS, CS)
-    fast = fast_in.reshape(groups, 4, PIX, CF)
-    fcot = to_quads(fast_cotangent)
-
+
+    fast = tie([], fast_in.reshape(groups, 4, PIX, CF))
+    fast, fast_in, wide, slow_in, slow_cotangent, fast_cotangent = tie(
+        [near], fast, fast_in, wide, slow_in, slow_cotangent, fast_cotangent
+    )
+    wide = Gather(mine, wide)
     link = (1 - clip_starts).astype(F32)
     links = link.reshape(groups)
     nexts = jnp.concatenate([link[:, 1:], jnp.ones((micro, 1), F32)], 1).reshape(groups)
     edge_down = from_before(fast_in[:, -2:])
     edge_up = from_after(fast_in[:, :1] * link[:, :1, None, None].astype(BF))
-    slow = tie([near], slow)
-    fast, fcot = tie([near], fast, fcot)
+    slow = pad_rows(slow_in).reshape(groups, ROWS, CS)
+    cot = pad_rows(slow_cotangent).reshape(groups, ROWS, CS)
+    fcot = to_quads(fast_cotangent)
+    slow, fcot, edge_down, edge_up = tie([near, wide], slow, fcot, edge_down, edge_up)
     cot = tie([near], cot)
 
-    weights = near.result()
-    cuts = [
-        flat_of(weights, int(at), shard, lanes)
-        for at, shard, lanes in zip(places, shards, (CM, CL, CFM, CFM, CF, share, share))
-    ]
-    slow_time = cuts[0].reshape(3, CS + CL, CM)
-    slow_time = jnp.concatenate([slow_time[tap] for tap in range(3)], -1)
-    lateral, fast_time, fast_space, fast_proj = cuts[1:5]
-    gb = jnp.stack([cuts[5].reshape(-1), cuts[6].reshape(-1)]).astype(F32)
     fast_both = jnp.stack([fast_gain, fast_bias]).astype(F32)
     fgb = jnp.concatenate(
         [
@@ -1000,39 +1099,70 @@
         1,
     )
 
-    fast_time = fast_time.reshape(3, CF, CFM)
-    order = [5, 0, 1, 2, 3, 6]
-    band = np.zeros((3, 7, 4), np.float32)
-    for q in range(4):
-        for k in range(3):
-            band[k, order[q + k], q] = 1
-    band = jnp.asarray(band, BF)
-    fast_band = jnp.sum(
-        band[:, :, None, :, None] * fast_time[:, None, :, None, :], 0, dtype=F32
-    ).astype(BF).reshape(7 * CF, 4 * CFM)
-    none = jnp.zeros((CF, CL), BF)
-    lat_band = jnp.concatenate([lateral[2 * CF :], none, lateral[: 2 * CF], none], 0)
-    w_first = jnp.concatenate([lat_band, fast_band], -1)
-    eye4 = jnp.eye(4, dtype=BF)
-    fproj = (fast_proj[None, :, None, :] * eye4[:, None, :, None]).reshape(4 * CFM, 4 * CF)
-    lat_prev = jnp.concatenate([jnp.zeros((2 * CF, CL), BF), lateral[: 2 * CF]], 0)
-    blank = jnp.zeros((CF, 3 * CFM), BF)
-    rim_rows = jnp.concatenate(
-        [
-            jnp.concatenate([blank, fast_time[2]], -1),
-            jnp.zeros((2 * CF, 4 * CFM), BF),
-            jnp.concatenate([fast_time[0], blank], -1),
-        ],
-        0,
-    )
-    w_back = jnp.concatenate([w_first[: 4 * CF], lat_prev, rim_rows], -1)
-
-    links, nexts, w_first, spots, mine, share_start, *mids = tie(
-        [], links, nexts, w_first, spots, mine, share_start,
-        gb, fgb, fast_space, fproj, w_back, projection, slow_time,
-    )
-    gb, fgb, fast_space, fproj, w_back, projection, slow_time = mids
-    far = Gather(mine, jnp.concatenate([as_rows(w_slow_space), as_rows(w_slow_out)], 0))
+    if whole_rows:
+        slow_time, w_first, w_back, fproj, fspace, gb = call(
+            functools.partial(k_prep, shares=near_rows),
+            1,
+            [whole(near.result())],
+            [
+                out_whole((CS + CL, 3 * CM), BF), out_whole((7 * CF, CL + 128), BF),
+                out_whole((4 * CF, 768), BF), out_whole((128, 4 * CF), BF),
+                out_whole((384, 384), BF), out_whole((2, 2816), F32),
+            ],
+            scratch=[
+                pltpu.VMEM((3 * (CS + CL), CM), F32), pltpu.VMEM((5 * CF, CL), F32),
+                pltpu.VMEM((3 * CF + 9 * CFM + CFM, 128), F32),
+            ],
+            name="first_weights",
+            limit=16,
+        )
+    else:
+        weights = near.result()
+        cuts = [
+            flat_of(weights, int(at), shard, lanes)
+            for at, shard, lanes in zip(places, shards, (CM, CL, CFM, CFM, CF, share, share))
+        ]
+        slow_time = cuts[0].reshape(3, CS + CL, CM)
+        slow_time = jnp.concatenate([slow_time[tap] for tap in range(3)], -1)
+        lateral, fast_time, fast_space, fast_proj = cuts[1:5]
+        gb = jnp.stack([cuts[5].reshape(-1), cuts[6].reshape(-1)]).astype(F32)
+        fast_time = fast_time.reshape(3, CF, CFM)
+        order = [5, 0, 1, 2, 3, 6]
+        band = np.zeros((3, 7, 4), np.float32)
+        for q in range(4):
+            for k in range(3):
+                band[k, order[q + k], q] = 1
+        band = jnp.asarray(band, BF)
+        fast_band = jnp.sum(
+            band[:, :, None, :, None] * fast_time[:, None, :, None, :], 0, dtype=F32
+        ).astype(BF).reshape(7 * CF, 4 * CFM)
+        none = jnp.zeros((CF, CL), BF)
+        lat_band = jnp.concatenate([lateral[2 * CF :], none, lateral[: 2 * CF], none], 0)
+        w_first = jnp.concatenate([lat_band, fast_band], -1)
+        eye4 = jnp.eye(4, dtype=BF)
+        fproj = (fast_proj[None, :, None, :] * eye4[:, None, :, None]).reshape(4 * CFM, 4 * CF)
+        lat_prev = jnp.concatenate([jnp.zeros((2 * CF, CL), BF), lateral[: 2 * CF]], 0)
+        blank = jnp.zeros((CF, 3 * CFM), BF)
+        rim_rows = jnp.concatenate(
+            [
+                jnp.concatenate([blank, fast_time[2]], -1),
+                jnp.zeros((2 * CF, 4 * CFM), BF),
+                jnp.concatenate([fast_time[0], blank], -1),
+            ],
+            0,
+        )
+        fspace = fast_space.reshape(3, 3, CFM, CFM).transpose(1, 2, 0, 3)
+        fspace = fspace[:, None, :, :, None, :] * eye4[None, :, None, None, :, None]
+        fspace = fspace.reshape(3 * 4 * CFM, 3 * 4 * CFM)
+        w_back = jnp.concatenate([w_first[: 4 * CF], lat_prev, rim_rows], -1)
+
+    far = jnp.concatenate([as_rows(w_slow_space), as_rows(w_slow_out)], 0)
+    links, nexts, w_first, spots, mine, share_start, far, *mids = tie(
+        [], links, nexts, w_first, spots, mine, share_start, far,
+        gb, fgb, fspace, fproj, w_back,
+    )
+    gb, fgb, fspace, fproj, w_back = mids
+    fars = []
     space_rows = -(-w_slow_space.shape[0] // CM)
 
     rows = groups * ROWS
@@ -1049,6 +1179,12 @@
 
     def hooked(*stages):
         return lambda value, stage: tie(stages[stage], value) if stage < len(stages) else value
+
+    def first_hook(value, stage):
+        if stage == 1:
+            value = tie([wide], value)
+            fars.append(Gather(mine, far))
+        return value
 
     lat_pre, fone, sums = call(
         k_first,
@@ -1062,7 +1198,7 @@
         flops=2 * rows * 896 * 384,
         name="lateral_and_fast_time",
     )
-    total1 = all_sum(sums, hooked([far]))
+    total1 = all_sum(sums, first_hook)
 
     lat_act, taps, tail, head = call(
         bind(k_taps, count=count),
@@ -1076,18 +1212,19 @@
         name="slow_time_taps",
     )
     rim_before, rim_after = from_before(tail), from_after(head)
-    lat_act, taps = tie([far], lat_act, taps)
+    far = fars[0]
+    lat_act = tie([wide, far], lat_act)
+    projection = wide.result().reshape(CS + CL, CS)
     per = frames
-    state, fact_cat, sums, fspace = call(
+    state, fact_cat, sums = call(
         bind(k_short, steps=1, count=count),
         micro,
         [
             group(slow, per), group(lat_act, per), whole(projection), group(fone, per),
-            stream(total1, 1), whole(fgb), whole(fast_space), whole(masks),
+            stream(total1, 1), whole(fgb), whole(fspace), whole(masks),
         ],
         [
             ("short", per), og(384, BF, per), ("ftwo", per), os(per, 2, CS + 128),
-            out_whole((384, 384), BF),
         ],
         state={},
         flops=2 * rows * 1280 * 1024,
@@ -1104,11 +1241,10 @@
         state=state,
         name="slow_one",
     )
-    total2 = all_sum(sums, hooked([far]))
+    total2 = all_sum(sums, hooked([far], [far]))
     weights = far.result()
     space = flat_of(weights, 0, w_slow_space, CM)
-    slow_proj = flat_of(weights, space_rows, w_slow_out, CM).reshape(CM, 4, CM)
-    slow_proj = jnp.concatenate([slow_proj[:, part] for part in range(4)], -1)
+    rows_out = flat_of(weights, space_rows, w_slow_out, CM)
 
     state, cat_one, fact_two, sums, slow_space = call(
         bind(k_two, steps=1, count=count),
@@ -1127,15 +1263,16 @@
     )
     total3 = all_sum(sums)
 
-    state, act_two, sums = call(
+    state, act_two, sums, slow_proj = call(
         bind(k_three, steps=1, count=count),
         micro,
         [
-            ("two", per), stream(total3, 1), whole(gb), whole(slow_proj),
+            ("two", per), stream(total3, 1), whole(gb), whole(rows_out),
             whole(masks),
         ],
-        [og(CM, BF, per), os(per, 2, CS)],
+        [og(CM, BF, per), os(per, 2, CS), out_whole((CM, CS), BF)],
         state=state,
+        scratch=[pltpu.VMEM((2, 4 * CM, 128), F32)],
         flops=2 * rows * 256 * 1024,
         name="slow_three",
     )
@@ -1168,7 +1305,7 @@
             out_group((groups, PIX, CS), BF, per, False), ("grad", per), os(per, 3, CS + 4 * CF),
         ],
         state=state,
-        scratch=[pltpu.VMEM((per, ROWS, CS), F32), pltpu.VMEM((3, 8, CS), F32)],
+        scratch=[pltpu.VMEM((ROWS, CS), F32), pltpu.VMEM((3, 8, CS), F32)],
         flops=2 * rows * 256 * 1024,
         name="slow_out",
     )
@@ -1177,23 +1314,32 @@
     def pixels_first(value, whole_shape):
         return jnp.swapaxes(value.reshape(whole_shape), 1, 2)
 
-    state, d_three, d_short, d_fthree, sums = call(
+    state, d_three, d_short, sums = call(
         bind(k_back_three, steps=steps, count=count),
         groups // per,
         [
             group(act_two, per), whole(slow_proj), ("short", per), ("grad", per),
             stream(total4, steps), stream(total2, steps), stream(sums_a, steps), whole(gb),
-            ("two", per), stream(total3, steps), ("fgrad", per), ("fthree", per),
-            ("ftwo", per), whole(fgb), whole(fproj), whole(masks),
-        ],
-        [
-            og(CS, BF, per), og(CS, BF, per), ("grad_two", per), og(4 * CF, BF, per),
-            ("fgrad_two", per), os(per, 2, CM + 128),
-        ],
+            ("two", per), stream(total3, steps),
+        ],
+        [og(CS, BF, per), og(CS, BF, per), ("grad_two", per), os(per, 2, CM)],
         state=state,
-        scratch=[pltpu.VMEM((per, ROWS, CS), F32)],
+        scratch=[pltpu.VMEM((ROWS, CS), F32)],
         flops=4 * rows * 256 * 1024,
         name="back_three",
+    )
+    state, d_fthree, sums = call(
+        bind(k_back_fast_three, steps=steps, count=count),
+        groups // per,
+        [
+            stream(sums, steps), stream(sums_a, steps), stream(total3, steps),
+            ("fgrad", per), ("fthree", per), ("ftwo", per), whole(fgb), whole(fproj),
+            stream(total2, steps),
+        ],
+        [og(4 * CF, BF, per), ("fgrad_two", per), os(per, 2, CM + 128)],
+        state=state,
+        flops=2 * rows * 128 * 512,
+        name="back_fast_three",
     )
 
     def shares(value):
@@ -1300,15 +1446,24 @@
     def weights_of_one(value, stage):
         if stage == 0:
             time_grad = outer_joined(slow, lat_act, trio, 3, "slow_time_grad")
-            value, time_grad = tie([flows["a"]], value, time_grad)
+            value, time_grad, flows["trio"] = tie([], value, time_grad, trio)
             both = jnp.concatenate([shares(time_grad), shares(flows["space"])], 1)
             flows["b"] = Shares(spots, both)
             flows["time_rows"] = time_grad.shape[0] * time_grad.shape[1] // devices
         elif stage == 1:
-            value = tie([flows["b"]], value)
+            value, later = tie([flows["b"]], value, flows["trio"])
+            flows["slow_in_grad"] = call(
+                k_slow_grad,
+                micro,
+                [group(later, per), group(d_short, per), whole(slow_time), whole(projection)],
+                [out_group((groups, PIX, CS), BF, per, False)],
+                flops=2 * rows * 1792 * 1024,
+                name="slow_in_grad",
+            )[0]
         return value
 
     sums_d = all_sum(sums, weights_of_one)
+    slow_in_grad = pixels_first(flows["slow_in_grad"], slow_in.shape)
 
     state, d_lat, head = call(
         bind(k_back_lat, count=count),
@@ -1321,39 +1476,44 @@
         state=state,
         name="back_lat",
     )
+    d_lat, head = tie([flows["b"]], d_lat, head)
     lat_rim = from_after(head)
-    first_grad, ftime_grad = call(
+    packed = devices <= CFM
+    tops = [
+        scalar(links), scalar(nexts), whole(fast), whole(edge_down), whole(edge_up),
+        whole(d_lat), whole(d_fone),
+    ]
+    if packed:
+        ends = [flows["fspace"].reshape(-1, CFM), flows["fast_out"]]
+        sizes = [5 * CF, 5 * CF, 3 * CF, 9 * CFM, CFM]
+        sizes = [size // devices for size in sizes]
+        tops += [whole(part) for part in ends]
+        outs = [out_whole((devices, -(-sum(sizes) // 8) * 8, 128), BF)]
+    else:
+        outs = [out_whole((5 * CF, CL), BF), out_whole((3, CF, CFM), BF)]
+    first_grad = call(
         bind(k_outer_first, micro=micro),
         1,
-        [
-            scalar(links), scalar(nexts), whole(fast), whole(edge_down), whole(edge_up),
-            whole(d_lat), whole(d_fone),
-        ],
-        [out_whole((5 * CF, CL), BF), out_whole((3, CF, CFM), BF)],
+        tops,
+        outs,
         scratch=[pltpu.VMEM((groups, ROWS, 7 * CF), BF)],
         flops=2 * rows * 896 * 384,
         name="lateral_grad",
     )
-    flat = [
-        part.reshape(devices, -1)
-        for part in (first_grad, ftime_grad, flows["fspace"], flows["fast_out"])
-    ]
-    sizes = [part.shape[1] for part in flat]
-    flat = jnp.concatenate(flat, 1)
-    flat = jnp.pad(flat, ((0, 0), (0, -flat.shape[1] % 1024)))
-    flat = flat.reshape(devices, -1, 128)
-    trio, flat = tie([], trio, flat)
+    if packed:
+        flat = first_grad[0]
+    else:
+        flat = [
+            part.reshape(devices, -1)
+            for part in (*first_grad, flows["fspace"], flows["fast_out"])
+        ]
+        sizes = [part.shape[1] for part in flat]
+        flat = jnp.concatenate(flat, 1)
+        flat = jnp.pad(flat, ((0, 0), (0, -flat.shape[1] % 1024)))
+        flat = flat.reshape(devices, -1, 128)
     last = Shares(spots, flat)
-    per = frames
-    slow_in_grad = call(
-        k_slow_grad,
-        micro,
-        [group(trio, per), group(d_short, per), whole(slow_time), whole(projection)],
-        [out_group((groups, PIX, CS), BF, per, False)],
-        flops=2 * rows * 1792 * 1024,
-        name="slow_in_grad",
-    )[0]
-    lat_rim, slow_in_grad = tie([flows["b"], last], lat_rim, slow_in_grad)
+    fast_out = pixels_first(fast_out, fast_in.shape)
+    lat_rim, fast_out = tie([flows["a"], last], lat_rim, fast_out)
     state, fast_in_grad = call(
         k_fast_grad,
         micro,
@@ -1369,6 +1529,7 @@
         name="fast_in_grad",
     )
     fast_in_grad, slow_in_grad = tie([flows["b"], last], fast_in_grad, slow_in_grad)
+    fast_in_grad = pixels_first(fast_in_grad, fast_in.shape)
     both_out = flows["a"].result().reshape(-1, CS)
     cut = flows["proj_rows"]
     proj_out, out_out = both_out[:cut].reshape(-1), both_out[cut:].reshape(-1)
@@ -1378,9 +1539,18 @@
     flat = last.result()
     smalls = []
     at = 0
-    for size in sizes:
-        smalls.append(flat[at : at + size])
-        at += size
+    if packed:
+        flat = flat.reshape(-1, 128)
+        parts = []
+        for size, lanes in zip(sizes, (128, 128, CFM, CFM, CF)):
+            parts.append(flat[at : at + size, :lanes])
+            at += size
+        parts = [jnp.concatenate(parts[:2], 1)] + parts[2:]
+        smalls = [part.reshape(-1) for part in parts]
+    else:
+        for size in sizes:
+            smalls.append(flat[at : at + size])
+            at += size
 
     norms, fnorms = call(
         k_params,
@@ -1396,9 +1566,9 @@
     )
     return (
         jnp.swapaxes(slow_out, 1, 2),
-        fast_out.reshape(fast_in.shape),
-        slow_in_grad.reshape(slow_in.shape),
-        fast_in_grad.reshape(fast_in.shape),
+        jnp.swapaxes(fast_out, 1, 2),
+        jnp.swapaxes(slow_in_grad, 1, 2),
+        jnp.swapaxes(fast_in_grad, 1, 2),
         smalls[0],
         time_out,
         space_out,

time: 409 us -> 358 us (0.88)
  local copies, waits for them, and re-layouts: 83.1 us -> 44.3 us
  between operations: 16.3 us -> 2.67 us
  other arithmetic: 17.9 us -> 11.4 us
  starting transfers between devices: 130 us -> 135 us
    unnamed x207 -> x110, local copies, waits for them, and re-layouts: 47.5 us -> 20.2 us
    all_gather x1 -> x0, waiting for transfers between devices: 13.3 us -> none  [local(): lax.all_gather(w_projection.reshape(-1, CS), AXES, axis=0, tiled=True)]
    ppermute x91 -> x98, waiting for transfers between devices: 45.7 us -> 58.5 us  [swap(): return lax.ppermute(value, AXES, [(i, i ^ bit) for i in range(count)])]
    slice x14 -> x3, local copies, waits for them, and re-layouts: 6.29 us -> 0.01 us  [local(): parts.append(flat[at:at + size, :lanes])]
    ppermute x91 -> x98, starting transfers between devices: 114 us -> 120 us  [swap(): return lax.ppermute(value, AXES, [(i, i ^ bit) for i in range(count)])]
    reshape x1 -> x3, local copies, waits for them, and re-layouts: 4.16 us -> 9.69 us  [pixels_first(): return jnp.swapaxes(value.reshape(whole_shape), 1, 2)]
    pallas_call x21 -> x23, Pallas kernels: 84.4 us -> 86.4 us  [call(): pl.pallas_call(kernel, in_specs=[pl.BlockSpec(memory_space=pltpu.SMEM) if...]
  transfers between devices with their start and end apart: 99 -> 105, of which waited for: 37 -> 42; matrix products, arithmetic and copies ran while one was open for 15% -> 10% of each run, Pallas kernels for 14% -> 15%
where the time goes in v1:
time: 358 us; the launch traced here: 354 us
  starting transfers between devices  135 us (38%)
  Pallas kernels  86.4 us (24%)
  waiting for transfers between devices  73.6 us (21%)
  local copies, waits for them, and re-layouts  44.3 us (12%)
  other arithmetic  11.4 us (3%)
    ppermute x98, starting transfers between devices, swap(): return lax.ppermute(value, AXES, [(i, i ^ bit) for i in range(count)])  120 us
    pallas_call x23, Pallas kernels, call(): pl.pallas_call(kernel, in_specs=[pl.BlockSpec(memory_space=pltpu.SMEM) if...  86.4 us
    ppermute x98, waiting for transfers between devices, swap(): return lax.ppermute(value, AXES, [(i, i ^ bit) for i in range(count)])  58.5 us
    unnamed x110, local copies, waits for them, and re-layouts  20.2 us
    reshape x3, local copies, waits for them, and re-layouts, pixels_first(): return jnp.swapaxes(value.reshape(whole_shape), 1, 2)  9.69 us
    ppermute x3, starting transfers between devices, from_before(): return lax.ppermute(value, AXES, [(i, i + 1) for i in range(count - 1)])  9.45 us
    ppermute x4, waiting for transfers between devices, from_after(): return lax.ppermute(value, AXES, [(i + 1, i) for i in range(count - 1)])  9.31 us
  transfers between devices with their start and end apart: 105, of which 42 were waited for; matrix products, arithmetic and copies ran while one was open for 10% of the time, Pallas kernels for 15%

profile of v1, /device:TPU:0, one launch (start us, length us, event | category | flops | bytes accessed | tf_op | source)
XLA Modules:
  0.0 353.5 jit_solution(11645866246222336881)
XLA Ops:
  5.9 5.1 %collective-permute-start.2 = (bf16[1,168,256]{2,1,0:T(8,128)(2,1)S(1)}, bf16[1,168,256]{2,1,0:T(8,128)(2,1)S(1)}, u32[]{:S(2)}, u32[]{:S(2)}) collective-permute-start(bf16[1,168,256]{2,1,0:T(8,128)(2,1)S(1)} %pad_bitcast_fusion), channel_id=1, source_target_pairs={{0,12},{1,13},{2,14},{3,15},{4,8},{5,9},{6,10},{7,11},{8,4},{9,5},... | collective-permute-start | bytes 258056 | tf_op jit(solution)/shard_map/ppermute | solution.py:29
  13.3 3.1 copy.65
  28.8 3.4 collective-permute-start.3
  37.4 8.9 %collective-permute-done.4.refs_4_ = bf16[2,1,196,128]{3,2,1,0:T(8,128)(2,1)S(1)} collective-permute-done((bf16[2,1,196,128]{3,2,1,0:T(8,128)(2,1)S(1)}, bf16[2,1,196,128]{3,2,1,0:T(8,128)(2,1)S(1)}, u32[]{:S(2)}, u32[]{:S(2)}) %collective-permute-start.4) | collective-permute-done | bytes 100384 | tf_op jit(solution)/shard_map/ppermute | solution.py:174
  48.5 2.9 copy.113
  60.6 2.8 lateral_and_fast_time.1
  67.6 4.2 %collective-permute-done.15 = f32[2,2,384]{2,1,0:T(2,128)S(1)} collective-permute-done((f32[2,2,384]{2,1,0:T(2,128)S(1)}, f32[2,2,384]{2,1,0:T(2,128)S(1)}, u32[]{:S(2)}, u32[]{:S(2)}) %collective-permute-start.15) | collective-permute-done | bytes 6176 | tf_op jit(solution)/shard_map/ppermute | solution.py:29
  84.8 4.6 %slow_time_taps.1 = (bf16[8,208,256]{2,1,0:T(8,128)(2,1)S(1)}, f32[8,208,768]{2,1,0:T(8,128)S(1)}, bf16[2,208,256]{2,1,0:T(8,128)(2,1)S(1)}, bf16[2,208,256]{2,1,0:T(8,128)(2,1)S(1)}) custom-call(f32[8]{0:T(128)S(1)} %reshape.404.refs_0_, f32[8,208,256]{2,1,0:T(8,128)S(1)} %get-tuple-element.200.refs_1_.refs_8_, ...), custom_call_target="tpu_custom_call" | custom-call | flops 3271557120 | bytes 14561312 | tf_op jit(solution)/shard_map/slow_time_taps/pallas_call | solution.py:262
  89.5 3.3 collective-permute-start.22
  99.4 6.1 %shortcut_and_fast_space.1 = (f32[8,208,1024]{2,1,0:T(8,128)S(1)}, bf16[8,208,384]{2,1,0:T(8,128)(2,1)S(1)}, f32[8,208,128]{2,1,0:T(8,128)S(1)}, f32[2,2,1152]{2,1,0:T(2,128)S(1)}) custom-call(bf16[8,208,1024]{2,1,0:T(8,128)(2,1)S(1)} %bitcast.404, bf16[8,208,256]{2,1,0:T(8,128)(2,1)S(1)} %get-tuple-element.217.refs_1_, bf16[1280,1024]{1,0:T(8,128)(2,1)S(1)} %bitcast.392, ...), custom_call_target="tpu_custom_call" | custom-call | flops 4362076160 | bytes 18069504 | tf_op jit(solution)/shard_map/shortcut_and_fast_space/pallas_call | solution.py:262
  124.7 4.0 %slow_space.1 = (bf16[8,208,768]{2,1,0:T(8,128)(2,1)S(1)}, f32[8,208,256]{2,1,0:T(8,128)S(1)}, bf16[8,208,128]{2,1,0:T(8,128)(2,1)S(1)}, f32[8,208,512]{2,1,0:T(...) custom-call(f32[8,208,256]{2,1,0:T(8,128)S(1)} %get-tuple-element.223.refs_0_.refs_6_.refs_1_, ...), custom_call_target="tpu_custom_call" | custom-call | flops 1962934272 | bytes 14268416 | tf_op jit(solution)/shard_map/slow_space/pallas_call | solution.py:262
  131.4 2.9 collective-permute-start.42
  158.7 4.1 %fast_out.1 = (bf16[8,4,196,128]{3,2,1,0:T(8,128)(2,1)S(1)}, f32[8,208,512]{2,1,0:T(8,128)S(1)}, f32[2,2,512]{2,1,0:T(2,128)S(1)}) custom-call(f32[8,208,512]{2,1,0:T(8,128)S(1)} %get-tuple-element.248.refs_0_.refs_4_, bf16[8,4,196,128]{3,2,1,0:T(8,128)(2,1)S(1)} %bitcast.398, bf16[8,208,512]{2,1,0:T(8,128)(2,1)S(1)} %pad_maximum_fusion.2.refs_2_, ...), custom_call_target="tpu_custom_call" | custom-call | flops 170393600 | bytes 11757568 | tf_op jit(solution)/shard_map/fast_out/pallas_call | solution.py:262
  164.0 11.0 %slow_out.1 = (bf16[8,196,1024]{2,1,0:T(8,128)(2,1)S(1)}, f32[8,208,1024]{2,1,0:T(8,128)S(1)}, f32[2,3,1536]{2,1,0:T(4,128)S(1)}) custom-call(bf16[8,208,256]{2,1,0:T(8,128)(2,1)S(1)} %get-tuple-element.243.refs_0_, bf16[256,1024]{1,0:T(8,128)(2,1)S(1)} %get-tuple-element.244.refs_1_, f32[8,208,1024]{2,1,0:T(8,128)S(1)} %get-tuple-element.245.refs_2_, ...), custom_call_target="tpu_custom_call" | custom-call | flops 872415232 | bytes 21733376 | tf_op jit(solution)/shard_map/slow_out/pallas_call | solution.py:262
  192.0 9.1 %back_three.1 = (bf16[8,208,1024]{2,1,0:T(8,128)(2,1)S(1)}, bf16[8,208,1024]{2,1,0:T(8,128)(2,1)S(1)}, f32[8,208,256]{2,1,0:T(8,128)S(1)}, f32[2,2,256]{2,1,0:T(2,128)S(1)}) custom-call(bf16[8,208,256]{2,1,0:T(8,128)(2,1)S(1)} %get-tuple-element.243.refs_0_, bf16[256,1024]{1,0:T(8,128)(2,1)S(1)} %get-tuple-element.244.refs_1_, ...), custom_call_target="tpu_custom_call" | custom-call | flops 1744830464 | bytes 25346048 | tf_op jit(solution)/shard_map/back_three/pallas_call | solution.py:262
  201.1 3.1 back_fast_three.1
  204.5 5.0 %projection_grad.1 = bf16[1280,1024]{1,0:T(8,128)(2,1)S(1)} custom-call(bf16[8,208,1024]{2,1,0:T(8,128)(2,1)S(1)} %bitcast.405, bf16[8,208,256]{2,1,0:T(8,128)(2,1)S(1)} %copy-done.26, bf16[8,208,1024]{2,1,0:T(8,128)(2,1)S(1)} %get-tuple-element.257.refs_2_.refs_5_.refs_1_), custom_call_target="tpu_custom_call" | custom-call | flops 4362076160 | bytes 10289152 | tf_op jit(solution)/shard_map/projection_grad/pallas_call | solution.py:262
  226.6 5.9 %back_two.1 = (bf16[8,208,768]{2,1,0:T(8,128)(2,1)S(1)}, f32[8,208,256]{2,1,0:T(8,128)S(1)}, bf16[8,208,384]{2,1,0:T(8,128)(2,1)S(1)}, f32[8,208,128]{2,1,0:T(8,128)S(1)}, f32[2,2,384]{2,1,0:T(2,128)S(1)}) custom-call(f32[8,208,256]{2,1,0:T(8,128)S(1)} %get-tuple-element.241.refs_0_.refs_8_, f32[2,2,768]{2,1,0:T(2,128)S(1)} %add_add_fusion.9.refs_1_.refs_3_.refs_9_.refs_2_, ...), custom_call_target="tpu_custom_call" | custom-call | flops 1962934272 | bytes 16678912 | tf_op jit(solution)/shard_map/back_two/pallas_call | solution.py:262
  232.6 3.2 slow_space_grad.1
  238.3 2.9 collective-permute-done.71
  254.0 2.7 collective-permute-start.78
  258.1 4.2 %copy.126 = bf16[2,4,196,1024]{3,1,2,0:T(4,128)(2,1)} copy(bf16[2,4,196,1024]{3,2,1,0:T(8,128)(2,1)S(1)} %bitcast.407) | data formatting | bytes 6422528 | tf_op jit(solution)/shard_map/reshape | solution.py:1315
  262.3 5.8 %collective-permute-done.78.refs_3_.refs_6_ = bf16[2,208,384]{2,1,0:T(8,128)(2,1)S(1)} collective-permute-done((bf16[2,208,384]{2,1,0:T(8,128)(2,1)S(1)}, bf16[2,208,384]{2,1,0:T(8,128)(2,1)S(1)}, u32[]{:S(2)}, u32[]{:S(2)}) %collective-permute-start.78) | collective-permute-done | bytes 319520 | tf_op jit(solution)/shard_map/ppermute | solution.py:169
  268.5 3.6 %back_lateral.1 = (bf16[8,208,768]{2,1,0:T(8,128)(2,1)S(1)}, f32[8,208,256]{2,1,0:T(8,128)S(1)}, f32[2,2,256]{2,1,0:T(2,128)S(1)}) custom-call(f32[8]{0:T(128)S(1)} %reshape.404.refs_0_, f32[8]{0:T(128)S(1)} %reshape.405.refs_1_, bf16[8,208,256]{2,1,0:T(8,128)(2,1)S(1)} %get-tuple-element.288.refs_2_, ...), custom_call_target="tpu_custom_call" | custom-call | flops 1526726656 | bytes 15482944 | tf_op jit(solution)/shard_map/back_lateral/pallas_call | solution.py:262
  272.2 3.9 %slow_time_grad.1 = bf16[3,1280,256]{2,1,0:T(8,128)(2,1)S(1)} custom-call(bf16[8,208,1024]{2,1,0:T(8,128)(2,1)S(1)} %bitcast.406, bf16[8,208,256]{2,1,0:T(8,128)(2,1)S(1)} %copy-done.27, bf16[8,208,768]{2,1,0:T(8,128)(2,1)S(1)} %get-tuple-element.318.refs_2_.refs_0_), custom_call_target="tpu_custom_call" | custom-call | flops 3271557120 | bytes 8781824 | tf_op jit(solution)/shard_map/slow_time_grad/pallas_call | solution.py:262
  292.0 6.6 %slow_in_grad.1 = bf16[8,196,1024]{2,1,0:T(8,128)(2,1)S(1)} custom-call(bf16[8,208,768]{2,1,0:T(8,128)(2,1)S(1)} %get-tuple-element.318.refs_2_.refs_0_, bf16[8,208,1024]{2,1,0:T(8,128)(2,1)S(1)} %copy-done.8, bf16[1280,768]{1,0:T(8,128)(2,1)S(1)} %copy-done.14, bf16[1280,1024]{1,0:T(8,128)(2,1)S(1)} %bitcast.394), custom_call_target="tpu_custom_call" | custom-call | flops 6106906624 | bytes 13762560 | tf_op jit(solution)/shard_map/slow_in_grad/pallas_call | solution.py:262
  299.1 4.2 %copy.125 = bf16[2,4,196,1024]{3,1,2,0:T(4,128)(2,1)} copy(bf16[2,4,196,1024]{3,2,1,0:T(8,128)(2,1)S(1)} %bitcast.408) | data formatting | bytes 6422528 | tf_op jit(solution)/shard_map/reshape | solution.py:1315
  309.3 7.0 %collective-permute-done.90 = bf16[4,192,256]{2,1,0:T(8,128)(2,1)S(1)} collective-permute-done((bf16[4,192,256]{2,1,0:T(8,128)(2,1)S(1)}, bf16[4,192,256]{2,1,0:T(8,128)(2,1)S(1)}, u32[]{:S(2)}, u32[]{:S(2)}) %collective-permute-start.90) | collective-permute-done | bytes 393248 | tf_op jit(solution)/shard_map/ppermute | solution.py:29
  316.6 5.0 %collective-permute-done.88 = bf16[4,192,256]{2,1,0:T(8,128)(2,1)S(1)} collective-permute-done((bf16[4,192,256]{2,1,0:T(8,128)(2,1)S(1)}, bf16[4,192,256]{2,1,0:T(8,128)(2,1)S(1)}, u32[]{:S(2)}, u32[]{:S(2)}) %collective-permute-start.88) | collective-permute-done | bytes 393248 | tf_op jit(solution)/shard_map/ppermute | solution.py:29
  323.2 2.8 lateral_grad.1
  326.0 3.5 %collective-permute-start.95 = (bf16[16,64,128]{2,1,0:T(8,128)(2,1)S(1)}, bf16[16,64,128]{2,1,0:T(8,128)(2,1)S(1)}, u32[]{:S(2)}, u32[]{:S(2)}) collective-permute-start(bf16[16,64,128]{2,1,0:T(8,128)(2,1)S(1)} %dynamic-slice_bitcast_fusion), channel_id=1, source_target_pairs={{0,16},{1,17},{2,18},{3,19},{4,20},{5,21},{6,22},{7,23},{8,24},{9,... | collective-permute-start | bytes 786440 | tf_op jit(solution)/shard_map/ppermute | solution.py:29
  331.5 2.8 collective-permute-start.96
  (432 shorter events, 203.0 us)
Async XLA Ops:
  20.9 14.7 %collective-permute-start.8 = (bf16[1,40,1024]{2,1,0:T(8,128)(2,1)S(1)}, bf16[1,40,1024]{2,1,0:T(8,128)(2,1)S(1)}, u32[]{:S(2)}, u32[]{:S(2)}) collective-permute-start(bf16[1,40,1024]{2,1,0:T(8,128)(2,1)S(1)} %bitcast.430), channel_id=1, source_target_pairs={{0,4},{1,5},{2,6},{3,7},{4,0},{5,1},{6,2},{7,3},{8,12},{9,13},{10,... | collective-permute-start | bytes 245768 | tf_op jit(solution)/shard_map/ppermute | solution.py:29
  22.8 23.5 %collective-permute-start.7 = (bf16[4,168,256]{2,1,0:T(8,128)(2,1)S(1)}, bf16[4,168,256]{2,1,0:T(8,128)(2,1)S(1)}, u32[]{:S(2)}, u32[]{:S(2)}) collective-permute-start(bf16[4,168,256]{2,1,0:T(8,128)(2,1)S(1)} %maximum_bitcast_fusion), channel_id=1, source_target_pairs={{0,3},{1,2},{2,1},{3,0},{4,7},{5,6},{6,5},{7,4},{8,11},{9,10},{10,... | collective-permute-start | bytes 1032200 | tf_op jit(solution)/shard_map/ppermute | solution.py:29
  25.3 21.0 %collective-permute-start.6 = (bf16[4,168,256]{2,1,0:T(8,128)(2,1)S(1)}, bf16[4,168,256]{2,1,0:T(8,128)(2,1)S(1)}, u32[]{:S(2)}, u32[]{:S(2)}) collective-permute-start(bf16[4,168,256]{2,1,0:T(8,128)(2,1)S(1)} %maximum_bitcast_fusion), channel_id=1, source_target_pairs={{0,2},{1,3},{2,0},{3,1},{4,6},{5,7},{6,4},{7,5},{8,10},{9,11},{10,... | collective-permute-start | bytes 1032200 | tf_op jit(solution)/shard_map/ppermute | solution.py:29
  28.2 18.0 %collective-permute-start.5 = (bf16[4,168,256]{2,1,0:T(8,128)(2,1)S(1)}, bf16[4,168,256]{2,1,0:T(8,128)(2,1)S(1)}, u32[]{:S(2)}, u32[]{:S(2)}) collective-permute-start(bf16[4,168,256]{2,1,0:T(8,128)(2,1)S(1)} %maximum_bitcast_fusion), channel_id=1, source_target_pairs={{0,1},{1,0},{2,3},{3,2},{4,5},{5,4},{6,7},{7,6},{8,9},{9,8},{10,11... | collective-permute-start | bytes 1032200 | tf_op jit(solution)/shard_map/ppermute | solution.py:29
  28.8 17.4 %collective-permute-start.3 = (bf16[2,2,196,128]{3,2,1,0:T(8,128)(2,1)S(1)}, bf16[2,2,196,128]{3,2,1,0:T(8,128)(2,1)S(1)}, u32[]{:S(2)}, u32[]{:S(2)}) collective-permute-start(bf16[2,2,196,128]{3,2,1,0:T(8,128)(2,1)S(1)} %slice.138), channel_id=1, source_target_pairs={{0,1},{1,2},{2,3},{3,4},{4,5},{5,6},{6,7},{7,8},{8,9},{9,10},{10,1... | collective-permute-start | bytes 602120 | tf_op jit(solution)/shard_map/ppermute | solution.py:169
  53.4 22.0 %collective-permute-start.18 = (bf16[4,40,1024]{2,1,0:T(8,128)(2,1)S(1)}, bf16[4,40,1024]{2,1,0:T(8,128)(2,1)S(1)}, u32[]{:S(2)}, u32[]{:S(2)}) collective-permute-start(bf16[4,40,1024]{2,1,0:T(8,128)(2,1)S(1)} %maximum_bitcast_fusion.1), channel_id=1, source_target_pairs={{0,3},{1,2},{2,1},{3,0},{4,7},{5,6},{6,5},{7,4},{8,11},{9,10},{10,... | collective-permute-start | bytes 983048 | tf_op jit(solution)/shard_map/ppermute | solution.py:29
  53.8 21.6 %collective-permute-start.17 = (bf16[4,40,1024]{2,1,0:T(8,128)(2,1)S(1)}, bf16[4,40,1024]{2,1,0:T(8,128)(2,1)S(1)}, u32[]{:S(2)}, u32[]{:S(2)}) collective-permute-start(bf16[4,40,1024]{2,1,0:T(8,128)(2,1)S(1)} %maximum_bitcast_fusion.1), channel_id=1, source_target_pairs={{0,2},{1,3},{2,0},{3,1},{4,6},{5,7},{6,4},{7,5},{8,10},{9,11},{10,... | collective-permute-start | bytes 983048 | tf_op jit(solution)/shard_map/ppermute | solution.py:29
  56.4 19.0 %collective-permute-start.16 = (bf16[4,40,1024]{2,1,0:T(8,128)(2,1)S(1)}, bf16[4,40,1024]{2,1,0:T(8,128)(2,1)S(1)}, u32[]{:S(2)}, u32[]{:S(2)}) collective-permute-start(bf16[4,40,1024]{2,1,0:T(8,128)(2,1)S(1)} %maximum_bitcast_fusion.1), channel_id=1, source_target_pairs={{0,1},{1,0},{2,3},{3,2},{4,5},{5,4},{6,7},{7,6},{8,9},{9,8},{10,11... | collective-permute-start | bytes 983048 | tf_op jit(solution)/shard_map/ppermute | solution.py:29
  75.9 18.7 %collective-permute-start.24 = (bf16[16,40,1024]{2,1,0:T(8,128)(2,1)S(1)}, bf16[16,40,1024]{2,1,0:T(8,128)(2,1)S(1)}, u32[]{:S(2)}, u32[]{:S(2)}) collective-permute-start(bf16[16,40,1024]{2,1,0:T(8,128)(2,1)S(1)} %bitcast.424), channel_id=1, source_target_pairs={{0,16},{1,17},{2,18},{3,19},{4,20},{5,21},{6,22},{7,23},{8,24},{9,... | collective-permute-start | bytes 3932168 | tf_op jit(solution)/shard_map/ppermute | solution.py:29
  80.4 12.4 %collective-permute-start.27 = (bf16[1,104,256]{2,1,0:T(8,128)(2,1)S(1)}, bf16[1,104,256]{2,1,0:T(8,128)(2,1)S(1)}, u32[]{:S(2)}, u32[]{:S(2)}) collective-permute-start(bf16[1,104,256]{2,1,0:T(8,128)(2,1)S(1)} %bitcast.431), channel_id=1, source_target_pairs={{0,12},{1,13},{2,14},{3,15},{4,8},{5,9},{6,10},{7,11},{8,4},{9,5},... | collective-permute-start | bytes 159752 | tf_op jit(solution)/shard_map/ppermute | solution.py:29
  82.6 12.0 %collective-permute-start.26 = (bf16[1,104,256]{2,1,0:T(8,128)(2,1)S(1)}, bf16[1,104,256]{2,1,0:T(8,128)(2,1)S(1)}, u32[]{:S(2)}, u32[]{:S(2)}) collective-permute-start(bf16[1,104,256]{2,1,0:T(8,128)(2,1)S(1)} %bitcast.432), channel_id=1, source_target_pairs={{0,8},{1,9},{2,10},{3,11},{4,12},{5,13},{6,14},{7,15},{8,0},{9,1},... | collective-permute-start | bytes 159752 | tf_op jit(solution)/shard_map/ppermute | solution.py:29
  82.8 11.8 %collective-permute-start.25 = (bf16[1,104,256]{2,1,0:T(8,128)(2,1)S(1)}, bf16[1,104,256]{2,1,0:T(8,128)(2,1)S(1)}, u32[]{:S(2)}, u32[]{:S(2)}) collective-permute-start(bf16[1,104,256]{2,1,0:T(8,128)(2,1)S(1)} %bitcast.433), channel_id=1, source_target_pairs={{0,4},{1,5},{2,6},{3,7},{4,0},{5,1},{6,2},{7,3},{8,12},{9,13},{10,... | collective-permute-start | bytes 159752 | tf_op jit(solution)/shard_map/ppermute | solution.py:29
  89.5 17.1 %collective-permute-start.22 = (bf16[2,208,256]{2,1,0:T(8,128)(2,1)S(1)}, bf16[2,208,256]{2,1,0:T(8,128)(2,1)S(1)}, u32[]{:S(2)}, u32[]{:S(2)}) collective-permute-start(bf16[2,208,256]{2,1,0:T(8,128)(2,1)S(1)} %get-tuple-element.210), channel_id=1, source_target_pairs={{0,1},{1,2},{2,3},{3,4},{4,5},{5,6},{6,7},{7,8},{8,9},{9,10},{10,1... | collective-permute-start | bytes 638984 | tf_op jit(solution)/shard_map/ppermute | solution.py:169
  92.8 13.8 %collective-permute-start.23 = (bf16[2,208,256]{2,1,0:T(8,128)(2,1)S(1)}, bf16[2,208,256]{2,1,0:T(8,128)(2,1)S(1)}, u32[]{:S(2)}, u32[]{:S(2)}) collective-permute-start(bf16[2,208,256]{2,1,0:T(8,128)(2,1)S(1)} %get-tuple-element.211), channel_id=1, source_target_pairs={{1,0},{2,1},{3,2},{4,3},{5,4},{6,5},{7,6},{8,7},{9,8},{10,9},{11,1... | collective-permute-start | bytes 638984 | tf_op jit(solution)/shard_map/ppermute | solution.py:174
  94.7 15.7 %collective-permute-start.31 = (bf16[4,104,256]{2,1,0:T(8,128)(2,1)S(1)}, bf16[4,104,256]{2,1,0:T(8,128)(2,1)S(1)}, u32[]{:S(2)}, u32[]{:S(2)}) collective-permute-start(bf16[4,104,256]{2,1,0:T(8,128)(2,1)S(1)} %maximum_bitcast_fusion.2), channel_id=1, source_target_pairs={{0,3},{1,2},{2,1},{3,0},{4,7},{5,6},{6,5},{7,4},{8,11},{9,10},{10,... | collective-permute-start | bytes 638984 | tf_op jit(solution)/shard_map/ppermute | solution.py:29
  96.4 14.0 %collective-permute-start.30 = (bf16[4,104,256]{2,1,0:T(8,128)(2,1)S(1)}, bf16[4,104,256]{2,1,0:T(8,128)(2,1)S(1)}, u32[]{:S(2)}, u32[]{:S(2)}) collective-permute-start(bf16[4,104,256]{2,1,0:T(8,128)(2,1)S(1)} %maximum_bitcast_fusion.2), channel_id=1, source_target_pairs={{0,2},{1,3},{2,0},{3,1},{4,6},{5,7},{6,4},{7,5},{8,10},{9,11},{10,... | collective-permute-start | bytes 638984 | tf_op jit(solution)/shard_map/ppermute | solution.py:29
  98.9 12.0 %collective-permute-start.29 = (bf16[4,104,256]{2,1,0:T(8,128)(2,1)S(1)}, bf16[4,104,256]{2,1,0:T(8,128)(2,1)S(1)}, u32[]{:S(2)}, u32[]{:S(2)}) collective-permute-start(bf16[4,104,256]{2,1,0:T(8,128)(2,1)S(1)} %maximum_bitcast_fusion.2), channel_id=1, source_target_pairs={{0,1},{1,0},{2,3},{3,2},{4,5},{5,4},{6,7},{7,6},{8,9},{9,8},{10,11... | collective-permute-start | bytes 638984 | tf_op jit(solution)/shard_map/ppermute | solution.py:29
  222.9 21.9 %collective-permute-start.74 = (bf16[4,48,1024]{2,1,0:T(8,128)(2,1)S(1)}, bf16[4,48,1024]{2,1,0:T(8,128)(2,1)S(1)}, u32[]{:S(2)}, u32[]{:S(2)}) collective-permute-start(bf16[4,48,1024]{2,1,0:T(8,128)(2,1)S(1)} %get-tuple-element.373), channel_id=1, source_target_pairs={{0,3},{1,2},{2,1},{3,0},{4,7},{5,6},{6,5},{7,4},{8,11},{9,10},{10,... | collective-permute-start | bytes 1179656 | tf_op jit(solution)/shard_map/ppermute | solution.py:29
  225.3 19.6 %collective-permute-start.72 = (bf16[4,48,1024]{2,1,0:T(8,128)(2,1)S(1)}, bf16[4,48,1024]{2,1,0:T(8,128)(2,1)S(1)}, u32[]{:S(2)}, u32[]{:S(2)}) collective-permute-start(bf16[4,48,1024]{2,1,0:T(8,128)(2,1)S(1)} %get-tuple-element.374), channel_id=1, source_target_pairs={{0,1},{1,0},{2,3},{3,2},{4,5},{5,4},{6,7},{7,6},{8,9},{9,8},{10,11... | collective-permute-start | bytes 1179656 | tf_op jit(solution)/shard_map/ppermute | solution.py:29
  225.5 19.4 %collective-permute-start.73 = (bf16[4,48,1024]{2,1,0:T(8,128)(2,1)S(1)}, bf16[4,48,1024]{2,1,0:T(8,128)(2,1)S(1)}, u32[]{:S(2)}, u32[]{:S(2)}) collective-permute-start(bf16[4,48,1024]{2,1,0:T(8,128)(2,1)S(1)} %get-tuple-element.375), channel_id=1, source_target_pairs={{0,2},{1,3},{2,0},{3,1},{4,6},{5,7},{6,4},{7,5},{8,10},{9,11},{10,... | collective-permute-start | bytes 1179656 | tf_op jit(solution)/shard_map/ppermute | solution.py:29
  254.0 14.1 %collective-permute-start.78 = (bf16[2,208,384]{2,1,0:T(8,128)(2,1)S(1)}, bf16[2,208,384]{2,1,0:T(8,128)(2,1)S(1)}, u32[]{:S(2)}, u32[]{:S(2)}) collective-permute-start(bf16[2,208,384]{2,1,0:T(8,128)(2,1)S(1)} %get-tuple-element.284), channel_id=1, source_target_pairs={{0,1},{1,2},{2,3},{3,4},{4,5},{5,6},{6,7},{7,8},{8,9},{9,10},{10,1... | collective-permute-start | bytes 958472 | tf_op jit(solution)/shard_map/ppermute | solution.py:169
  256.8 11.7 %collective-permute-start.79 = (bf16[2,208,384]{2,1,0:T(8,128)(2,1)S(1)}, bf16[2,208,384]{2,1,0:T(8,128)(2,1)S(1)}, u32[]{:S(2)}, u32[]{:S(2)}) collective-permute-start(bf16[2,208,384]{2,1,0:T(8,128)(2,1)S(1)} %get-tuple-element.285), channel_id=1, source_target_pairs={{1,0},{2,1},{3,2},{4,3},{5,4},{6,5},{7,6},{8,7},{9,8},{10,9},{11,1... | collective-permute-start | bytes 958472 | tf_op jit(solution)/shard_map/ppermute | solution.py:174
  283.9 45.9 %collective-permute-start.94 = (bf16[1,48,1024]{2,1,0:T(8,128)(2,1)S(1)}, bf16[1,48,1024]{2,1,0:T(8,128)(2,1)S(1)}, u32[]{:S(2)}, u32[]{:S(2)}) collective-permute-start(bf16[1,48,1024]{2,1,0:T(8,128)(2,1)S(1)} %get-tuple-element.398), channel_id=1, source_target_pairs={{0,12},{1,13},{2,14},{3,15},{4,8},{5,9},{6,10},{7,11},{8,4},{9,5},... | collective-permute-start | bytes 294920 | tf_op jit(solution)/shard_map/ppermute | solution.py:29
  285.8 44.6 %collective-permute-start.93 = (bf16[1,48,1024]{2,1,0:T(8,128)(2,1)S(1)}, bf16[1,48,1024]{2,1,0:T(8,128)(2,1)S(1)}, u32[]{:S(2)}, u32[]{:S(2)}) collective-permute-start(bf16[1,48,1024]{2,1,0:T(8,128)(2,1)S(1)} %get-tuple-element.399), channel_id=1, source_target_pairs={{0,8},{1,9},{2,10},{3,11},{4,12},{5,13},{6,14},{7,15},{8,0},{9,1},... | collective-permute-start | bytes 294920 | tf_op jit(solution)/shard_map/ppermute | solution.py:29
  287.5 15.8 %collective-permute-start.87 = (f32[2,2,256]{2,1,0:T(2,128)S(1)}, f32[2,2,256]{2,1,0:T(2,128)S(1)}, u32[]{:S(2)}, u32[]{:S(2)}) collective-permute-start(f32[2,2,256]{2,1,0:T(2,128)S(1)} %add_add_fusion.18), channel_id=1, source_target_pairs={{0,12},{1,13},{2,14},{3,15},{4,8},{5,9},{6,10},{7,11},{8,4},{9,5},... | collective-permute-start | bytes 12296 | tf_op jit(solution)/shard_map/ppermute | solution.py:29
  289.1 15.4 %collective-permute-start.86 = (f32[2,2,256]{2,1,0:T(2,128)S(1)}, f32[2,2,256]{2,1,0:T(2,128)S(1)}, u32[]{:S(2)}, u32[]{:S(2)}) collective-permute-start(f32[2,2,256]{2,1,0:T(2,128)S(1)} %add_add_fusion.18), channel_id=1, source_target_pairs={{0,8},{1,9},{2,10},{3,11},{4,12},{5,13},{6,14},{7,15},{8,0},{9,1},... | collective-permute-start | bytes 12296 | tf_op jit(solution)/shard_map/ppermute | solution.py:29
  290.2 15.7 %collective-permute-start.85 = (f32[2,2,256]{2,1,0:T(2,128)S(1)}, f32[2,2,256]{2,1,0:T(2,128)S(1)}, u32[]{:S(2)}, u32[]{:S(2)}) collective-permute-start(f32[2,2,256]{2,1,0:T(2,128)S(1)} %add_add_fusion.18), channel_id=1, source_target_pairs={{0,4},{1,5},{2,6},{3,7},{4,0},{5,1},{6,2},{7,3},{8,12},{9,13},{10,... | collective-permute-start | bytes 12296 | tf_op jit(solution)/shard_map/ppermute | solution.py:29
  303.3 13.0 %collective-permute-start.90 = (bf16[4,192,256]{2,1,0:T(8,128)(2,1)S(1)}, bf16[4,192,256]{2,1,0:T(8,128)(2,1)S(1)}, u32[]{:S(2)}, u32[]{:S(2)}) collective-permute-start(bf16[4,192,256]{2,1,0:T(8,128)(2,1)S(1)} %get-tuple-element.370), channel_id=1, source_target_pairs={{0,3},{1,2},{2,1},{3,0},{4,7},{5,6},{6,5},{7,4},{8,11},{9,10},{10,... | collective-permute-start | bytes 1179656 | tf_op jit(solution)/shard_map/ppermute | solution.py:29
  304.4 17.2 %collective-permute-start.88 = (bf16[4,192,256]{2,1,0:T(8,128)(2,1)S(1)}, bf16[4,192,256]{2,1,0:T(8,128)(2,1)S(1)}, u32[]{:S(2)}, u32[]{:S(2)}) collective-permute-start(bf16[4,192,256]{2,1,0:T(8,128)(2,1)S(1)} %get-tuple-element.371), channel_id=1, source_target_pairs={{0,1},{1,0},{2,3},{3,2},{4,5},{5,4},{6,7},{7,6},{8,9},{9,8},{10,11... | collective-permute-start | bytes 1179656 | tf_op jit(solution)/shard_map/ppermute | solution.py:29
  305.9 15.7 %collective-permute-start.89 = (bf16[4,192,256]{2,1,0:T(8,128)(2,1)S(1)}, bf16[4,192,256]{2,1,0:T(8,128)(2,1)S(1)}, u32[]{:S(2)}, u32[]{:S(2)}) collective-permute-start(bf16[4,192,256]{2,1,0:T(8,128)(2,1)S(1)} %get-tuple-element.372), channel_id=1, source_target_pairs={{0,2},{1,3},{2,0},{3,1},{4,6},{5,7},{6,4},{7,5},{8,10},{9,11},{10,... | collective-permute-start | bytes 1179656 | tf_op jit(solution)/shard_map/ppermute | solution.py:29
  316.3 15.2 %collective-permute-start.92 = (bf16[1,48,1024]{2,1,0:T(8,128)(2,1)S(1)}, bf16[1,48,1024]{2,1,0:T(8,128)(2,1)S(1)}, u32[]{:S(2)}, u32[]{:S(2)}) collective-permute-start(bf16[1,48,1024]{2,1,0:T(8,128)(2,1)S(1)} %get-tuple-element.400), channel_id=1, source_target_pairs={{0,4},{1,5},{2,6},{3,7},{4,0},{5,1},{6,2},{7,3},{8,12},{9,13},{10,... | collective-permute-start | bytes 294920 | tf_op jit(solution)/shard_map/ppermute | solution.py:29
  321.6 12.7 %collective-permute-start.91 = (bf16[2,208,256]{2,1,0:T(8,128)(2,1)S(1)}, bf16[2,208,256]{2,1,0:T(8,128)(2,1)S(1)}, u32[]{:S(2)}, u32[]{:S(2)}) collective-permute-start(bf16[2,208,256]{2,1,0:T(8,128)(2,1)S(1)} %get-tuple-element.302), channel_id=1, source_target_pairs={{1,0},{2,1},{3,2},{4,3},{5,4},{6,5},{7,6},{8,7},{9,8},{10,9},{11,1... | collective-permute-start | bytes 638984 | tf_op jit(solution)/shard_map/ppermute | solution.py:174
  (121 other events, 740.4 us)

commit v2 on v1

--- a/solution.py
+++ b/solution.py
@@ -196,10 +196,6 @@
     micro, frames, _, lanes = value.shape
     quads = pad_rows(value).reshape(micro * frames // 4, 4, ROWS, lanes)
     return jnp.concatenate([quads[:, place] for place in range(4)], -1)
-
-
-def in_vmem(array):
-    return pltpu.with_memory_space_constraint(array, pltpu.VMEM)
 
 
 PARTS = dict(
@@ -222,7 +218,7 @@
     return pltpu.with_memory_space_constraint(array, pltpu.VMEM)
 
 
-def call(body, steps, ins, outs, scratch=(), flops=0, name=None, limit=8, unroll=False, state=None):
+def call(body, steps, ins, outs, scratch=(), flops=0, name=None, limit=8, unroll=False, state=None, cheap=False):
     names = [given[0] if len(given) == 2 else None for given in outs]
     ins = [group(state[given[0]], given[1]) if len(given) == 2 else given for given in ins]
     if state is not None:
@@ -236,7 +232,7 @@
     blocks += [(shape, block, index) for shape, _, block, index, _ in outs]
 
     def view(ref, shape, block, index, step):
-        if block is None or tuple(block) == tuple(shape):
+        if block in (None, "hbm") or tuple(block) == tuple(shape):
             return ref
         spot = [
             slice(None) if size == full else pl.ds(place * size, size)
@@ -258,12 +254,22 @@
 
     moved = sum(array.size * array.dtype.itemsize for array in arrays)
     moved += sum(math.prod(shape) * jnp.dtype(dtype).itemsize for shape, dtype, *_ in outs)
+    if cheap:
+        flops = moved = 1
     vmem = pl.BlockSpec(memory_space=pltpu.VMEM)
+
+    def placed(array, block):
+        if block is None:
+            return array
+        return pltpu.with_memory_space_constraint(
+            array, pltpu.HBM if block == "hbm" else pltpu.VMEM
+        )
+
+    kinds = {None: pl.BlockSpec(memory_space=pltpu.SMEM), "hbm": pl.BlockSpec(memory_space=pl.ANY)}
     result = pl.pallas_call(
         kernel,
         in_specs=[
-            pl.BlockSpec(memory_space=pltpu.SMEM) if block is None else vmem
-            for _, block, _ in ins
+            kinds[block] if block in (None, "hbm") else vmem for _, block, _ in ins
         ],
         out_specs=[vmem] * len(outs),
         out_shape=[
@@ -276,7 +282,7 @@
             flops=int(flops), bytes_accessed=int(moved), transcendentals=0
         ),
         name=name,
-    )(*[array if block is None else in_vmem(array) for array, block, _ in ins])
+    )(*[placed(array, block) for array, block, _ in ins])
     if state is None:
         return result
     fresh = {name: array for name, array in zip(names, result) if name}
@@ -622,22 +628,26 @@
     return value * half, slope
 
 
-def chunked(body, frames, lanes, first=lambda f: None):
+def chunked(body, frames, lanes, first=lambda f: None, sums=None):
     full = PIX // CHUNK
     last = full * CHUNK
 
     def frame(f, carry):
         first(f)
-
-        def step(i, carry):
-            at = pl.ds(pl.multiple_of(i * CHUNK, CHUNK), CHUNK)
-            for start in range(0, lanes, SPAN):
-                body(f, at, CHUNK, slice(start, start + SPAN))
-            return carry
-
-        lax.fori_loop(0, full, step, 0)
         for start in range(0, lanes, SPAN):
-            body(f, pl.ds(last, CHUNK), PIX - last, slice(start, start + SPAN))
+            span = slice(start, start + SPAN)
+
+            def step(i, totals):
+                at = pl.ds(pl.multiple_of(i * CHUNK, CHUNK), CHUNK)
+                terms = body(f, at, CHUNK, span) or ()
+                return tuple(total + halves(term) for total, term in zip(totals, terms))
+
+            count = 0 if sums is None else sums.shape[0]
+            totals = tuple(jnp.zeros((8, SPAN), F32) for _ in range(count))
+            totals = lax.fori_loop(0, full, step, totals, unroll=full if lanes == SPAN else 4)
+            terms = body(f, pl.ds(last, CHUNK), PIX - last, span) or ()
+            for n, (total, term) in enumerate(zip(totals, terms)):
+                sums[n, :, span] += total + halves(term)
         return carry
 
     lax.fori_loop(0, frames, frame, 0)
@@ -649,35 +659,37 @@
 
 def k_fast_out(step, fthree, fast, cot, total, fgb, out, grad, sums, acc, *, steps, count):
     mean, scale = stats(total, CM, 4 * CF, 4.0 * count, CF)
-    gain, bias = fgb[0:1, 256:], fgb[1:2, 256:]
+    factor = fgb[0:1, 256:] * scale
+    shift = fgb[1:2, 256:] - mean * factor
 
     @pl.when(step % steps == 0)
     def _():
         acc[...] = jnp.zeros_like(acc)
 
     def body(f, rows, real, lanes):
-        hat = (fthree[f, rows, lanes] - mean[:, lanes]) * scale[:, lanes]
+        value = fthree[f, rows, lanes]
         quads = [fast[f, q, pl.ds(rows.start, real), :].astype(F32) for q in range(4)]
         if real < CHUNK:
             blank = jnp.zeros((CHUNK - real, CF), F32)
             quads = [jnp.concatenate([part, blank], 0) for part in quads]
-        value = hat * gain[:, lanes] + bias[:, lanes] + jnp.concatenate(quads, -1)
-        act, slope = gelu_both(value)
+        act, slope = gelu_both(
+            value * factor[:, lanes] + (shift[:, lanes] + jnp.concatenate(quads, -1))
+        )
         act = act.astype(BF)
         for q in range(4):
             piece = act[:real, q * CF : (q + 1) * CF]
             out[f, q, pl.ds(rows.start, real), :] = piece
         slope = slope * cot[f, rows, lanes].astype(F32)
         grad[f, rows, lanes] = slope
-        acc[0] += halves(slope)
-        acc[1] += halves(slope * hat)
-
-    chunked(body, fthree.shape[0], 4 * CF)
+        return slope, slope * value
+
+    chunked(body, fthree.shape[0], 4 * CF, sums=acc)
 
     @pl.when(step % steps == steps - 1)
     def _():
-        for row in range(2):
-            sums[0, row : row + 1] = jnp.sum(acc[row], 0, keepdims=True)
+        one = jnp.sum(acc[0], 0, keepdims=True)
+        sums[0, 0:1] = one
+        sums[0, 1:2] = scale * (jnp.sum(acc[1], 0, keepdims=True) - mean * one)
 
 
 def k_out(
@@ -689,31 +701,32 @@
 
     mean_a, scale_a = stats(total, 0, CS, count)
     mean_b, scale_b = stats(short_total, 0, CS, count)
-    gain_a, gain_b = gb[0:1, 768:1792], gb[0:1, 1792:]
-    bias = gb[1:2, 768:1792] + gb[1:2, 1792:]
+    factor_a = gb[0:1, 768:1792] * scale_a
+    factor_b = gb[0:1, 1792:] * scale_b
+    shift = gb[1:2, 768:1792] - mean_a * factor_a + (gb[1:2, 1792:] - mean_b * factor_b)
 
     @pl.when(step % steps == 0)
     def _():
         acc[...] = jnp.zeros_like(acc)
 
     def body(f, rows, real, lanes):
-        hat_a = (three[rows, lanes] - mean_a[:, lanes]) * scale_a[:, lanes]
-        hat_b = (short[f, rows, lanes] - mean_b[:, lanes]) * scale_b[:, lanes]
-        value = hat_a * gain_a[:, lanes] + (hat_b * gain_b[:, lanes] + bias[:, lanes])
-        smooth, slope = gelu_both(value)
+        value_a, value_b = three[rows, lanes], short[f, rows, lanes]
+        smooth, slope = gelu_both(
+            value_a * factor_a[:, lanes] + (value_b * factor_b[:, lanes] + shift[:, lanes])
+        )
         out[f, pl.ds(rows.start, real), lanes] = smooth.astype(BF)[:real]
         grad = slope * cot[f, rows, lanes].astype(F32)
         grad_out[f, rows, lanes] = grad
-        acc[0, :, lanes] += halves(grad)
-        acc[1, :, lanes] += halves(grad * hat_a)
-        acc[2, :, lanes] += halves(grad * hat_b)
-
-    chunked(body, act.shape[0], CS, expand)
+        return grad, grad * value_a, grad * value_b
+
+    chunked(body, act.shape[0], CS, expand, acc)
 
     @pl.when(step % steps == steps - 1)
     def _():
-        for row in range(3):
-            sums[0, row : row + 1, :CS] = jnp.sum(acc[row], 0, keepdims=True)
+        one, two_a, two_b = (jnp.sum(acc[row], 0, keepdims=True) for row in range(3))
+        sums[0, 0:1, :CS] = one
+        sums[0, 1:2, :CS] = scale_a * (two_a - mean_a * one)
+        sums[0, 2:3, :CS] = scale_b * (two_b - mean_b * one)
         sums[0, 0:2, CS:] = given[0]
         sums[0, 2:3, CS:] = jnp.zeros((1, 4 * CF), F32)
 
@@ -731,13 +744,16 @@
     _, two_b = back_parts(sums, 0, CS, count, rows=(0, 2))
     factor_a = gb[0:1, 768:1792] * scale_a
     factor_b = gb[0:1, 1792:] * scale_b
+    slant_a, slant_b = -factor_a * two_a * scale_a, -factor_b * two_b * scale_b
+    shift_a = -factor_a * one - slant_a * mean_a
+    shift_b = -factor_b * one - slant_b * mean_b
 
     def body(f, rows, real, lanes):
-        given = grad[f, rows, lanes] - one[:, lanes]
-        hat_a = (three[rows, lanes] - mean_a[:, lanes]) * scale_a[:, lanes]
-        hat_b = (short[f, rows, lanes] - mean_b[:, lanes]) * scale_b[:, lanes]
-        value_a = factor_a[:, lanes] * (given - hat_a * two_a[:, lanes])
-        value_b = factor_b[:, lanes] * (given - hat_b * two_b[:, lanes])
+        given = grad[f, rows, lanes]
+        value_a = three[rows, lanes] * slant_a[:, lanes] + shift_a[:, lanes]
+        value_b = short[f, rows, lanes] * slant_b[:, lanes] + shift_b[:, lanes]
+        value_a = value_a + given * factor_a[:, lanes]
+        value_b = value_b + given * factor_b[:, lanes]
         if real < CHUNK:
             row = lax.broadcasted_iota(jnp.int32, value_a.shape, 0)
             value_a = jnp.where(row < real, value_a, 0.0)
@@ -765,11 +781,12 @@
     mean, scale = stats(total3, CM, 4 * CF, 4.0 * count, CF)
     one, two = back_parts(sums, CS, 4 * CF, 4.0 * count, CF)
     factor = fgb[0:1, 256:] * scale
+    slant = -factor * two * scale
+    shift = -factor * one - slant * mean
 
     def fast_body(f, rows, real, lanes):
-        hat = (fthree[f, rows, lanes] - mean[:, lanes]) * scale[:, lanes]
-        value = fgrad[f, rows, lanes] - one[:, lanes] - hat * two[:, lanes]
-        value = factor[:, lanes] * value
+        value = fthree[f, rows, lanes] * slant[:, lanes] + shift[:, lanes]
+        value = value + fgrad[f, rows, lanes] * factor[:, lanes]
         if real < CHUNK:
             row = lax.broadcasted_iota(jnp.int32, value.shape, 0)
             value = jnp.where(row < real, value, 0.0)
@@ -900,8 +917,21 @@
         out[:, q] = value[:, :PIX, q * CF : (q + 1) * CF].astype(BF)
 
 
-def k_outer_joined(step, slow, lat, right, out, *, parts, taps):
-    value = mul_rows(slow if step < parts else lat, right).astype(BF)
+def k_outer_joined(step, slow, lat, right, out, slots, done, *, parts, taps):
+    wide = slots.shape[-1]
+
+    def fetch(part):
+        source = slow.at[:, :, part * wide : (part + 1) * wide]
+        return pltpu.make_async_copy(source, slots.at[part % 2], done.at[part % 2])
+
+    part = step - 1
+    if step == 0:
+        fetch(0).start()
+    else:
+        fetch(part).wait()
+        if step < parts:
+            fetch(step).start()
+    value = mul_rows(slots.at[part % 2] if step else lat, right).astype(BF)
     if taps == 1:
         out[...] = value
     else:
@@ -915,18 +945,21 @@
     block = slow.shape[:2] + (wide,)
     rows, lanes = slow.shape[-1] + lat.shape[-1], right.shape[-1]
     if taps == 1:
-        out = ((rows, lanes), BF, (wide, lanes), lambda g: (g, 0), True)
+        out = ((rows, lanes), BF, (wide, lanes), lambda g: ((g - 1) % (parts + 1), 0), True)
     else:
-        out = ((taps, rows, CM), BF, (taps, wide, CM), lambda g: (0, g, 0), True)
+        out = (
+            (taps, rows, CM), BF, (taps, wide, CM), lambda g: (0, (g - 1) % (parts + 1), 0), True
+        )
     return call(
         functools.partial(k_outer_joined, parts=parts, taps=taps),
         rows // wide,
         [
-            (slow, block, lambda g: (0, 0, min(g, parts - 1))),
+            (slow, "hbm", None),
             whole(lat),
             whole(right),
         ],
         [out],
+        scratch=[pltpu.VMEM((2,) + block, slow.dtype), pltpu.SemaphoreType.DMA((2,))],
         flops=2 * slow.shape[0] * slow.shape[1] * rows * lanes,
         name=name,
         unroll=True,
@@ -1087,8 +1120,8 @@
     slow = pad_rows(slow_in).reshape(groups, ROWS, CS)
     cot = pad_rows(slow_cotangent).reshape(groups, ROWS, CS)
     fcot = to_quads(fast_cotangent)
-    slow, fcot, edge_down, edge_up = tie([near, wide], slow, fcot, edge_down, edge_up)
-    cot = tie([near], cot)
+    slow, fcot = tie([near, wide], slow, fcot)
+    cot, edge_down, edge_up = tie([near], cot, edge_down, edge_up)
 
     fast_both = jnp.stack([fast_gain, fast_bias]).astype(F32)
     fgb = jnp.concatenate(
@@ -1390,26 +1423,7 @@
     slim = (groups, ROWS, 128)
 
     def weights_of_two(value, stage):
-        if stage == 0:
-            flows["space"], flows["fspace"] = call(
-                k_outer_space,
-                3,
-                [
-                    (cat_one, block, lambda g: (0, 0, g)), whole(two_taps),
-                    (fact_cat, slim, lambda g: (0, 0, g)), whole(ftwo_taps),
-                ],
-                [
-                    ((3, 3, CM, CM), BF, (3, 1, CM, CM), lambda g: (0, g, 0, 0), True),
-                    ((3, 3, CFM, CFM), BF, (3, 1, CFM, CFM), lambda g: (0, g, 0, 0), True),
-                ],
-                flops=2 * rows * 768 * 768,
-                name="slow_space_grad",
-                unroll=True,
-            )
-            value, flows["space"] = tie([], value, flows["space"])
-        elif stage == 1:
-            value = tie([flows["a"]], value)
-        return value
+        return tie([flows["a"]], value) if stage == 1 else value
 
     sums_c = all_sum(sums, weights_of_two)
 
@@ -1426,8 +1440,25 @@
         name="back_one",
     )
     rim_before, rim_after = from_before(tail), from_after(head)
+    flows["space"], flows["fspace"] = call(
+        k_outer_space,
+        3,
+        [
+            (cat_one, block, lambda g: (0, 0, g)), whole(two_taps),
+            (fact_cat, slim, lambda g: (0, 0, g)), whole(ftwo_taps),
+        ],
+        [
+            ((3, 3, CM, CM), BF, (3, 1, CM, CM), lambda g: (0, g, 0, 0), True),
+            ((3, 3, CFM, CFM), BF, (3, 1, CFM, CFM), lambda g: (0, g, 0, 0), True),
+        ],
+        flops=2 * rows * 768 * 768,
+        name="slow_space_grad",
+        unroll=True,
+    )
     slow_out = pixels_first(slow_out, slow_in.shape)
-    rim_before, rim_after, slow_out = tie([], rim_before, rim_after, slow_out)
+    rim_before, rim_after, slow_out, flows["space"] = tie(
+        [], rim_before, rim_after, slow_out, flows["space"]
+    )
     state, trio, sums = call(
         bind(k_trio, count=count),
         micro,
@@ -1460,10 +1491,12 @@
                 flops=2 * rows * 1792 * 1024,
                 name="slow_in_grad",
             )[0]
+        elif stage == 2:
+            value, flows["slow_in_grad"] = tie([flows["b"]], value, flows["slow_in_grad"])
         return value
 
     sums_d = all_sum(sums, weights_of_one)
-    slow_in_grad = pixels_first(flows["slow_in_grad"], slow_in.shape)
+    slow_in_grad = flows["slow_in_grad"]
 
     state, d_lat, head = call(
         bind(k_back_lat, count=count),
@@ -1476,7 +1509,6 @@
         state=state,
         name="back_lat",
     )
-    d_lat, head = tie([flows["b"]], d_lat, head)
     lat_rim = from_after(head)
     packed = devices <= CFM
     tops = [
@@ -1513,7 +1545,10 @@
         flat = flat.reshape(devices, -1, 128)
     last = Shares(spots, flat)
     fast_out = pixels_first(fast_out, fast_in.shape)
-    lat_rim, fast_out = tie([flows["a"], last], lat_rim, fast_out)
+    lat_rim, fast_out, slow_in_grad = tie(
+        [flows["a"], last], lat_rim, fast_out, slow_in_grad
+    )
+    slow_in_grad = pixels_first(slow_in_grad, slow_in.shape)
     state, fast_in_grad = call(
         k_fast_grad,
         micro,

time: 358 us -> 350 us (0.978)
  waiting for transfers between devices: 73.6 us -> 61.5 us
  starting transfers between devices: 135 us -> 139 us
    ppermute x4, waiting for transfers between devices: 9.31 us -> 1.5 us  [from_after(): return lax.ppermute(value, AXES, [(i + 1, i) for i in range(count - 1)])]
    ppermute x3, waiting for transfers between devices: 5.82 us -> 0.01 us  [from_before(): return lax.ppermute(value, AXES, [(i, i + 1) for i in range(count - 1)])]
    ppermute x98, starting transfers between devices: 120 us -> 123 us  [swap(): return lax.ppermute(value, AXES, [(i, i ^ bit) for i in range(count)])]
    unnamed x110 -> x104, local copies, waits for them, and re-layouts: 20.2 us -> 20 us
  transfers between devices with their start and end apart: 105 -> 105, of which waited for: 42 -> 47; matrix products, arithmetic and copies ran while one was open for 10% -> 11% of each run, Pallas kernels for 15% -> 16%
where the time goes in v2:
time: 350 us; the launch traced here: 345 us
  starting transfers between devices  139 us (40%)
  Pallas kernels  84.1 us (24%)
  waiting for transfers between devices  61.5 us (18%)
  local copies, waits for them, and re-layouts  47.1 us (13%)
  other arithmetic  10.5 us (3%)
    ppermute x98, starting transfers between devices, swap(): return lax.ppermute(value, AXES, [(i, i ^ bit) for i in range(count)])  123 us
    pallas_call x23, Pallas kernels, call(): pl.pallas_call(kernel, in_specs=[kinds[block] if block in (None, 'hbm') e...  84.1 us
    ppermute x98, waiting for transfers between devices, swap(): return lax.ppermute(value, AXES, [(i, i ^ bit) for i in range(count)])  60 us
    unnamed x104, local copies, waits for them, and re-layouts  20 us
    ppermute x3, starting transfers between devices, from_before(): return lax.ppermute(value, AXES, [(i, i + 1) for i in range(count - 1)])  9.91 us
    reshape x3, local copies, waits for them, and re-layouts, pixels_first(): return jnp.swapaxes(value.reshape(whole_shape), 1, 2)  9.69 us
  transfers between devices with their start and end apart: 105, of which 47 were waited for; matrix products, arithmetic and copies ran while one was open for 11% of the time, Pallas kernels for 16%

profile of v2, /device:TPU:0, one launch (start us, length us, event | category | flops | bytes accessed | tf_op | source)
XLA Modules:
  0.0 344.5 jit_solution(10707573039454697894)
XLA Ops:
  5.9 5.1 %collective-permute-start.2 = (bf16[1,168,256]{2,1,0:T(8,128)(2,1)S(1)}, bf16[1,168,256]{2,1,0:T(8,128)(2,1)S(1)}, u32[]{:S(2)}, u32[]{:S(2)}) collective-permute-start(bf16[1,168,256]{2,1,0:T(8,128)(2,1)S(1)} %pad_bitcast_fusion), channel_id=1, source_target_pairs={{0,12},{1,13},{2,14},{3,15},{4,8},{5,9},{6,10},{7,11},{8,4},{9,5},... | collective-permute-start | bytes 258056 | tf_op jit(solution)/shard_map/ppermute | solution.py:29
  14.9 3.2 copy.65
  18.2 3.7 %collective-permute-start.10 = (bf16[1,40,1024]{2,1,0:T(8,128)(2,1)S(1)}, bf16[1,40,1024]{2,1,0:T(8,128)(2,1)S(1)}, u32[]{:S(2)}, u32[]{:S(2)}) collective-permute-start(bf16[1,40,1024]{2,1,0:T(8,128)(2,1)S(1)} %bitcast.428), channel_id=1, source_target_pairs={{0,12},{1,13},{2,14},{3,15},{4,8},{5,9},{6,10},{7,11},{8,4},{9,5},... | collective-permute-start | bytes 245768 | tf_op jit(solution)/shard_map/ppermute | solution.py:29
  32.3 3.5 %collective-permute-done.8 = bf16[1,40,1024]{2,1,0:T(8,128)(2,1)S(1)} collective-permute-done((bf16[1,40,1024]{2,1,0:T(8,128)(2,1)S(1)}, bf16[1,40,1024]{2,1,0:T(8,128)(2,1)S(1)}, u32[]{:S(2)}, u32[]{:S(2)}) %collective-permute-start.8) | collective-permute-done | bytes 81952 | tf_op jit(solution)/shard_map/ppermute | solution.py:29
  35.8 3.2 collective-permute-done.6
  44.6 4.8 %collective-permute-start.3 = (bf16[2,2,196,128]{3,2,1,0:T(8,128)(2,1)S(1)}, bf16[2,2,196,128]{3,2,1,0:T(8,128)(2,1)S(1)}, u32[]{:S(2)}, u32[]{:S(2)}) collective-permute-start(bf16[2,2,196,128]{3,2,1,0:T(8,128)(2,1)S(1)} %slice.134), channel_id=1, source_target_pairs={{0,1},{1,2},{2,3},{3,4},{4,5},{5,6},{6,7},{7,8},{8,9},{9,10},{10,1... | collective-permute-start | bytes 602120 | tf_op jit(solution)/shard_map/ppermute | solution.py:169
  51.5 3.5 %collective-permute-start.18 = (bf16[4,40,1024]{2,1,0:T(8,128)(2,1)S(1)}, bf16[4,40,1024]{2,1,0:T(8,128)(2,1)S(1)}, u32[]{:S(2)}, u32[]{:S(2)}) collective-permute-start(bf16[4,40,1024]{2,1,0:T(8,128)(2,1)S(1)} %maximum_bitcast_fusion.1), channel_id=1, source_target_pairs={{0,3},{1,2},{2,1},{3,0},{4,7},{5,6},{6,5},{7,4},{8,11},{9,10},{10,... | collective-permute-start | bytes 983048 | tf_op jit(solution)/shard_map/ppermute | solution.py:29
  62.2 3.2 collective-permute-start.12
  66.8 5.5 %collective-permute-done.15 = f32[2,2,384]{2,1,0:T(2,128)S(1)} collective-permute-done((f32[2,2,384]{2,1,0:T(2,128)S(1)}, f32[2,2,384]{2,1,0:T(2,128)S(1)}, u32[]{:S(2)}, u32[]{:S(2)}) %collective-permute-start.15) | collective-permute-done | bytes 6176 | tf_op jit(solution)/shard_map/ppermute | solution.py:29
  72.3 3.6 %collective-permute-done.13 = f32[2,2,384]{2,1,0:T(2,128)S(1)} collective-permute-done((f32[2,2,384]{2,1,0:T(2,128)S(1)}, f32[2,2,384]{2,1,0:T(2,128)S(1)}, u32[]{:S(2)}, u32[]{:S(2)}) %collective-permute-start.13) | collective-permute-done | bytes 6176 | tf_op jit(solution)/shard_map/ppermute | solution.py:29
  76.5 3.4 collective-permute-start.21
  80.9 3.3 collective-permute-start.27
  85.9 4.6 %slow_time_taps.1 = (bf16[8,208,256]{2,1,0:T(8,128)(2,1)S(1)}, f32[8,208,768]{2,1,0:T(8,128)S(1)}, bf16[2,208,256]{2,1,0:T(8,128)(2,1)S(1)}, bf16[2,208,256]{2,1,0:T(8,128)(2,1)S(1)}) custom-call(f32[8]{0:T(128)S(1)} %reshape.404.refs_0_, f32[8,208,256]{2,1,0:T(8,128)S(1)} %get-tuple-element.200.refs_1_.refs_8_, ...), custom_call_target="tpu_custom_call" | custom-call | flops 3271557120 | bytes 14561312 | tf_op jit(solution)/shard_map/slow_time_taps/pallas_call | solution.py:269
  93.9 3.6 %collective-permute-start.31 = (bf16[4,104,256]{2,1,0:T(8,128)(2,1)S(1)}, bf16[4,104,256]{2,1,0:T(8,128)(2,1)S(1)}, u32[]{:S(2)}, u32[]{:S(2)}) collective-permute-start(bf16[4,104,256]{2,1,0:T(8,128)(2,1)S(1)} %maximum_bitcast_fusion.2), channel_id=1, source_target_pairs={{0,3},{1,2},{2,1},{3,0},{4,7},{5,6},{6,5},{7,4},{8,11},{9,10},{10,... | collective-permute-start | bytes 638984 | tf_op jit(solution)/shard_map/ppermute | solution.py:29
  99.1 6.5 %shortcut_and_fast_space.1 = (f32[8,208,1024]{2,1,0:T(8,128)S(1)}, bf16[8,208,384]{2,1,0:T(8,128)(2,1)S(1)}, f32[8,208,128]{2,1,0:T(8,128)S(1)}, f32[2,2,1152]{2,1,0:T(2,128)S(1)}) custom-call(bf16[8,208,1024]{2,1,0:T(8,128)(2,1)S(1)} %bitcast.406, bf16[8,208,256]{2,1,0:T(8,128)(2,1)S(1)} %get-tuple-element.217.refs_1_, bf16[1280,1024]{1,0:T(8,128)(2,1)S(1)} %bitcast.392, ...), custom_call_target="tpu_custom_call" | custom-call | flops 4362076160 | bytes 18069504 | tf_op jit(solution)/shard_map/shortcut_and_fast_space/pallas_call | solution.py:269
  125.8 4.0 %slow_space.1 = (bf16[8,208,768]{2,1,0:T(8,128)(2,1)S(1)}, f32[8,208,256]{2,1,0:T(8,128)S(1)}, bf16[8,208,128]{2,1,0:T(8,128)(2,1)S(1)}, f32[8,208,512]{2,1,0:T(...) custom-call(f32[8,208,256]{2,1,0:T(8,128)S(1)} %get-tuple-element.223.refs_0_.refs_6_.refs_1_, ...), custom_call_target="tpu_custom_call" | custom-call | flops 1962934272 | bytes 14268416 | tf_op jit(solution)/shard_map/slow_space/pallas_call | solution.py:269
  159.5 3.2 fast_out.1
  163.9 9.7 %slow_out.1 = (bf16[8,196,1024]{2,1,0:T(8,128)(2,1)S(1)}, f32[8,208,1024]{2,1,0:T(8,128)S(1)}, f32[2,3,1536]{2,1,0:T(4,128)S(1)}) custom-call(bf16[8,208,256]{2,1,0:T(8,128)(2,1)S(1)} %get-tuple-element.243.refs_0_, bf16[256,1024]{1,0:T(8,128)(2,1)S(1)} %get-tuple-element.244.refs_1_, f32[8,208,1024]{2,1,0:T(8,128)S(1)} %get-tuple-element.245.refs_2_, ...), custom_call_target="tpu_custom_call" | custom-call | flops 872415232 | bytes 21733376 | tf_op jit(solution)/shard_map/slow_out/pallas_call | solution.py:269
  191.1 7.2 %back_three.1 = (bf16[8,208,1024]{2,1,0:T(8,128)(2,1)S(1)}, bf16[8,208,1024]{2,1,0:T(8,128)(2,1)S(1)}, f32[8,208,256]{2,1,0:T(8,128)S(1)}, f32[2,2,256]{2,1,0:T(2,128)S(1)}) custom-call(bf16[8,208,256]{2,1,0:T(8,128)(2,1)S(1)} %get-tuple-element.243.refs_0_, bf16[256,1024]{1,0:T(8,128)(2,1)S(1)} %get-tuple-element.244.refs_1_, ...), custom_call_target="tpu_custom_call" | custom-call | flops 1744830464 | bytes 25346048 | tf_op jit(solution)/shard_map/back_three/pallas_call | solution.py:269
  200.6 5.8 %projection_grad.1 = bf16[1280,1024]{1,0:T(8,128)(2,1)S(1)} custom-call(bf16[8,208,1024]{2,1,0:T(8,128)(2,1)} %bitcast.403, bf16[8,208,256]{2,1,0:T(8,128)(2,1)S(1)} %copy-done.25, bf16[8,208,1024]{2,1,0:T(8,128)(2,1)S(1)} %get-tuple-element.257.refs_2_.refs_5_.refs_1_), custom_call_target="tpu_custom_call" | custom-call | flops 4362076160 | bytes 10289152 | tf_op jit(solution)/shard_map/projection_grad/pallas_call | solution.py:269
  223.1 5.8 %back_two.1 = (bf16[8,208,768]{2,1,0:T(8,128)(2,1)S(1)}, f32[8,208,256]{2,1,0:T(8,128)S(1)}, bf16[8,208,384]{2,1,0:T(8,128)(2,1)S(1)}, f32[8,208,128]{2,1,0:T(8,128)S(1)}, f32[2,2,384]{2,1,0:T(2,128)S(1)}) custom-call(f32[8,208,256]{2,1,0:T(8,128)S(1)} %get-tuple-element.241.refs_0_.refs_8_, f32[2,2,768]{2,1,0:T(2,128)S(1)} %add_add_fusion.9.refs_1_.refs_3_.refs_9_.refs_2_, ...), custom_call_target="tpu_custom_call" | custom-call | flops 1962934272 | bytes 16678912 | tf_op jit(solution)/shard_map/back_two/pallas_call | solution.py:269
  234.1 3.9 %collective-permute-done.71 = f32[2,2,384]{2,1,0:T(2,128)S(1)} collective-permute-done((f32[2,2,384]{2,1,0:T(2,128)S(1)}, f32[2,2,384]{2,1,0:T(2,128)S(1)}, u32[]{:S(2)}, u32[]{:S(2)}) %collective-permute-start.71) | collective-permute-done | bytes 6176 | tf_op jit(solution)/shard_map/ppermute | solution.py:29
  250.3 3.2 collective-permute-start.78
  255.1 4.2 %copy.126 = bf16[2,4,196,1024]{3,1,2,0:T(4,128)(2,1)} copy(bf16[2,4,196,1024]{3,2,1,0:T(8,128)(2,1)S(1)} %bitcast.407) | data formatting | bytes 6422528 | tf_op jit(solution)/shard_map/reshape | solution.py:1348
  259.3 3.1 slow_space_grad.1
  263.9 3.4 back_lateral.1
  269.1 5.8 %slow_time_grad.1 = bf16[3,1280,256]{2,1,0:T(8,128)(2,1)S(1)} custom-call(bf16[8,208,1024]{2,1,0:T(8,128)(2,1)} %bitcast.404, bf16[8,208,256]{2,1,0:T(8,128)(2,1)S(1)} %copy-done.26, bf16[8,208,768]{2,1,0:T(8,128)(2,1)S(1)} %get-tuple-element.298.refs_2_.refs_0_), custom_call_target="tpu_custom_call" | custom-call | flops 3271557120 | bytes 8781824 | tf_op jit(solution)/shard_map/slow_time_grad/pallas_call | solution.py:269
  293.5 6.6 %slow_in_grad.1 = bf16[8,196,1024]{2,1,0:T(8,128)(2,1)S(1)} custom-call(bf16[8,208,768]{2,1,0:T(8,128)(2,1)S(1)} %get-tuple-element.298.refs_2_.refs_0_, bf16[8,208,1024]{2,1,0:T(8,128)(2,1)S(1)} %copy-done.7, bf16[1280,768]{1,0:T(8,128)(2,1)S(1)} %copy-done.13, bf16[1280,1024]{1,0:T(8,128)(2,1)S(1)} %bitcast.394), custom_call_target="tpu_custom_call" | custom-call | flops 6106906624 | bytes 13762560 | tf_op jit(solution)/shard_map/slow_in_grad/pallas_call | solution.py:269
  304.7 3.5 %collective-permute-done.88 = bf16[4,192,256]{2,1,0:T(8,128)(2,1)S(1)} collective-permute-done((bf16[4,192,256]{2,1,0:T(8,128)(2,1)S(1)}, bf16[4,192,256]{2,1,0:T(8,128)(2,1)S(1)}, u32[]{:S(2)}, u32[]{:S(2)}) %collective-permute-start.88) | collective-permute-done | bytes 393248 | tf_op jit(solution)/shard_map/ppermute | solution.py:29
  314.7 3.5 %collective-permute-start.95 = (bf16[16,64,128]{2,1,0:T(8,128)(2,1)S(1)}, bf16[16,64,128]{2,1,0:T(8,128)(2,1)S(1)}, u32[]{:S(2)}, u32[]{:S(2)}) collective-permute-start(bf16[16,64,128]{2,1,0:T(8,128)(2,1)S(1)} %dynamic-slice_bitcast_fusion), channel_id=1, source_target_pairs={{0,16},{1,17},{2,18},{3,19},{4,20},{5,21},{6,22},{7,23},{8,24},{9,... | collective-permute-start | bytes 786440 | tf_op jit(solution)/shard_map/ppermute | solution.py:29
  320.4 3.0 collective-permute-start.96
  325.9 4.2 %copy.125 = bf16[2,4,196,1024]{3,1,2,0:T(4,128)(2,1)} copy(bf16[2,4,196,1024]{3,2,1,0:T(8,128)(2,1)S(1)} %bitcast.408) | data formatting | bytes 6422528 | tf_op jit(solution)/shard_map/reshape | solution.py:1348
  (426 shorter events, 201.3 us)
Async XLA Ops:
  5.9 12.2 %collective-permute-start.2 = (bf16[1,168,256]{2,1,0:T(8,128)(2,1)S(1)}, bf16[1,168,256]{2,1,0:T(8,128)(2,1)S(1)}, u32[]{:S(2)}, u32[]{:S(2)}) collective-permute-start(bf16[1,168,256]{2,1,0:T(8,128)(2,1)S(1)} %pad_bitcast_fusion), channel_id=1, source_target_pairs={{0,12},{1,13},{2,14},{3,15},{4,8},{5,9},{6,10},{7,11},{8,4},{9,5},... | collective-permute-start | bytes 258056 | tf_op jit(solution)/shard_map/ppermute | solution.py:29
  18.2 13.2 %collective-permute-start.10 = (bf16[1,40,1024]{2,1,0:T(8,128)(2,1)S(1)}, bf16[1,40,1024]{2,1,0:T(8,128)(2,1)S(1)}, u32[]{:S(2)}, u32[]{:S(2)}) collective-permute-start(bf16[1,40,1024]{2,1,0:T(8,128)(2,1)S(1)} %bitcast.428), channel_id=1, source_target_pairs={{0,12},{1,13},{2,14},{3,15},{4,8},{5,9},{6,10},{7,11},{8,4},{9,5},... | collective-permute-start | bytes 245768 | tf_op jit(solution)/shard_map/ppermute | solution.py:29
  22.1 13.8 %collective-permute-start.7 = (bf16[4,168,256]{2,1,0:T(8,128)(2,1)S(1)}, bf16[4,168,256]{2,1,0:T(8,128)(2,1)S(1)}, u32[]{:S(2)}, u32[]{:S(2)}) collective-permute-start(bf16[4,168,256]{2,1,0:T(8,128)(2,1)S(1)} %maximum_bitcast_fusion), channel_id=1, source_target_pairs={{0,3},{1,2},{2,1},{3,0},{4,7},{5,6},{6,5},{7,4},{8,11},{9,10},{10,... | collective-permute-start | bytes 1032200 | tf_op jit(solution)/shard_map/ppermute | solution.py:29
  24.6 14.5 %collective-permute-start.6 = (bf16[4,168,256]{2,1,0:T(8,128)(2,1)S(1)}, bf16[4,168,256]{2,1,0:T(8,128)(2,1)S(1)}, u32[]{:S(2)}, u32[]{:S(2)}) collective-permute-start(bf16[4,168,256]{2,1,0:T(8,128)(2,1)S(1)} %maximum_bitcast_fusion), channel_id=1, source_target_pairs={{0,2},{1,3},{2,0},{3,1},{4,6},{5,7},{6,4},{7,5},{8,10},{9,11},{10,... | collective-permute-start | bytes 1032200 | tf_op jit(solution)/shard_map/ppermute | solution.py:29
  25.1 14.1 %collective-permute-start.5 = (bf16[4,168,256]{2,1,0:T(8,128)(2,1)S(1)}, bf16[4,168,256]{2,1,0:T(8,128)(2,1)S(1)}, u32[]{:S(2)}, u32[]{:S(2)}) collective-permute-start(bf16[4,168,256]{2,1,0:T(8,128)(2,1)S(1)} %maximum_bitcast_fusion), channel_id=1, source_target_pairs={{0,1},{1,0},{2,3},{3,2},{4,5},{5,4},{6,7},{7,6},{8,9},{9,8},{10,11... | collective-permute-start | bytes 1032200 | tf_op jit(solution)/shard_map/ppermute | solution.py:29
  40.7 14.9 %collective-permute-start.11 = (bf16[16,168,256]{2,1,0:T(8,128)(2,1)}, bf16[16,168,256]{2,1,0:T(8,128)(2,1)}, u32[]{:S(2)}, u32[]{:S(2)}) collective-permute-start(bf16[16,168,256]{2,1,0:T(8,128)(2,1)} %bitcast.32), channel_id=1, source_target_pairs={{0,16},{1,17},{2,18},{3,19},{4,20},{5,21},{6,22},{7,23},{8,24},{9,... | collective-permute-start | bytes 4128776 | tf_op jit(solution)/shard_map/ppermute | solution.py:29
  43.3 12.1 %collective-permute-start.4 = (bf16[2,1,196,128]{3,2,1,0:T(8,128)(2,1)S(1)}, bf16[2,1,196,128]{3,2,1,0:T(8,128)(2,1)S(1)}, u32[]{:S(2)}, u32[]{:S(2)}) collective-permute-start(bf16[2,1,196,128]{3,2,1,0:T(8,128)(2,1)S(1)} %slice_multiply_fusion), channel_id=1, source_target_pairs={{1,0},{2,1},{3,2},{4,3},{5,4},{6,5},{7,6},{8,7},{9,8},{10,9},{11,1... | collective-permute-start | bytes 301064 | tf_op jit(solution)/shard_map/ppermute | solution.py:174
  51.5 24.5 %collective-permute-start.18 = (bf16[4,40,1024]{2,1,0:T(8,128)(2,1)S(1)}, bf16[4,40,1024]{2,1,0:T(8,128)(2,1)S(1)}, u32[]{:S(2)}, u32[]{:S(2)}) collective-permute-start(bf16[4,40,1024]{2,1,0:T(8,128)(2,1)S(1)} %maximum_bitcast_fusion.1), channel_id=1, source_target_pairs={{0,3},{1,2},{2,1},{3,0},{4,7},{5,6},{6,5},{7,4},{8,11},{9,10},{10,... | collective-permute-start | bytes 983048 | tf_op jit(solution)/shard_map/ppermute | solution.py:29
  55.0 21.0 %collective-permute-start.17 = (bf16[4,40,1024]{2,1,0:T(8,128)(2,1)S(1)}, bf16[4,40,1024]{2,1,0:T(8,128)(2,1)S(1)}, u32[]{:S(2)}, u32[]{:S(2)}) collective-permute-start(bf16[4,40,1024]{2,1,0:T(8,128)(2,1)S(1)} %maximum_bitcast_fusion.1), channel_id=1, source_target_pairs={{0,2},{1,3},{2,0},{3,1},{4,6},{5,7},{6,4},{7,5},{8,10},{9,11},{10,... | collective-permute-start | bytes 983048 | tf_op jit(solution)/shard_map/ppermute | solution.py:29
  55.4 20.6 %collective-permute-start.16 = (bf16[4,40,1024]{2,1,0:T(8,128)(2,1)S(1)}, bf16[4,40,1024]{2,1,0:T(8,128)(2,1)S(1)}, u32[]{:S(2)}, u32[]{:S(2)}) collective-permute-start(bf16[4,40,1024]{2,1,0:T(8,128)(2,1)S(1)} %maximum_bitcast_fusion.1), channel_id=1, source_target_pairs={{0,1},{1,0},{2,3},{3,2},{4,5},{5,4},{6,7},{7,6},{8,9},{9,8},{10,11... | collective-permute-start | bytes 983048 | tf_op jit(solution)/shard_map/ppermute | solution.py:29
  76.4 17.5 %collective-permute-start.24 = (bf16[16,40,1024]{2,1,0:T(8,128)(2,1)S(1)}, bf16[16,40,1024]{2,1,0:T(8,128)(2,1)S(1)}, u32[]{:S(2)}, u32[]{:S(2)}) collective-permute-start(bf16[16,40,1024]{2,1,0:T(8,128)(2,1)S(1)} %bitcast.424), channel_id=1, source_target_pairs={{0,16},{1,17},{2,18},{3,19},{4,20},{5,21},{6,22},{7,23},{8,24},{9,... | collective-permute-start | bytes 3932168 | tf_op jit(solution)/shard_map/ppermute | solution.py:29
  80.9 11.6 %collective-permute-start.27 = (bf16[1,104,256]{2,1,0:T(8,128)(2,1)S(1)}, bf16[1,104,256]{2,1,0:T(8,128)(2,1)S(1)}, u32[]{:S(2)}, u32[]{:S(2)}) collective-permute-start(bf16[1,104,256]{2,1,0:T(8,128)(2,1)S(1)} %bitcast.431), channel_id=1, source_target_pairs={{0,12},{1,13},{2,14},{3,15},{4,8},{5,9},{6,10},{7,11},{8,4},{9,5},... | collective-permute-start | bytes 159752 | tf_op jit(solution)/shard_map/ppermute | solution.py:29
  90.6 16.1 %collective-permute-start.22 = (bf16[2,208,256]{2,1,0:T(8,128)(2,1)S(1)}, bf16[2,208,256]{2,1,0:T(8,128)(2,1)S(1)}, u32[]{:S(2)}, u32[]{:S(2)}) collective-permute-start(bf16[2,208,256]{2,1,0:T(8,128)(2,1)S(1)} %get-tuple-element.210), channel_id=1, source_target_pairs={{0,1},{1,2},{2,3},{3,4},{4,5},{5,6},{6,7},{7,8},{8,9},{9,10},{10,1... | collective-permute-start | bytes 638984 | tf_op jit(solution)/shard_map/ppermute | solution.py:169
  92.5 14.2 %collective-permute-start.23 = (bf16[2,208,256]{2,1,0:T(8,128)(2,1)S(1)}, bf16[2,208,256]{2,1,0:T(8,128)(2,1)S(1)}, u32[]{:S(2)}, u32[]{:S(2)}) collective-permute-start(bf16[2,208,256]{2,1,0:T(8,128)(2,1)S(1)} %get-tuple-element.211), channel_id=1, source_target_pairs={{1,0},{2,1},{3,2},{4,3},{5,4},{6,5},{7,6},{8,7},{9,8},{10,9},{11,1... | collective-permute-start | bytes 638984 | tf_op jit(solution)/shard_map/ppermute | solution.py:174
  93.9 17.4 %collective-permute-start.31 = (bf16[4,104,256]{2,1,0:T(8,128)(2,1)S(1)}, bf16[4,104,256]{2,1,0:T(8,128)(2,1)S(1)}, u32[]{:S(2)}, u32[]{:S(2)}) collective-permute-start(bf16[4,104,256]{2,1,0:T(8,128)(2,1)S(1)} %maximum_bitcast_fusion.2), channel_id=1, source_target_pairs={{0,3},{1,2},{2,1},{3,0},{4,7},{5,6},{6,5},{7,4},{8,11},{9,10},{10,... | collective-permute-start | bytes 638984 | tf_op jit(solution)/shard_map/ppermute | solution.py:29
  97.5 13.9 %collective-permute-start.30 = (bf16[4,104,256]{2,1,0:T(8,128)(2,1)S(1)}, bf16[4,104,256]{2,1,0:T(8,128)(2,1)S(1)}, u32[]{:S(2)}, u32[]{:S(2)}) collective-permute-start(bf16[4,104,256]{2,1,0:T(8,128)(2,1)S(1)} %maximum_bitcast_fusion.2), channel_id=1, source_target_pairs={{0,2},{1,3},{2,0},{3,1},{4,6},{5,7},{6,4},{7,5},{8,10},{9,11},{10,... | collective-permute-start | bytes 638984 | tf_op jit(solution)/shard_map/ppermute | solution.py:29
  98.1 13.3 %collective-permute-start.29 = (bf16[4,104,256]{2,1,0:T(8,128)(2,1)S(1)}, bf16[4,104,256]{2,1,0:T(8,128)(2,1)S(1)}, u32[]{:S(2)}, u32[]{:S(2)}) collective-permute-start(bf16[4,104,256]{2,1,0:T(8,128)(2,1)S(1)} %maximum_bitcast_fusion.2), channel_id=1, source_target_pairs={{0,1},{1,0},{2,3},{3,2},{4,5},{5,4},{6,7},{7,6},{8,9},{9,8},{10,11... | collective-permute-start | bytes 638984 | tf_op jit(solution)/shard_map/ppermute | solution.py:29
  219.5 22.1 %collective-permute-start.74 = (bf16[4,48,1024]{2,1,0:T(8,128)(2,1)S(1)}, bf16[4,48,1024]{2,1,0:T(8,128)(2,1)S(1)}, u32[]{:S(2)}, u32[]{:S(2)}) collective-permute-start(bf16[4,48,1024]{2,1,0:T(8,128)(2,1)S(1)} %get-tuple-element.373), channel_id=1, source_target_pairs={{0,3},{1,2},{2,1},{3,0},{4,7},{5,6},{6,5},{7,4},{8,11},{9,10},{10,... | collective-permute-start | bytes 1179656 | tf_op jit(solution)/shard_map/ppermute | solution.py:29
  221.9 19.7 %collective-permute-start.72 = (bf16[4,48,1024]{2,1,0:T(8,128)(2,1)S(1)}, bf16[4,48,1024]{2,1,0:T(8,128)(2,1)S(1)}, u32[]{:S(2)}, u32[]{:S(2)}) collective-permute-start(bf16[4,48,1024]{2,1,0:T(8,128)(2,1)S(1)} %get-tuple-element.374), channel_id=1, source_target_pairs={{0,1},{1,0},{2,3},{3,2},{4,5},{5,4},{6,7},{7,6},{8,9},{9,8},{10,11... | collective-permute-start | bytes 1179656 | tf_op jit(solution)/shard_map/ppermute | solution.py:29
  222.5 19.2 %collective-permute-start.73 = (bf16[4,48,1024]{2,1,0:T(8,128)(2,1)S(1)}, bf16[4,48,1024]{2,1,0:T(8,128)(2,1)S(1)}, u32[]{:S(2)}, u32[]{:S(2)}) collective-permute-start(bf16[4,48,1024]{2,1,0:T(8,128)(2,1)S(1)} %get-tuple-element.375), channel_id=1, source_target_pairs={{0,2},{1,3},{2,0},{3,1},{4,6},{5,7},{6,4},{7,5},{8,10},{9,11},{10,... | collective-permute-start | bytes 1179656 | tf_op jit(solution)/shard_map/ppermute | solution.py:29
  250.3 12.1 %collective-permute-start.78 = (bf16[2,208,384]{2,1,0:T(8,128)(2,1)S(1)}, bf16[2,208,384]{2,1,0:T(8,128)(2,1)S(1)}, u32[]{:S(2)}, u32[]{:S(2)}) collective-permute-start(bf16[2,208,384]{2,1,0:T(8,128)(2,1)S(1)} %get-tuple-element.278), channel_id=1, source_target_pairs={{0,1},{1,2},{2,3},{3,4},{4,5},{5,6},{6,7},{7,8},{8,9},{9,10},{10,1... | collective-permute-start | bytes 958472 | tf_op jit(solution)/shard_map/ppermute | solution.py:169
  286.4 13.7 %collective-permute-start.86 = (f32[2,2,256]{2,1,0:T(2,128)S(1)}, f32[2,2,256]{2,1,0:T(2,128)S(1)}, u32[]{:S(2)}, u32[]{:S(2)}) collective-permute-start(f32[2,2,256]{2,1,0:T(2,128)S(1)} %add_add_fusion.18), channel_id=1, source_target_pairs={{0,8},{1,9},{2,10},{3,11},{4,12},{5,13},{6,14},{7,15},{8,0},{9,1},... | collective-permute-start | bytes 12296 | tf_op jit(solution)/shard_map/ppermute | solution.py:29
  287.4 14.3 %collective-permute-start.85 = (f32[2,2,256]{2,1,0:T(2,128)S(1)}, f32[2,2,256]{2,1,0:T(2,128)S(1)}, u32[]{:S(2)}, u32[]{:S(2)}) collective-permute-start(f32[2,2,256]{2,1,0:T(2,128)S(1)} %add_add_fusion.18), channel_id=1, source_target_pairs={{0,4},{1,5},{2,6},{3,7},{4,0},{5,1},{6,2},{7,3},{8,12},{9,13},{10,... | collective-permute-start | bytes 12296 | tf_op jit(solution)/shard_map/ppermute | solution.py:29
  289.9 13.0 %collective-permute-start.90 = (bf16[4,192,256]{2,1,0:T(8,128)(2,1)S(1)}, bf16[4,192,256]{2,1,0:T(8,128)(2,1)S(1)}, u32[]{:S(2)}, u32[]{:S(2)}) collective-permute-start(bf16[4,192,256]{2,1,0:T(8,128)(2,1)S(1)} %get-tuple-element.370), channel_id=1, source_target_pairs={{0,3},{1,2},{2,1},{3,0},{4,7},{5,6},{6,5},{7,4},{8,11},{9,10},{10,... | collective-permute-start | bytes 1179656 | tf_op jit(solution)/shard_map/ppermute | solution.py:29
  291.0 17.2 %collective-permute-start.88 = (bf16[4,192,256]{2,1,0:T(8,128)(2,1)S(1)}, bf16[4,192,256]{2,1,0:T(8,128)(2,1)S(1)}, u32[]{:S(2)}, u32[]{:S(2)}) collective-permute-start(bf16[4,192,256]{2,1,0:T(8,128)(2,1)S(1)} %get-tuple-element.371), channel_id=1, source_target_pairs={{0,1},{1,0},{2,3},{3,2},{4,5},{5,4},{6,7},{7,6},{8,9},{9,8},{10,11... | collective-permute-start | bytes 1179656 | tf_op jit(solution)/shard_map/ppermute | solution.py:29
  292.8 15.6 %collective-permute-start.89 = (bf16[4,192,256]{2,1,0:T(8,128)(2,1)S(1)}, bf16[4,192,256]{2,1,0:T(8,128)(2,1)S(1)}, u32[]{:S(2)}, u32[]{:S(2)}) collective-permute-start(bf16[4,192,256]{2,1,0:T(8,128)(2,1)S(1)} %get-tuple-element.372), channel_id=1, source_target_pairs={{0,2},{1,3},{2,0},{3,1},{4,6},{5,7},{6,4},{7,5},{8,10},{9,11},{10,... | collective-permute-start | bytes 1179656 | tf_op jit(solution)/shard_map/ppermute | solution.py:29
  300.1 18.9 %collective-permute-start.94 = (bf16[1,48,1024]{2,1,0:T(8,128)(2,1)S(1)}, bf16[1,48,1024]{2,1,0:T(8,128)(2,1)S(1)}, u32[]{:S(2)}, u32[]{:S(2)}) collective-permute-start(bf16[1,48,1024]{2,1,0:T(8,128)(2,1)S(1)} %get-tuple-element.398), channel_id=1, source_target_pairs={{0,12},{1,13},{2,14},{3,15},{4,8},{5,9},{6,10},{7,11},{8,4},{9,5},... | collective-permute-start | bytes 294920 | tf_op jit(solution)/shard_map/ppermute | solution.py:29
  301.7 17.9 %collective-permute-start.93 = (bf16[1,48,1024]{2,1,0:T(8,128)(2,1)S(1)}, bf16[1,48,1024]{2,1,0:T(8,128)(2,1)S(1)}, u32[]{:S(2)}, u32[]{:S(2)}) collective-permute-start(bf16[1,48,1024]{2,1,0:T(8,128)(2,1)S(1)} %get-tuple-element.399), channel_id=1, source_target_pairs={{0,8},{1,9},{2,10},{3,11},{4,12},{5,13},{6,14},{7,15},{8,0},{9,1},... | collective-permute-start | bytes 294920 | tf_op jit(solution)/shard_map/ppermute | solution.py:29
  303.0 17.4 %collective-permute-start.92 = (bf16[1,48,1024]{2,1,0:T(8,128)(2,1)S(1)}, bf16[1,48,1024]{2,1,0:T(8,128)(2,1)S(1)}, u32[]{:S(2)}, u32[]{:S(2)}) collective-permute-start(bf16[1,48,1024]{2,1,0:T(8,128)(2,1)S(1)} %get-tuple-element.400), channel_id=1, source_target_pairs={{0,4},{1,5},{2,6},{3,7},{4,0},{5,1},{6,2},{7,3},{8,12},{9,13},{10,... | collective-permute-start | bytes 294920 | tf_op jit(solution)/shard_map/ppermute | solution.py:29
  310.3 13.1 %collective-permute-start.91 = (bf16[2,208,256]{2,1,0:T(8,128)(2,1)S(1)}, bf16[2,208,256]{2,1,0:T(8,128)(2,1)S(1)}, u32[]{:S(2)}, u32[]{:S(2)}) collective-permute-start(bf16[2,208,256]{2,1,0:T(8,128)(2,1)S(1)} %get-tuple-element.301), channel_id=1, source_target_pairs={{1,0},{2,1},{3,2},{4,3},{5,4},{6,5},{7,6},{8,7},{9,8},{10,9},{11,1... | collective-permute-start | bytes 638984 | tf_op jit(solution)/shard_map/ppermute | solution.py:174
  319.6 15.3 %collective-permute-start.97 = (bf16[1,192,256]{2,1,0:T(8,128)(2,1)S(1)}, bf16[1,192,256]{2,1,0:T(8,128)(2,1)S(1)}, u32[]{:S(2)}, u32[]{:S(2)}) collective-permute-start(bf16[1,192,256]{2,1,0:T(8,128)(2,1)S(1)} %get-tuple-element.396), channel_id=1, source_target_pairs={{0,8},{1,9},{2,10},{3,11},{4,12},{5,13},{6,14},{7,15},{8,0},{9,1},... | collective-permute-start | bytes 294920 | tf_op jit(solution)/shard_map/ppermute | solution.py:29
  320.4 14.6 %collective-permute-start.96 = (bf16[1,192,256]{2,1,0:T(8,128)(2,1)S(1)}, bf16[1,192,256]{2,1,0:T(8,128)(2,1)S(1)}, u32[]{:S(2)}, u32[]{:S(2)}) collective-permute-start(bf16[1,192,256]{2,1,0:T(8,128)(2,1)S(1)} %get-tuple-element.397), channel_id=1, source_target_pairs={{0,4},{1,5},{2,6},{3,7},{4,0},{5,1},{6,2},{7,3},{8,12},{9,13},{10,... | collective-permute-start | bytes 294920 | tf_op jit(solution)/shard_map/ppermute | solution.py:29
  (118 other events, 662.4 us)

commit v3 on v2

--- a/solution.py
+++ b/solution.py
@@ -1107,10 +1107,11 @@
     packed = jnp.concatenate(packed, 0)
     near = Gather(mine, jnp.pad(packed, ((0, -packed.shape[0] % 8), (0, 0))))
 
-    fast = tie([], fast_in.reshape(groups, 4, PIX, CF))
-    fast, fast_in, wide, slow_in, slow_cotangent, fast_cotangent = tie(
-        [near], fast, fast_in, wide, slow_in, slow_cotangent, fast_cotangent
-    )
+    fast_in, slow_in, slow_cotangent, fast_cotangent = tie(
+        [near], fast_in, slow_in, slow_cotangent, fast_cotangent
+    )
+    fast = fast_in.reshape(groups, 4, PIX, CF)
+    fast, wide = tie([], fast, wide)
     wide = Gather(mine, wide)
     link = (1 - clip_starts).astype(F32)
     links = link.reshape(groups)
@@ -1214,9 +1215,12 @@
         return lambda value, stage: tie(stages[stage], value) if stage < len(stages) else value
 
     def first_hook(value, stage):
-        if stage == 1:
+        if stage == 0:
+            fars.append(Gather(mine, far))
+        elif stage == 1:
             value = tie([wide], value)
-            fars.append(Gather(mine, far))
+        elif stage == 2:
+            value = tie(fars, value)
         return value
 
     lat_pre, fone, sums = call(
@@ -1246,7 +1250,7 @@
     )
     rim_before, rim_after = from_before(tail), from_after(head)
     far = fars[0]
-    lat_act = tie([wide, far], lat_act)
+    lat_act = tie([wide], lat_act)
     projection = wide.result().reshape(CS + CL, CS)
     per = frames
     state, fact_cat, sums = call(
@@ -1492,7 +1496,9 @@
                 name="slow_in_grad",
             )[0]
         elif stage == 2:
-            value, flows["slow_in_grad"] = tie([flows["b"]], value, flows["slow_in_grad"])
+            value, flows["slow_in_grad"] = tie(
+                [flows["b"]], value, pixels_first(flows["slow_in_grad"], slow_in.shape)
+            )
         return value
 
     sums_d = all_sum(sums, weights_of_one)
@@ -1509,7 +1515,6 @@
         state=state,
         name="back_lat",
     )
-    lat_rim = from_after(head)
     packed = devices <= CFM
     tops = [
         scalar(links), scalar(nexts), whole(fast), whole(edge_down), whole(edge_up),
@@ -1532,6 +1537,7 @@
         flops=2 * rows * 896 * 384,
         name="lateral_grad",
     )
+    *first_grad, head = tie([], *first_grad, head)
     if packed:
         flat = first_grad[0]
     else:
@@ -1544,11 +1550,11 @@
         flat = jnp.pad(flat, ((0, 0), (0, -flat.shape[1] % 1024)))
         flat = flat.reshape(devices, -1, 128)
     last = Shares(spots, flat)
+    lat_rim = from_after(head)
     fast_out = pixels_first(fast_out, fast_in.shape)
     lat_rim, fast_out, slow_in_grad = tie(
         [flows["a"], last], lat_rim, fast_out, slow_in_grad
     )
-    slow_in_grad = pixels_first(slow_in_grad, slow_in.shape)
     state, fast_in_grad = call(
         k_fast_grad,
         micro,

time: 350 us -> 348 us (level)
    ppermute x98, waiting for transfers between devices: 60 us -> 55.5 us  [swap(): return lax.ppermute(value, AXES, [(i, i ^ bit) for i in range(count)])]
    unnamed x104 -> x115, local copies, waits for them, and re-layouts: 20 us -> 21.3 us
  transfers between devices with their start and end apart: 105 -> 105, of which waited for: 47 -> 48; matrix products, arithmetic and copies ran while one was open for 11% -> 11% of each run, Pallas kernels for 16% -> 16%
where the time goes in v3:
time: 348 us; the launch traced here: 343 us
  starting transfers between devices  139 us (40%)
  Pallas kernels  84.8 us (24%)
  waiting for transfers between devices  58.2 us (17%)
  local copies, waits for them, and re-layouts  47.6 us (14%)
  other arithmetic  11.2 us (3%)
    ppermute x98, starting transfers between devices, swap(): return lax.ppermute(value, AXES, [(i, i ^ bit) for i in range(count)])  123 us
    pallas_call x23, Pallas kernels, call(): pl.pallas_call(kernel, in_specs=[kinds[block] if block in (None, 'hbm') e...  84.8 us
    ppermute x98, waiting for transfers between devices, swap(): return lax.ppermute(value, AXES, [(i, i ^ bit) for i in range(count)])  55.5 us
    unnamed x115, local copies, waits for them, and re-layouts  21.3 us
    ppermute x3, starting transfers between devices, from_before(): return lax.ppermute(value, AXES, [(i, i + 1) for i in range(count - 1)])  10.7 us
    reshape x3, local copies, waits for them, and re-layouts, pixels_first(): return jnp.swapaxes(value.reshape(whole_shape), 1, 2)  9.69 us
  transfers between devices with their start and end apart: 105, of which 48 were waited for; matrix products, arithmetic and copies ran while one was open for 11% of the time, Pallas kernels for 16%

profile of v3, /device:TPU:0, one launch (start us, length us, event | category | flops | bytes accessed | tf_op | source)
XLA Modules:
  0.0 343.2 jit_solution(9445974891125604293)
XLA Ops:
  6.0 5.1 %collective-permute-start.2 = (bf16[1,168,256]{2,1,0:T(8,128)(2,1)S(1)}, bf16[1,168,256]{2,1,0:T(8,128)(2,1)S(1)}, u32[]{:S(2)}, u32[]{:S(2)}) collective-permute-start(bf16[1,168,256]{2,1,0:T(8,128)(2,1)S(1)} %pad_bitcast_fusion), channel_id=1, source_target_pairs={{0,12},{1,13},{2,14},{3,15},{4,8},{5,9},{6,10},{7,11},{8,4},{9,5},... | collective-permute-start | bytes 258056 | tf_op jit(solution)/shard_map/ppermute | solution.py:29
  15.1 3.3 collective-permute-done.1
  18.5 2.5 collective-permute-start.7
  22.5 2.7 collective-permute-start.10
  38.8 5.1 %collective-permute-start.3 = (bf16[2,2,196,128]{3,2,1,0:T(8,128)(2,1)S(1)}, bf16[2,2,196,128]{3,2,1,0:T(8,128)(2,1)S(1)}, u32[]{:S(2)}, u32[]{:S(2)}) collective-permute-start(bf16[2,2,196,128]{3,2,1,0:T(8,128)(2,1)S(1)} %slice.134), channel_id=1, source_target_pairs={{0,1},{1,2},{2,3},{3,4},{4,5},{5,6},{6,7},{7,8},{8,9},{9,10},{10,1... | collective-permute-start | bytes 602120 | tf_op jit(solution)/shard_map/ppermute | solution.py:169
  43.9 2.9 copy.113
  48.0 3.9 %collective-permute-start.18 = (bf16[4,40,1024]{2,1,0:T(8,128)(2,1)S(1)}, bf16[4,40,1024]{2,1,0:T(8,128)(2,1)S(1)}, u32[]{:S(2)}, u32[]{:S(2)}) collective-permute-start(bf16[4,40,1024]{2,1,0:T(8,128)(2,1)S(1)} %maximum_bitcast_fusion.1), channel_id=1, source_target_pairs={{0,3},{1,2},{2,1},{3,0},{4,7},{5,6},{6,5},{7,4},{8,11},{9,10},{10,... | collective-permute-start | bytes 983048 | tf_op jit(solution)/shard_map/ppermute | solution.py:29
  54.9 2.8 lateral_and_fast_time.1
  61.9 6.7 %collective-permute-done.15 = f32[2,2,384]{2,1,0:T(2,128)S(1)} collective-permute-done((f32[2,2,384]{2,1,0:T(2,128)S(1)}, f32[2,2,384]{2,1,0:T(2,128)S(1)}, u32[]{:S(2)}, u32[]{:S(2)}) %collective-permute-start.15) | collective-permute-done | bytes 6176 | tf_op jit(solution)/shard_map/ppermute | solution.py:29
  68.6 3.6 %collective-permute-done.13 = f32[2,2,384]{2,1,0:T(2,128)S(1)} collective-permute-done((f32[2,2,384]{2,1,0:T(2,128)S(1)}, f32[2,2,384]{2,1,0:T(2,128)S(1)}, u32[]{:S(2)}, u32[]{:S(2)}) %collective-permute-start.13) | collective-permute-done | bytes 6176 | tf_op jit(solution)/shard_map/ppermute | solution.py:29
  74.5 2.7 collective-permute-start.19
  79.0 2.5 collective-permute-start.22
  88.2 4.6 %slow_time_taps.1 = (bf16[8,208,256]{2,1,0:T(8,128)(2,1)S(1)}, f32[8,208,768]{2,1,0:T(8,128)S(1)}, bf16[2,208,256]{2,1,0:T(8,128)(2,1)S(1)}, bf16[2,208,256]{2,1,0:T(8,128)(2,1)S(1)}) custom-call(f32[8]{0:T(128)S(1)} %reshape.404.refs_0_, f32[8,208,256]{2,1,0:T(8,128)S(1)} %get-tuple-element.203.refs_1_.refs_8_, ...), custom_call_target="tpu_custom_call" | custom-call | flops 3271557120 | bytes 14561312 | tf_op jit(solution)/shard_map/slow_time_taps/pallas_call | solution.py:269
  96.8 6.1 %shortcut_and_fast_space.1 = (f32[8,208,1024]{2,1,0:T(8,128)S(1)}, bf16[8,208,384]{2,1,0:T(8,128)(2,1)S(1)}, f32[8,208,128]{2,1,0:T(8,128)S(1)}, f32[2,2,1152]{2,1,0:T(2,128)S(1)}) custom-call(bf16[8,208,1024]{2,1,0:T(8,128)(2,1)S(1)} %bitcast.406, bf16[8,208,256]{2,1,0:T(8,128)(2,1)S(1)} %get-tuple-element.221.refs_1_, bf16[1280,1024]{1,0:T(8,128)(2,1)S(1)} %bitcast.392, ...), custom_call_target="tpu_custom_call" | custom-call | flops 4362076160 | bytes 18069504 | tf_op jit(solution)/shard_map/shortcut_and_fast_space/pallas_call | solution.py:269
  122.2 4.0 %slow_space.1 = (bf16[8,208,768]{2,1,0:T(8,128)(2,1)S(1)}, f32[8,208,256]{2,1,0:T(8,128)S(1)}, bf16[8,208,128]{2,1,0:T(8,128)(2,1)S(1)}, f32[8,208,512]{2,1,0:T(...) custom-call(f32[8,208,256]{2,1,0:T(8,128)S(1)} %get-tuple-element.227.refs_0_.refs_6_.refs_1_, ...), custom_call_target="tpu_custom_call" | custom-call | flops 1962934272 | bytes 14268416 | tf_op jit(solution)/shard_map/slow_space/pallas_call | solution.py:269
  155.7 3.2 fast_out.1
  160.2 9.7 %slow_out.1 = (bf16[8,196,1024]{2,1,0:T(8,128)(2,1)S(1)}, f32[8,208,1024]{2,1,0:T(8,128)S(1)}, f32[2,3,1536]{2,1,0:T(4,128)S(1)}) custom-call(bf16[8,208,256]{2,1,0:T(8,128)(2,1)S(1)} %get-tuple-element.247.refs_0_, bf16[256,1024]{1,0:T(8,128)(2,1)S(1)} %get-tuple-element.248.refs_1_, f32[8,208,1024]{2,1,0:T(8,128)S(1)} %get-tuple-element.249.refs_2_, ...), custom_call_target="tpu_custom_call" | custom-call | flops 872415232 | bytes 21733376 | tf_op jit(solution)/shard_map/slow_out/pallas_call | solution.py:269
  187.7 7.2 %back_three.1 = (bf16[8,208,1024]{2,1,0:T(8,128)(2,1)S(1)}, bf16[8,208,1024]{2,1,0:T(8,128)(2,1)S(1)}, f32[8,208,256]{2,1,0:T(8,128)S(1)}, f32[2,2,256]{2,1,0:T(2,128)S(1)}) custom-call(bf16[8,208,256]{2,1,0:T(8,128)(2,1)S(1)} %get-tuple-element.247.refs_0_, bf16[256,1024]{1,0:T(8,128)(2,1)S(1)} %get-tuple-element.248.refs_1_, ...), custom_call_target="tpu_custom_call" | custom-call | flops 1744830464 | bytes 25346048 | tf_op jit(solution)/shard_map/back_three/pallas_call | solution.py:269
  197.4 5.8 %projection_grad.1 = bf16[1280,1024]{1,0:T(8,128)(2,1)S(1)} custom-call(bf16[8,208,1024]{2,1,0:T(8,128)(2,1)} %bitcast.403, bf16[8,208,256]{2,1,0:T(8,128)(2,1)S(1)} %copy-done.28, bf16[8,208,1024]{2,1,0:T(8,128)(2,1)S(1)} %get-tuple-element.261.refs_2_.refs_5_.refs_1_), custom_call_target="tpu_custom_call" | custom-call | flops 4362076160 | bytes 10289152 | tf_op jit(solution)/shard_map/projection_grad/pallas_call | solution.py:269
  219.7 5.9 %back_two.1 = (bf16[8,208,768]{2,1,0:T(8,128)(2,1)S(1)}, f32[8,208,256]{2,1,0:T(8,128)S(1)}, bf16[8,208,384]{2,1,0:T(8,128)(2,1)S(1)}, f32[8,208,128]{2,1,0:T(8,128)S(1)}, f32[2,2,384]{2,1,0:T(2,128)S(1)}) custom-call(f32[8,208,256]{2,1,0:T(8,128)S(1)} %get-tuple-element.245.refs_0_.refs_8_, f32[2,2,768]{2,1,0:T(2,128)S(1)} %add_add_fusion.9.refs_1_.refs_3_.refs_9_.refs_2_, ...), custom_call_target="tpu_custom_call" | custom-call | flops 1962934272 | bytes 16678912 | tf_op jit(solution)/shard_map/back_two/pallas_call | solution.py:269
  244.6 2.8 back_one.1
  248.3 3.7 %collective-permute-start.78 = (bf16[2,208,384]{2,1,0:T(8,128)(2,1)}, bf16[2,208,384]{2,1,0:T(8,128)(2,1)S(1)}, u32[]{:S(2)}, u32[]{:S(2)}) collective-permute-start(bf16[2,208,384]{2,1,0:T(8,128)(2,1)} %get-tuple-element.282), channel_id=1, source_target_pairs={{0,1},{1,2},{2,3},{3,4},{4,5},{5,6},{6,7},{7,8},{8,9},{9,10},{10,1... | collective-permute-start | bytes 958472 | tf_op jit(solution)/shard_map/ppermute | solution.py:169
  253.6 4.2 %copy.126 = bf16[2,4,196,1024]{3,1,2,0:T(4,128)(2,1)} copy(bf16[2,4,196,1024]{3,2,1,0:T(8,128)(2,1)S(1)} %bitcast.407) | data formatting | bytes 6422528 | tf_op jit(solution)/shard_map/reshape | solution.py:1352
  259.5 3.1 slow_space_grad.1
  263.3 3.4 back_lateral.1
  268.1 5.8 %slow_time_grad.1 = bf16[3,1280,256]{2,1,0:T(8,128)(2,1)S(1)} custom-call(bf16[8,208,1024]{2,1,0:T(8,128)(2,1)} %bitcast.404, bf16[8,208,256]{2,1,0:T(8,128)(2,1)S(1)} %copy-done.29, bf16[8,208,768]{2,1,0:T(8,128)(2,1)S(1)} %get-tuple-element.302.refs_2_.refs_0_), custom_call_target="tpu_custom_call" | custom-call | flops 3271557120 | bytes 8781824 | tf_op jit(solution)/shard_map/slow_time_grad/pallas_call | solution.py:269
  293.0 6.8 %slow_in_grad.1 = bf16[8,196,1024]{2,1,0:T(8,128)(2,1)S(1)} custom-call(bf16[8,208,768]{2,1,0:T(8,128)(2,1)S(1)} %get-tuple-element.302.refs_2_.refs_0_, bf16[8,208,1024]{2,1,0:T(8,128)(2,1)S(1)} %copy-done.6, bf16[1280,768]{1,0:T(8,128)(2,1)S(1)} %copy-done.14, bf16[1280,1024]{1,0:T(8,128)(2,1)S(1)} %bitcast.394), custom_call_target="tpu_custom_call" | custom-call | flops 6106906624 | bytes 13762560 | tf_op jit(solution)/shard_map/slow_in_grad/pallas_call | solution.py:269
  299.8 4.2 %copy.125 = bf16[2,4,196,1024]{3,1,2,0:T(4,128)(2,1)} copy(bf16[2,4,196,1024]{3,2,1,0:T(8,128)(2,1)S(1)} %bitcast.408) | data formatting | bytes 6422528 | tf_op jit(solution)/shard_map/reshape | solution.py:1352
  305.6 2.8 collective-permute-start.92
  310.2 2.8 lateral_grad.1
  314.3 3.4 collective-permute-start.95
  321.2 2.9 collective-permute-start.96
  (437 shorter events, 204.8 us)
Async XLA Ops:
  18.5 16.9 %collective-permute-start.7 = (bf16[4,168,256]{2,1,0:T(8,128)(2,1)S(1)}, bf16[4,168,256]{2,1,0:T(8,128)(2,1)S(1)}, u32[]{:S(2)}, u32[]{:S(2)}) collective-permute-start(bf16[4,168,256]{2,1,0:T(8,128)(2,1)S(1)} %maximum_bitcast_fusion), channel_id=1, source_target_pairs={{0,3},{1,2},{2,1},{3,0},{4,7},{5,6},{6,5},{7,4},{8,11},{9,10},{10,... | collective-permute-start | bytes 1032200 | tf_op jit(solution)/shard_map/ppermute | solution.py:29
  21.0 15.0 %collective-permute-start.6 = (bf16[4,168,256]{2,1,0:T(8,128)(2,1)S(1)}, bf16[4,168,256]{2,1,0:T(8,128)(2,1)S(1)}, u32[]{:S(2)}, u32[]{:S(2)}) collective-permute-start(bf16[4,168,256]{2,1,0:T(8,128)(2,1)S(1)} %maximum_bitcast_fusion), channel_id=1, source_target_pairs={{0,2},{1,3},{2,0},{3,1},{4,6},{5,7},{6,4},{7,5},{8,10},{9,11},{10,... | collective-permute-start | bytes 1032200 | tf_op jit(solution)/shard_map/ppermute | solution.py:29
  21.5 14.7 %collective-permute-start.5 = (bf16[4,168,256]{2,1,0:T(8,128)(2,1)S(1)}, bf16[4,168,256]{2,1,0:T(8,128)(2,1)S(1)}, u32[]{:S(2)}, u32[]{:S(2)}) collective-permute-start(bf16[4,168,256]{2,1,0:T(8,128)(2,1)S(1)} %maximum_bitcast_fusion), channel_id=1, source_target_pairs={{0,1},{1,0},{2,3},{3,2},{4,5},{5,4},{6,7},{7,6},{8,9},{9,8},{10,11... | collective-permute-start | bytes 1032200 | tf_op jit(solution)/shard_map/ppermute | solution.py:29
  36.7 15.8 %collective-permute-start.11 = (bf16[16,168,256]{2,1,0:T(8,128)(2,1)S(1)}, bf16[16,168,256]{2,1,0:T(8,128)(2,1)}, u32[]{:S(2)}, u32[]{:S(2)}) collective-permute-start(bf16[16,168,256]{2,1,0:T(8,128)(2,1)S(1)} %bitcast.424), channel_id=1, source_target_pairs={{0,16},{1,17},{2,18},{3,19},{4,20},{5,21},{6,22},{7,23},{8,24},{9,... | collective-permute-start | bytes 4128776 | tf_op jit(solution)/shard_map/ppermute | solution.py:29
  37.6 14.4 %collective-permute-start.4 = (bf16[2,1,196,128]{3,2,1,0:T(8,128)(2,1)S(1)}, bf16[2,1,196,128]{3,2,1,0:T(8,128)(2,1)S(1)}, u32[]{:S(2)}, u32[]{:S(2)}) collective-permute-start(bf16[2,1,196,128]{3,2,1,0:T(8,128)(2,1)S(1)} %slice_multiply_fusion), channel_id=1, source_target_pairs={{1,0},{2,1},{3,2},{4,3},{5,4},{6,5},{7,6},{8,7},{9,8},{10,9},{11,1... | collective-permute-start | bytes 301064 | tf_op jit(solution)/shard_map/ppermute | solution.py:174
  38.8 13.7 %collective-permute-start.3 = (bf16[2,2,196,128]{3,2,1,0:T(8,128)(2,1)S(1)}, bf16[2,2,196,128]{3,2,1,0:T(8,128)(2,1)S(1)}, u32[]{:S(2)}, u32[]{:S(2)}) collective-permute-start(bf16[2,2,196,128]{3,2,1,0:T(8,128)(2,1)S(1)} %slice.134), channel_id=1, source_target_pairs={{0,1},{1,2},{2,3},{3,4},{4,5},{5,6},{6,7},{7,8},{8,9},{9,10},{10,1... | collective-permute-start | bytes 602120 | tf_op jit(solution)/shard_map/ppermute | solution.py:169
  48.0 24.2 %collective-permute-start.18 = (bf16[4,40,1024]{2,1,0:T(8,128)(2,1)S(1)}, bf16[4,40,1024]{2,1,0:T(8,128)(2,1)S(1)}, u32[]{:S(2)}, u32[]{:S(2)}) collective-permute-start(bf16[4,40,1024]{2,1,0:T(8,128)(2,1)S(1)} %maximum_bitcast_fusion.1), channel_id=1, source_target_pairs={{0,3},{1,2},{2,1},{3,0},{4,7},{5,6},{6,5},{7,4},{8,11},{9,10},{10,... | collective-permute-start | bytes 983048 | tf_op jit(solution)/shard_map/ppermute | solution.py:29
  51.9 20.3 %collective-permute-start.17 = (bf16[4,40,1024]{2,1,0:T(8,128)(2,1)S(1)}, bf16[4,40,1024]{2,1,0:T(8,128)(2,1)S(1)}, u32[]{:S(2)}, u32[]{:S(2)}) collective-permute-start(bf16[4,40,1024]{2,1,0:T(8,128)(2,1)S(1)} %maximum_bitcast_fusion.1), channel_id=1, source_target_pairs={{0,2},{1,3},{2,0},{3,1},{4,6},{5,7},{6,4},{7,5},{8,10},{9,11},{10,... | collective-permute-start | bytes 983048 | tf_op jit(solution)/shard_map/ppermute | solution.py:29
  51.9 20.3 %collective-permute-start.16 = (bf16[4,40,1024]{2,1,0:T(8,128)(2,1)S(1)}, bf16[4,40,1024]{2,1,0:T(8,128)(2,1)S(1)}, u32[]{:S(2)}, u32[]{:S(2)}) collective-permute-start(bf16[4,40,1024]{2,1,0:T(8,128)(2,1)S(1)} %maximum_bitcast_fusion.1), channel_id=1, source_target_pairs={{0,1},{1,0},{2,3},{3,2},{4,5},{5,4},{6,7},{7,6},{8,9},{9,8},{10,11... | collective-permute-start | bytes 983048 | tf_op jit(solution)/shard_map/ppermute | solution.py:29
  72.6 22.2 %collective-permute-start.27 = (bf16[16,40,1024]{2,1,0:T(8,128)(2,1)S(1)}, bf16[16,40,1024]{2,1,0:T(8,128)(2,1)S(1)}, u32[]{:S(2)}, u32[]{:S(2)}) collective-permute-start(bf16[16,40,1024]{2,1,0:T(8,128)(2,1)S(1)} %bitcast.425), channel_id=1, source_target_pairs={{0,16},{1,17},{2,18},{3,19},{4,20},{5,21},{6,22},{7,23},{8,24},{9,... | collective-permute-start | bytes 3932168 | tf_op jit(solution)/shard_map/ppermute | solution.py:29
  84.7 24.4 %collective-permute-start.31 = (bf16[4,104,256]{2,1,0:T(8,128)(2,1)S(1)}, bf16[4,104,256]{2,1,0:T(8,128)(2,1)S(1)}, u32[]{:S(2)}, u32[]{:S(2)}) collective-permute-start(bf16[4,104,256]{2,1,0:T(8,128)(2,1)S(1)} %maximum_bitcast_fusion.2), channel_id=1, source_target_pairs={{0,3},{1,2},{2,1},{3,0},{4,7},{5,6},{6,5},{7,4},{8,11},{9,10},{10,... | collective-permute-start | bytes 638984 | tf_op jit(solution)/shard_map/ppermute | solution.py:29
  85.9 23.2 %collective-permute-start.30 = (bf16[4,104,256]{2,1,0:T(8,128)(2,1)S(1)}, bf16[4,104,256]{2,1,0:T(8,128)(2,1)S(1)}, u32[]{:S(2)}, u32[]{:S(2)}) collective-permute-start(bf16[4,104,256]{2,1,0:T(8,128)(2,1)S(1)} %maximum_bitcast_fusion.2), channel_id=1, source_target_pairs={{0,2},{1,3},{2,0},{3,1},{4,6},{5,7},{6,4},{7,5},{8,10},{9,11},{10,... | collective-permute-start | bytes 638984 | tf_op jit(solution)/shard_map/ppermute | solution.py:29
  86.2 22.9 %collective-permute-start.29 = (bf16[4,104,256]{2,1,0:T(8,128)(2,1)S(1)}, bf16[4,104,256]{2,1,0:T(8,128)(2,1)S(1)}, u32[]{:S(2)}, u32[]{:S(2)}) collective-permute-start(bf16[4,104,256]{2,1,0:T(8,128)(2,1)S(1)} %maximum_bitcast_fusion.2), channel_id=1, source_target_pairs={{0,1},{1,0},{2,3},{3,2},{4,5},{5,4},{6,7},{7,6},{8,9},{9,8},{10,11... | collective-permute-start | bytes 638984 | tf_op jit(solution)/shard_map/ppermute | solution.py:29
  92.9 10.1 %collective-permute-start.25 = (bf16[2,208,256]{2,1,0:T(8,128)(2,1)S(1)}, bf16[2,208,256]{2,1,0:T(8,128)(2,1)S(1)}, u32[]{:S(2)}, u32[]{:S(2)}) collective-permute-start(bf16[2,208,256]{2,1,0:T(8,128)(2,1)S(1)} %get-tuple-element.215), channel_id=1, source_target_pairs={{0,1},{1,2},{2,3},{3,4},{4,5},{5,6},{6,7},{7,8},{8,9},{9,10},{10,1... | collective-permute-start | bytes 638984 | tf_op jit(solution)/shard_map/ppermute | solution.py:169
  94.8 10.1 %collective-permute-start.26 = (bf16[2,208,256]{2,1,0:T(8,128)(2,1)S(1)}, bf16[2,208,256]{2,1,0:T(8,128)(2,1)S(1)}, u32[]{:S(2)}, u32[]{:S(2)}) collective-permute-start(bf16[2,208,256]{2,1,0:T(8,128)(2,1)S(1)} %get-tuple-element.216), channel_id=1, source_target_pairs={{1,0},{2,1},{3,2},{4,3},{5,4},{6,5},{7,6},{8,7},{9,8},{10,9},{11,1... | collective-permute-start | bytes 638984 | tf_op jit(solution)/shard_map/ppermute | solution.py:174
  216.1 21.8 %collective-permute-start.74 = (bf16[4,48,1024]{2,1,0:T(8,128)(2,1)S(1)}, bf16[4,48,1024]{2,1,0:T(8,128)(2,1)S(1)}, u32[]{:S(2)}, u32[]{:S(2)}) collective-permute-start(bf16[4,48,1024]{2,1,0:T(8,128)(2,1)S(1)} %get-tuple-element.379), channel_id=1, source_target_pairs={{0,3},{1,2},{2,1},{3,0},{4,7},{5,6},{6,5},{7,4},{8,11},{9,10},{10,... | collective-permute-start | bytes 1179656 | tf_op jit(solution)/shard_map/ppermute | solution.py:29
  217.6 20.4 %collective-permute-start.72 = (bf16[4,48,1024]{2,1,0:T(8,128)(2,1)S(1)}, bf16[4,48,1024]{2,1,0:T(8,128)(2,1)S(1)}, u32[]{:S(2)}, u32[]{:S(2)}) collective-permute-start(bf16[4,48,1024]{2,1,0:T(8,128)(2,1)S(1)} %get-tuple-element.380), channel_id=1, source_target_pairs={{0,1},{1,0},{2,3},{3,2},{4,5},{5,4},{6,7},{7,6},{8,9},{9,8},{10,11... | collective-permute-start | bytes 1179656 | tf_op jit(solution)/shard_map/ppermute | solution.py:29
  218.9 19.1 %collective-permute-start.73 = (bf16[4,48,1024]{2,1,0:T(8,128)(2,1)S(1)}, bf16[4,48,1024]{2,1,0:T(8,128)(2,1)S(1)}, u32[]{:S(2)}, u32[]{:S(2)}) collective-permute-start(bf16[4,48,1024]{2,1,0:T(8,128)(2,1)S(1)} %get-tuple-element.381), channel_id=1, source_target_pairs={{0,2},{1,3},{2,0},{3,1},{4,6},{5,7},{6,4},{7,5},{8,10},{9,11},{10,... | collective-permute-start | bytes 1179656 | tf_op jit(solution)/shard_map/ppermute | solution.py:29
  248.3 15.0 %collective-permute-start.78 = (bf16[2,208,384]{2,1,0:T(8,128)(2,1)}, bf16[2,208,384]{2,1,0:T(8,128)(2,1)S(1)}, u32[]{:S(2)}, u32[]{:S(2)}) collective-permute-start(bf16[2,208,384]{2,1,0:T(8,128)(2,1)} %get-tuple-element.282), channel_id=1, source_target_pairs={{0,1},{1,2},{2,3},{3,4},{4,5},{5,6},{6,7},{7,8},{8,9},{9,10},{10,1... | collective-permute-start | bytes 958472 | tf_op jit(solution)/shard_map/ppermute | solution.py:169
  252.0 11.3 %collective-permute-start.79 = (bf16[2,208,384]{2,1,0:T(8,128)(2,1)S(1)}, bf16[2,208,384]{2,1,0:T(8,128)(2,1)S(1)}, u32[]{:S(2)}, u32[]{:S(2)}) collective-permute-start(bf16[2,208,384]{2,1,0:T(8,128)(2,1)S(1)} %get-tuple-element.283), channel_id=1, source_target_pairs={{1,0},{2,1},{3,2},{4,3},{5,4},{6,5},{7,6},{8,7},{9,8},{10,9},{11,1... | collective-permute-start | bytes 958472 | tf_op jit(solution)/shard_map/ppermute | solution.py:174
  274.2 10.2 %collective-permute-start.84 = (bf16[16,192,256]{2,1,0:T(8,128)(2,1)S(1)}, bf16[16,192,256]{2,1,0:T(8,128)(2,1)S(1)}, u32[]{:S(2)}, u32[]{:S(2)}) collective-permute-start(bf16[16,192,256]{2,1,0:T(8,128)(2,1)S(1)} %fusion.7), channel_id=1, source_target_pairs={{0,16},{1,17},{2,18},{3,19},{4,20},{5,21},{6,22},{7,23},{8,24},{9,... | collective-permute-start | bytes 4718600 | tf_op jit(solution)/shard_map/ppermute | solution.py:29
  285.8 18.1 %collective-permute-start.86 = (f32[2,2,256]{2,1,0:T(2,128)S(1)}, f32[2,2,256]{2,1,0:T(2,128)S(1)}, u32[]{:S(2)}, u32[]{:S(2)}) collective-permute-start(f32[2,2,256]{2,1,0:T(2,128)S(1)} %add_add_fusion.18), channel_id=1, source_target_pairs={{0,8},{1,9},{2,10},{3,11},{4,12},{5,13},{6,14},{7,15},{8,0},{9,1},... | collective-permute-start | bytes 12296 | tf_op jit(solution)/shard_map/ppermute | solution.py:29
  287.0 18.4 %collective-permute-start.85 = (f32[2,2,256]{2,1,0:T(2,128)S(1)}, f32[2,2,256]{2,1,0:T(2,128)S(1)}, u32[]{:S(2)}, u32[]{:S(2)}) collective-permute-start(f32[2,2,256]{2,1,0:T(2,128)S(1)} %add_add_fusion.18), channel_id=1, source_target_pairs={{0,4},{1,5},{2,6},{3,7},{4,0},{5,1},{6,2},{7,3},{8,12},{9,13},{10,... | collective-permute-start | bytes 12296 | tf_op jit(solution)/shard_map/ppermute | solution.py:29
  289.4 16.2 %collective-permute-start.90 = (bf16[4,192,256]{2,1,0:T(8,128)(2,1)S(1)}, bf16[4,192,256]{2,1,0:T(8,128)(2,1)S(1)}, u32[]{:S(2)}, u32[]{:S(2)}) collective-permute-start(bf16[4,192,256]{2,1,0:T(8,128)(2,1)S(1)} %get-tuple-element.376), channel_id=1, source_target_pairs={{0,3},{1,2},{2,1},{3,0},{4,7},{5,6},{6,5},{7,4},{8,11},{9,10},{10,... | collective-permute-start | bytes 1179656 | tf_op jit(solution)/shard_map/ppermute | solution.py:29
  290.7 17.7 %collective-permute-start.88 = (bf16[4,192,256]{2,1,0:T(8,128)(2,1)S(1)}, bf16[4,192,256]{2,1,0:T(8,128)(2,1)S(1)}, u32[]{:S(2)}, u32[]{:S(2)}) collective-permute-start(bf16[4,192,256]{2,1,0:T(8,128)(2,1)S(1)} %get-tuple-element.377), channel_id=1, source_target_pairs={{0,1},{1,0},{2,3},{3,2},{4,5},{5,4},{6,7},{7,6},{8,9},{9,8},{10,11... | collective-permute-start | bytes 1179656 | tf_op jit(solution)/shard_map/ppermute | solution.py:29
  291.1 17.3 %collective-permute-start.89 = (bf16[4,192,256]{2,1,0:T(8,128)(2,1)S(1)}, bf16[4,192,256]{2,1,0:T(8,128)(2,1)S(1)}, u32[]{:S(2)}, u32[]{:S(2)}) collective-permute-start(bf16[4,192,256]{2,1,0:T(8,128)(2,1)S(1)} %get-tuple-element.378), channel_id=1, source_target_pairs={{0,2},{1,3},{2,0},{3,1},{4,6},{5,7},{6,4},{7,5},{8,10},{9,11},{10,... | collective-permute-start | bytes 1179656 | tf_op jit(solution)/shard_map/ppermute | solution.py:29
  303.9 15.8 %collective-permute-start.94 = (bf16[1,48,1024]{2,1,0:T(8,128)(2,1)}, bf16[1,48,1024]{2,1,0:T(8,128)(2,1)S(1)}, u32[]{:S(2)}, u32[]{:S(2)}) collective-permute-start(bf16[1,48,1024]{2,1,0:T(8,128)(2,1)} %get-tuple-element.404), channel_id=1, source_target_pairs={{0,12},{1,13},{2,14},{3,15},{4,8},{5,9},{6,10},{7,11},{8,4},{9,5},... | collective-permute-start | bytes 294920 | tf_op jit(solution)/shard_map/ppermute | solution.py:29
  305.4 14.6 %collective-permute-start.93 = (bf16[1,48,1024]{2,1,0:T(8,128)(2,1)}, bf16[1,48,1024]{2,1,0:T(8,128)(2,1)S(1)}, u32[]{:S(2)}, u32[]{:S(2)}) collective-permute-start(bf16[1,48,1024]{2,1,0:T(8,128)(2,1)} %get-tuple-element.405), channel_id=1, source_target_pairs={{0,8},{1,9},{2,10},{3,11},{4,12},{5,13},{6,14},{7,15},{8,0},{9,1},... | collective-permute-start | bytes 294920 | tf_op jit(solution)/shard_map/ppermute | solution.py:29
  305.6 15.6 %collective-permute-start.92 = (bf16[1,48,1024]{2,1,0:T(8,128)(2,1)}, bf16[1,48,1024]{2,1,0:T(8,128)(2,1)S(1)}, u32[]{:S(2)}, u32[]{:S(2)}) collective-permute-start(bf16[1,48,1024]{2,1,0:T(8,128)(2,1)} %get-tuple-element.406), channel_id=1, source_target_pairs={{0,4},{1,5},{2,6},{3,7},{4,0},{5,1},{6,2},{7,3},{8,12},{9,13},{10,... | collective-permute-start | bytes 294920 | tf_op jit(solution)/shard_map/ppermute | solution.py:29
  313.0 11.2 %collective-permute-start.91 = (bf16[2,208,256]{2,1,0:T(8,128)(2,1)S(1)}, bf16[2,208,256]{2,1,0:T(8,128)(2,1)S(1)}, u32[]{:S(2)}, u32[]{:S(2)}) collective-permute-start(bf16[2,208,256]{2,1,0:T(8,128)(2,1)S(1)} %get-tuple-element.310), channel_id=1, source_target_pairs={{1,0},{2,1},{3,2},{4,3},{5,4},{6,5},{7,6},{8,7},{9,8},{10,9},{11,1... | collective-permute-start | bytes 638984 | tf_op jit(solution)/shard_map/ppermute | solution.py:174
  320.0 11.5 %collective-permute-start.97 = (bf16[1,192,256]{2,1,0:T(8,128)(2,1)S(1)}, bf16[1,192,256]{2,1,0:T(8,128)(2,1)S(1)}, u32[]{:S(2)}, u32[]{:S(2)}) collective-permute-start(bf16[1,192,256]{2,1,0:T(8,128)(2,1)S(1)} %get-tuple-element.402), channel_id=1, source_target_pairs={{0,8},{1,9},{2,10},{3,11},{4,12},{5,13},{6,14},{7,15},{8,0},{9,1},... | collective-permute-start | bytes 294920 | tf_op jit(solution)/shard_map/ppermute | solution.py:29
  321.2 10.3 %collective-permute-start.96 = (bf16[1,192,256]{2,1,0:T(8,128)(2,1)S(1)}, bf16[1,192,256]{2,1,0:T(8,128)(2,1)S(1)}, u32[]{:S(2)}, u32[]{:S(2)}) collective-permute-start(bf16[1,192,256]{2,1,0:T(8,128)(2,1)S(1)} %get-tuple-element.403), channel_id=1, source_target_pairs={{0,4},{1,5},{2,6},{3,7},{4,0},{5,1},{6,2},{7,3},{8,12},{9,13},{10,... | collective-permute-start | bytes 294920 | tf_op jit(solution)/shard_map/ppermute | solution.py:29
  (124 other events, 697.1 us)
